TPU v7x, 32 devices: a whole 2x2x4 slice. The times are simulated.
32 devices in a mesh: narrow: 4 (over y, x), wide: 8 (over z, core).
Axes of the slice: x: 2, y: 2, z: 4, core: 2. Of those that a mesh axis runs over, the one named last changes fastest.
Arguments:
- hidden_in: bfloat16 [32768, 768], P(('narrow', 'wide')), may hold values from -6 to 6
- norm_gain_one: float32 [768], replicated, may hold values from 0.5 to 1.5
- w_qkv: bfloat16 [768, 2304], replicated, may hold values from -0.21875 to 0.21875
- w_out: bfloat16 [768, 768], replicated, may hold values from -0.875 to 0.875
- pos_table: float32 [32, 12], replicated, may hold values from -4 to 4
- norm_gain_two: float32 [768], replicated, may hold values from 0.5 to 1.5
- w_router: bfloat16 [768, 32], replicated, may hold values from -0.08984375 to 0.08984375
- w_in: bfloat16 [32, 768, 3072], P(('narrow', 'wide')), may hold values from -0.21875 to 0.21875
- w_down: bfloat16 [32, 3072, 768], P(('narrow', 'wide')), may hold values from -3.453125 to 3.453125
- expert_ids: int32 [32768, 1], P(('narrow', 'wide')), may hold values from 0 to 31
- segment_ids: int32 [64, 512], P(('narrow', 'wide')), may hold values from 0 to 3, never falling along the last dimension, each value on 1 to 256 neighbouring positions
- rel_buckets: int32 [512, 512], replicated, may hold values from 0 to 31
- out_grad: bfloat16 [32768, 768], P(('narrow', 'wide')), may hold values from -6 to 6
Outputs:
- layer_out: bfloat16 [32768, 768], P(('narrow', 'wide'))
- in_grad: float32 [32768, 768], P(('narrow', 'wide'))
- gain_one_grad: float32 [768], replicated
- qkv_grad: float32 [768, 2304], replicated
- out_proj_grad: float32 [768, 768], replicated
- table_grad: float32 [32, 12], replicated
- gain_two_grad: float32 [768], replicated
- router_grad: float32 [768, 32], replicated
- w_in_grad: float32 [32, 768, 3072], P(('narrow', 'wide'))
- w_down_grad: float32 [32, 3072, 768], P(('narrow', 'wide'))
Inputs may be any that keep to these rules, and one draw needn't show every extreme that they name: `segment_ids`: document numbers never fall along a row.
All inputs are finite; a program needn't handle non-finite values.
Results may differ from a plain program's by a relative error of at most 0.015.
Values may be sent and summed in bfloat16 or wider, within the bound.
A program may use at most 256 MiB of HBM per device.

v0:
```python
import jax
import jax.numpy as jnp
from jax import lax
from jax.sharding import PartitionSpec as P

HEADS = 12
HEAD_DIM = 64
LEN = 512
BUCKETS = 32


EPS = 1e-06


def matmul(a, b):
    return jnp.dot(a, b, preferred_element_type=jnp.float32)


def matmul_tn(a, b):
    return lax.dot_general(a, b, (((0,), (0,)), ((), ())), preferred_element_type=jnp.float32)


def matmul_nt(a, b):
    return lax.dot_general(a, b, (((1,), (1,)), ((), ())), preferred_element_type=jnp.float32)


def norm_back(grad_normed, source, scale, gain):
    normed = source * scale
    scaled_grad = grad_normed * gain
    grad_source = scale * (
        scaled_grad - normed * jnp.mean(scaled_grad * normed, axis=-1, keepdims=True)
    )
    grad_gain = jnp.sum(grad_normed * normed, axis=0)
    return (grad_source, grad_gain)


def local(
    hidden_in,
    norm_gain_one,
    w_qkv,
    w_out,
    pos_table,
    norm_gain_two,
    w_router,
    w_in,
    w_down,
    expert_ids,
    segment_ids,
    rel_buckets,
    out_grad,
):
    narrow_count = lax.axis_size("narrow")
    wide_count = lax.axis_size("wide")
    expert_count = narrow_count * wide_count
    tok_count, width = hidden_in.shape
    seq_count = segment_ids.shape[0]
    capacity = max(2, (5 * tok_count + 4 * expert_count - 1) // (4 * expert_count))
    factor = HEAD_DIM ** (-0.5)
    source = hidden_in.astype(jnp.float32)
    scale_one = lax.rsqrt(jnp.mean(source * source, axis=-1, keepdims=True) + EPS)
    normed_one = (source * scale_one * norm_gain_one).astype(jnp.bfloat16)
    qkv = matmul(normed_one, w_qkv).astype(jnp.bfloat16)
    blocks = qkv.reshape(seq_count, LEN, 3, HEADS, HEAD_DIM)
    bucket_hot = (
        rel_buckets[:, :, None] == jnp.arange(BUCKETS, dtype=jnp.int32)[None, None, :]
    ).astype(jnp.float32)
    bias = jnp.einsum("qkb,bh->hqk", bucket_hot, pos_table, precision=lax.Precision.HIGHEST)

    def scores_of(index):
        raw = (
            jnp.einsum(
                "qhd,khd->hqk",
                blocks[index, :, 0],
                blocks[index, :, 1],
                preferred_element_type=jnp.float32,
            )
            * factor
            + bias
        )
        same = segment_ids[index][:, None] == segment_ids[index][None, :]
        return jnp.where(same[None], raw, -1000000000.0)

    mixed_rows = []
    log_totals = []
    for index in range(seq_count):
        scores = scores_of(index)
        peak = jnp.max(scores, axis=-1, keepdims=True)
        weights = jnp.exp(scores - peak)
        total = jnp.sum(weights, axis=-1, keepdims=True)
        probs = (weights / total).astype(jnp.bfloat16)
        mixed = jnp.einsum(
            "hqk,khd->qhd", probs, blocks[index, :, 2], preferred_element_type=jnp.float32
        )
        mixed_rows.append(mixed.reshape(LEN, width))
        log_totals.append(peak + jnp.log(total))
    attn = jnp.concatenate(mixed_rows, axis=0).astype(jnp.bfloat16)
    resid = source + matmul(attn, w_out)
    scale_two = lax.rsqrt(jnp.mean(resid * resid, axis=-1, keepdims=True) + EPS)
    normed_two = (resid * scale_two * norm_gain_two).astype(jnp.bfloat16)
    logits = matmul(normed_two, w_router)
    route = jax.nn.softmax(logits, axis=-1)
    expert_list = expert_ids[:, 0]
    route_hot = expert_list[:, None] == jnp.arange(expert_count, dtype=jnp.int32)[None, :]
    gate = jnp.sum(jnp.where(route_hot, route, 0.0), axis=-1)
    row_index = jnp.arange(tok_count, dtype=jnp.int32)
    earlier = (row_index[:, None] > row_index[None, :]).astype(jnp.bfloat16)
    counts = matmul(earlier, route_hot.astype(jnp.bfloat16))
    position = jnp.sum(jnp.where(route_hot, counts, 0.0), axis=-1).astype(jnp.int32)
    slot = jnp.where(position < capacity, expert_list * capacity + position, -1)
    slot_table = (
        jnp.arange(expert_count * capacity, dtype=jnp.int32)[:, None] == slot[None, :]
    ).astype(jnp.bfloat16)
    packed = (
        matmul(slot_table, normed_two)
        .astype(jnp.bfloat16)
        .reshape(narrow_count, wide_count, capacity, width)
    )
    arrived = lax.all_to_all(
        lax.all_to_all(packed, "narrow", split_axis=0, concat_axis=0, tiled=True),
        "wide",
        split_axis=1,
        concat_axis=1,
        tiled=True,
    )
    expert_in = arrived.reshape(-1, width)
    inner = matmul(expert_in, w_in[0])
    active = jax.nn.gelu(inner).astype(jnp.bfloat16)
    expert_out = (
        matmul(active, w_down[0])
        .astype(jnp.bfloat16)
        .reshape(narrow_count, wide_count, capacity, width)
    )
    returned = lax.all_to_all(
        lax.all_to_all(expert_out, "narrow", split_axis=0, concat_axis=0, tiled=True),
        "wide",
        split_axis=1,
        concat_axis=1,
        tiled=True,
    )
    combined = matmul_tn(slot_table, returned.reshape(-1, width))
    layer_out = (resid + gate[:, None] * combined).astype(jnp.bfloat16)
    grad_out = out_grad.astype(jnp.float32)
    weighted = (gate[:, None] * grad_out).astype(jnp.bfloat16)
    grad_slots = (
        matmul(slot_table, weighted)
        .astype(jnp.bfloat16)
        .reshape(narrow_count, wide_count, capacity, width)
    )
    grad_arrived = lax.all_to_all(
        lax.all_to_all(grad_slots, "narrow", split_axis=0, concat_axis=0, tiled=True),
        "wide",
        split_axis=1,
        concat_axis=1,
        tiled=True,
    ).reshape(-1, width)
    grad_w_down = matmul_tn(active, grad_arrived)
    grad_active = matmul_nt(grad_arrived, w_down[0])
    unused, gelu_pull = jax.vjp(jax.nn.gelu, inner)
    grad_inner = gelu_pull(grad_active)[0].astype(jnp.bfloat16)
    grad_w_in = matmul_tn(expert_in, grad_inner)
    grad_rows = (
        matmul_nt(grad_inner, w_in[0])
        .astype(jnp.bfloat16)
        .reshape(narrow_count, wide_count, capacity, width)
    )
    grad_back = lax.all_to_all(
        lax.all_to_all(grad_rows, "narrow", split_axis=0, concat_axis=0, tiled=True),
        "wide",
        split_axis=1,
        concat_axis=1,
        tiled=True,
    ).reshape(-1, width)
    grad_gate = jnp.sum(grad_out * combined, axis=-1)
    grad_logits = ((grad_gate * gate)[:, None] * (route_hot.astype(jnp.float32) - route)).astype(
        jnp.bfloat16
    )
    grad_router = matmul_tn(normed_two, grad_logits)
    grad_normed_two = matmul_tn(slot_table, grad_back) + matmul_nt(grad_logits, w_router)
    grad_resid_norm, grad_gain_two = norm_back(grad_normed_two, resid, scale_two, norm_gain_two)
    grad_resid = grad_out + grad_resid_norm
    grad_branch = grad_resid.astype(jnp.bfloat16)
    grad_w_out = matmul_tn(attn, grad_branch)
    grad_attn = (
        matmul_nt(grad_branch, w_out).astype(jnp.bfloat16).reshape(seq_count, LEN, HEADS, HEAD_DIM)
    )
    bias_grad = jnp.zeros((HEADS, LEN, LEN), jnp.float32)
    grad_pieces = []
    for index in range(seq_count):
        scores = scores_of(index)
        probs_full = jnp.exp(scores - log_totals[index])
        probs = probs_full.astype(jnp.bfloat16)
        query = blocks[index, :, 0]
        key = blocks[index, :, 1]
        value = blocks[index, :, 2]
        grad_value = jnp.einsum(
            "hqk,qhd->khd", probs, grad_attn[index], preferred_element_type=jnp.float32
        )
        grad_probs = jnp.einsum(
            "qhd,khd->hqk", grad_attn[index], value, preferred_element_type=jnp.float32
        )
        inner_sum = jnp.sum(probs_full * grad_probs, axis=-1, keepdims=True)
        grad_scores = (probs_full * (grad_probs - inner_sum)).astype(jnp.bfloat16)
        bias_grad = bias_grad + grad_scores.astype(jnp.float32)
        grad_query = (
            jnp.einsum("hqk,khd->qhd", grad_scores, key, preferred_element_type=jnp.float32)
            * factor
        )
        grad_key = (
            jnp.einsum("hqk,qhd->khd", grad_scores, query, preferred_element_type=jnp.float32)
            * factor
        )
        grad_pieces.append(
            jnp.stack([grad_query, grad_key, grad_value], axis=1).reshape(LEN, 3 * width)
        )
    grad_qkv = jnp.concatenate(grad_pieces, axis=0).astype(jnp.bfloat16)
    grad_table = jnp.einsum("qkb,hqk->bh", bucket_hot, bias_grad, precision=lax.Precision.HIGHEST)
    grad_w_qkv = matmul_tn(normed_one, grad_qkv)
    grad_normed_one = matmul_nt(grad_qkv, w_qkv)
    grad_source_norm, grad_gain_one = norm_back(grad_normed_one, source, scale_one, norm_gain_one)
    in_grad = grad_resid + grad_source_norm
    grad_w_qkv, grad_w_out, grad_table, grad_gain_one, grad_gain_two, grad_router = lax.psum(
        (grad_w_qkv, grad_w_out, grad_table, grad_gain_one, grad_gain_two, grad_router),
        ("narrow", "wide"),
    )
    return (
        layer_out,
        in_grad,
        grad_gain_one,
        grad_w_qkv,
        grad_w_out,
        grad_table,
        grad_gain_two,
        grad_router,
        grad_w_in[None],
        grad_w_down[None],
    )


def solution(mesh):
    placed = (
        P(("narrow", "wide"), None),
        P(),
        P(),
        P(),
        P(),
        P(),
        P(),
        P(("narrow", "wide"), None, None),
        P(("narrow", "wide"), None, None),
        P(("narrow", "wide"), None),
        P(("narrow", "wide"), None),
        P(),
        P(("narrow", "wide"), None),
    )
    return jax.shard_map(
        local,
        mesh=mesh,
        in_specs=placed,
        out_specs=(
            P(("narrow", "wide"), None),
            P(("narrow", "wide"), None),
            P(),
            P(),
            P(),
            P(),
            P(),
            P(),
            P(("narrow", "wide"), None, None),
            P(("narrow", "wide"), None, None),
        ),
        check_vma=False,
    )
```

profile of v0, /device:TPU:0, one launch (start us, length us, event | category | flops | bytes accessed | tf_op | source)
XLA Modules:
  0.0 751.3 jit_solution(3760716563853040460)
XLA Ops:
  11.9 2.6 copy.147
  14.5 2.6 copy.142
  19.4 7.6 %convolution_convert_fusion = bf16[1024,2304]{1,0:T(8,128)(2,1)} fusion(bf16[768,2304]{1,0:T(8,128)(2,1)S(1)} %copy-done, bf16[1024,768]{0,1:T(8,128)(2,1)} %copy.142, f32[768]{0:T(1024)S(1)} %copy-done.56, f32[1024]{0:T(1024)S(1)} %add_rsqrt_fusion.1), kind=kOutput, calls=%fused_computation.43 | convolution fusion | flops 3629383680 | bytes 9837568 | tf_op jit(solution)/shard_map/dot_general | solution.py:16
  27.0 6.6 copy.143
  33.6 8.8 %reshape.196 = bf16[2,512,3,12,64]{1,0,4,3,2:T(2,128)(2,1)} reshape(bf16[1024,2304]{0,1:T(8,128)(2,1)} %copy.143) | data formatting | bytes 9437184 | tf_op jit(solution)/shard_map/reshape | solution.py:63
  42.4 12.0 %fusion.106 = (bf16[1,512,1,12,64]{1,0,4,3,2:T(2,128)(2,1)}, bf16[1,512,1,12,64]{1,0,4,3,2:T(2,128)(2,1)}, bf16[1,512,1,12,64]{1,0,4,3,2:T(2,128)(2,1)}, bf16[1,...) fusion(bf16[2,512,3,12,64]{1,0,4,3,2:T(2,128)(2,1)} %reshape.196), kind=kLoop, calls=%fused_computation.150 | loop fusion | bytes 9437184 | tf_op jit(solution)/shard_map/slice | solution.py:92
  54.5 13.8 %fusion.1 = f32[512,512,12]{0,2,1:T(8,128)} fusion(s32[512,512]{0,1:T(8,128)S(1)} %copy-done.9, f32[32,12]{0,1:T(8,128)S(1)} %copy-done.55), kind=kOutput, calls=%fused_computation.2 | convolution fusion | flops 1216348160 | bytes 13633024 | tf_op jit(solution)/shard_map/qkb,bh->hqk/dot_general | solution.py:67
  68.3 15.3 %fusion.109 = (f32[12,512]{1,0:T(8,128)S(1)}, f32[12,512,512]{1,2,0:T(8,128)S(1)}) fusion(f32[512,512,12]{0,2,1:T(8,128)} %fusion.1, bf16[1,512,1,12,64]{1,0,4,3,2:T(2,128)(2,1)} %get-tuple-element.78, bf16[1,512,1,12,64]{1,0,4,3,2:T(2,128)(2,1)} %get-tuple-element.74, pred[512,512]{0,1:T(8,128)(4,1)} %broadcast_compare_fusion), kind=kOutput, calls=%fused_computation.153 | convolution fusion | flops 415229952 | bytes 27025408 | tf_op jit(solution)/shard_map/qhd,khd->hqk/dot_general | solution.py:71
  83.7 1.9 fusion.15
  85.6 20.0 %fusion.110 = (f32[12,512]{1,0:T(8,128)S(1)}, f32[12,512,512]{1,2,0:T(8,128)}) fusion(f32[512,512,12]{0,2,1:T(8,128)} %fusion.1, bf16[1,512,1,12,64]{1,0,4,3,2:T(2,128)(2,1)S(1)} %get-tuple-element.76, bf16[1,512,1,12,64]{1,0,4,3,2:T(2,128)(2,1)} %get-tuple-element.77, pred[512,512]{0,1:T(8,128)(4,1)} %broadcast_compare_fusion.1), kind=kOutput, calls=%fused_computation.154 | convolution fusion | flops 415229952 | bytes 27025408 | tf_op jit(solution)/shard_map/qhd,khd->hqk/dot_general | solution.py:71
  105.6 6.5 fusion.14
  112.1 6.0 fusion.74
  118.3 2.5 fusion.73
  124.5 3.7 fusion.48
  128.2 5.2 all-to-all-start
  133.4 2.6 copy.159
  139.7 5.2 fusion.49
  144.9 12.8 %all-to-all-done = bf16[4,8,40,768]{3,2,1,0:T(8,128)(2,1)} async-done(((bf16[4,8,40,768]{3,2,1,0:T(8,128)(2,1)}), bf16[4,8,40,768]{3,2,1,0:T(8,128)(2,1)}, u32[]{:S(2)}, u32[]{:S(2)}) %all-to-all-start) | async-done | bytes 1966112 | tf_op jit(solution)/shard_map/all_to_all | solution.py:119
  157.7 4.4 all-to-all-start.4
  162.1 3.0 copy.155
  165.1 20.3 %all-to-all-done.4 = bf16[4,8,40,768]{3,2,1,0:T(8,128)(2,1)} async-done(((bf16[4,8,40,768]{3,2,1,0:T(8,128)(2,1)}), bf16[4,8,40,768]{3,2,1,0:T(8,128)(2,1)}, u32[]{:S(2)}, u32[]{:S(2)}) %all-to-all-start.4) | async-done | bytes 1966112 | tf_op jit(solution)/shard_map/all_to_all | solution.py:150
  185.4 4.9 all-to-all-start.1
  190.3 3.0 copy.160
  193.2 43.4 %all-to-all-done.1 = bf16[4,8,40,768]{3,2,0,1:T(8,128)(2,1)} async-done(((bf16[4,8,40,768]{3,2,0,1:T(8,128)(2,1)}), bf16[4,8,40,768]{3,2,0,1:T(8,128)(2,1)}, u32[]{:S(2)}, u32[]{:S(2)}) %all-to-all-start.1) | async-done | bytes 1966112 | tf_op jit(solution)/shard_map/all_to_all | solution.py:118
  236.6 4.6 all-to-all-start.5
  244.2 8.2 %fusion.39 = f32[1280,3072]{1,0:T(8,128)S(1)} fusion(bf16[1280,768]{1,0:T(8,128)(2,1)S(1)} %bitcast.152, bf16[1,768,3072]{2,1,0:T(8,128)(2,1)} %param.20), kind=kOutput, calls=%fused_computation.65 | convolution fusion | flops 6039797760 | bytes 22413312 | tf_op jit(solution)/shard_map/dot_general | solution.py:16
  252.4 5.4 copy-done.68
  257.8 12.5 %fusion.45 = bf16[1280,768]{1,0:T(8,128)(2,1)} fusion(bf16[1,3072,768]{2,1,0:T(8,128)(2,1)} %param.21, f32[1280,3072]{1,0:T(8,128)S(1)} %fusion.39), kind=kOutput, calls=%fused_computation.70 | convolution fusion | flops 6076170240 | bytes 22413312 | tf_op jit(solution)/shard_map/dot_general | solution.py:16
  270.3 17.1 %all-to-all-done.5 = bf16[4,8,40,768]{3,2,0,1:T(8,128)(2,1)} async-done(((bf16[4,8,40,768]{3,2,0,1:T(8,128)(2,1)}), bf16[4,8,40,768]{3,2,0,1:T(8,128)(2,1)}, u32[]{:S(2)}, u32[]{:S(2)}) %all-to-all-start.5) | async-done | bytes 1966112 | tf_op jit(solution)/shard_map/all_to_all | solution.py:149
  287.4 4.7 all-to-all-start.2
  293.8 18.1 %fusion.11 = bf16[1280,3072]{1,0:T(8,128)(2,1)S(1)} fusion(f32[1280,3072]{1,0:T(8,128)} %copy-done.68, bf16[1280,768]{1,0:T(8,128)(2,1)S(1)} %bitcast.150, bf16[1,3072,768]{2,1,0:T(8,128)(2,1)} %param.21), kind=kOutput, calls=%fused_computation.14 | convolution fusion | flops 6118440960 | bytes 30277632 | tf_op jit(solution)/shard_map/dot_general | solution.py:24
  312.0 3.2 copy-done.67
  315.2 9.8 %fusion.42 = bf16[1280,768]{1,0:T(8,128)(2,1)} fusion(bf16[1280,3072]{1,0:T(8,128)(2,1)S(1)} %fusion.11, bf16[1,768,3072]{2,1,0:T(8,128)(2,1)} %param.20), kind=kOutput, calls=%fused_computation.69 | convolution fusion | flops 6040780800 | bytes 14548992 | tf_op jit(solution)/shard_map/dot_general | solution.py:24
  325.0 4.4 all-to-all-start.6
  329.4 3.0 copy.157
  332.4 20.7 %all-to-all-done.6 = bf16[4,8,40,768]{3,2,1,0:T(8,128)(2,1)} async-done(((bf16[4,8,40,768]{3,2,1,0:T(8,128)(2,1)}), bf16[4,8,40,768]{3,2,1,0:T(8,128)(2,1)}, u32[]{:S(2)}, u32[]{:S(2)}) %all-to-all-start.6) | async-done | bytes 1966112 | tf_op jit(solution)/shard_map/all_to_all | solution.py:167
  353.0 4.4 all-to-all-start.3
  357.4 3.0 copy.162
  360.4 43.3 %all-to-all-done.3 = bf16[4,8,40,768]{3,2,0,1:T(8,128)(2,1)} async-done(((bf16[4,8,40,768]{3,2,0,1:T(8,128)(2,1)}), bf16[4,8,40,768]{3,2,0,1:T(8,128)(2,1)}, u32[]{:S(2)}, u32[]{:S(2)}) %all-to-all-start.3) | async-done | bytes 1966112 | tf_op jit(solution)/shard_map/all_to_all | solution.py:133
  403.7 4.3 all-to-all-start.7
  409.5 11.9 %convolution_bitcast_fusion.1 = f32[1,768,3072]{2,1,0:T(8,128)} fusion(bf16[1280,768]{1,0:T(8,128)(2,1)} %bitcast.153, bf16[1280,3072]{1,0:T(8,128)(2,1)} %copy-done.67), kind=kOutput, calls=%fused_computation.42 | convolution fusion | flops 6039797760 | bytes 19267584 | tf_op jit(solution)/shard_map/dot_general | solution.py:20
  423.4 4.0 fusion.58
  429.2 25.0 %all-to-all-done.7 = bf16[4,8,40,768]{3,2,0,1:T(8,128)(2,1)} async-done(((bf16[4,8,40,768]{3,2,0,1:T(8,128)(2,1)}), bf16[4,8,40,768]{3,2,0,1:T(8,128)(2,1)}, u32[]{:S(2)}, u32[]{:S(2)}) %all-to-all-start.7) | async-done | bytes 1966112 | tf_op jit(solution)/shard_map/all_to_all | solution.py:166
  456.0 2.4 fusion.26
  460.8 2.2 convert_add_fusion.1
  463.0 2.8 fusion.90
  468.0 7.7 %fusion.78 = bf16[512,1,12,64]{0,3,2,1:T(8,128)(2,1)} fusion(bf16[512,12,64]{0,2,1:T(8,128)(2,1)S(1)} %bitcast.144, f32[12,512,512]{1,2,0:T(8,128)} %get-tuple-element.88, f32[12,512]{1,0:T(8,128)S(1)} %copy-done.35), kind=kOutput, calls=%fused_computation.108 | convolution fusion | flops 409337856 | bytes 14180352 | tf_op jit(solution)/shard_map/hqk,qhd->khd/dot_general | solution.py:195
  475.8 9.5 %multiply_reduce_fusion.1 = (f32[12,512]{1,0:T(8,128)}, f32[12,512,512]{1,2,0:T(8,128)}) fusion(f32[12,512,512]{1,2,0:T(8,128)} %get-tuple-element.88, f32[12,512]{1,0:T(8,128)S(1)} %copy-done.35, bf16[512,12,64]{0,2,1:T(8,128)(2,1)S(1)} %bitcast.145, bf16[1,512,1,12,64]{1,0,4,3,2:T(2,128)(2,1)S(1)} %copy-done.22), kind=kOutput, calls=%fused_computation.25 | convolution fusion | flops 412084224 | bytes 26787840 | tf_op jit(solution)/shard_map/qhd,khd->hqk/dot_general | solution.py:198
  485.3 2.9 fusion.75
  488.3 6.6 multiply_reduce_fusion
  494.9 27.0 %convert_add_fusion = (f32[12,512,512]{1,2,0:T(8,128)}, bf16[12,512,512]{1,2,0:T(8,128)(2,1)}, bf16[12,512,512]{1,2,0:T(8,128)(2,1)}) fusion(f32[12,512,512]{1,2,0:T(8,128)} %get-tuple-element.97, f32[12,512]{1,0:T(8,128)} %get-tuple-element.96, f32[12,512,512]{1,2,0:T(8,128)} %get-tuple-element.88, f32[12,512]{1,0:T(8,128)} %get-tuple-element.102, ...), kind=kLoop, calls=%fused_computation.20 | loop fusion | flops 34603008 | bytes 75595776 | tf_op jit(solution)/shard_map/add | solution.py:203
  521.9 5.0 fusion.84
  526.9 4.1 fusion.83
  531.0 2.0 fusion.82
  537.9 6.0 fusion.59
  543.9 14.7 %convolution_bitcast_fusion = f32[1,3072,768]{2,1,0:T(8,128)} fusion(bf16[1280,768]{1,0:T(8,128)(2,1)} %bitcast.151, f32[1280,3072]{1,0:T(8,128)} %copy-done.68), kind=kOutput, calls=%fused_computation.41 | convolution fusion | flops 6075187200 | bytes 27131904 | tf_op jit(solution)/shard_map/dot_general | solution.py:20
  558.5 2.6 copy.175
  561.1 7.2 fusion.55
  568.4 2.4 fusion.54
  570.8 3.6 copy.176
  574.3 24.8 %fusion.87 = f32[32,12]{0,1:T(8,128)S(1)} fusion(f32[12,512,512]{1,2,0:T(8,128)} %get-tuple-element.70, s32[512,512]{0,1:T(8,128)} %copy.147), kind=kOutput, calls=%fused_computation.115 | convolution fusion | flops 1216348160 | bytes 13633024 | tf_op jit(solution)/shard_map/qkb,hqk->bh/dot_general | solution.py:216
  599.2 38.5 %all-reduce = (f32[768]{0:T(1024)}, f32[32,12]{0,1:T(8,128)}, f32[768]{0:T(1024)}) all-reduce(f32[768]{0:T(1024)S(1)} %get-tuple-element.62, f32[32,12]{0,1:T(8,128)S(1)} %fusion.87, f32[768]{0:T(1024)S(1)} %copy-done.54), channel_id=1, replica_groups=mesh['narrow'=4,'wide'=8] {'narrow','wide'}, use_global_device_ids=true, to_apply=%region_16.17 | all-reduce | flops 1920 | bytes 15360 | tf_op jit(solution)/shard_map/psum | solution.py:221
  637.7 97.8 %all-reduce.4.cloned.1.call-done = (f32[768,2304]{1,0:T(8,128)}, f32[768,768]{1,0:T(8,128)}, f32[768,32]{0,1:T(8,128)}) async-done(((f32[768,2304]{1,0:T(8,128)}, f32[768,768]{1,0:T(8,128)}, f32[768,32]{0,1:T(8,128)}), (f32[768,2304]{1,0:T(8,128)}, f32[768,768]{1,0:T(8,128)}, f32[768,32]{0,1:T(8,128)})) %all-reduce.4.cloned.1.call-update) | async-done | bytes 9535504 | tf_op jit(solution)/shard_map/psum | solution.py:221
  735.4 6.6 copy.236
  (181 shorter events, 37.5 us)
Async XLA Ops:
  7.2 12.3 %copy-start = (bf16[768,2304]{1,0:T(8,128)(2,1)S(1)}, bf16[768,2304]{1,0:T(8,128)(2,1)}, u32[]{:S(2)}) copy-start(bf16[768,2304]{1,0:T(8,128)(2,1)} %param.15) | copy-start | bytes 10616836
  9.3 115.2 %copy-start.58 = (s32[1024]{0:T(1024)}, s32[1024]{0:T(1024)S(1)}, u32[]{:S(2)}) copy-start(s32[1024]{0:T(1024)S(1)} %add_select_fusion) | copy-start | bytes 12292
  11.9 7.6 %copy-start.56 = (f32[768]{0:T(1024)S(1)}, f32[768]{0:T(1024)}, u32[]{:S(2)}) copy-start(f32[768]{0:T(1024)} %param.14) | copy-start | bytes 9220
  42.4 12.0 %copy-start.9 = (s32[512,512]{0,1:T(8,128)S(1)}, s32[512,512]{0,1:T(8,128)}, u32[]{:S(2)}) copy-start(s32[512,512]{0,1:T(8,128)} %copy.147) | copy-start | bytes 3145732
  42.4 12.0 %copy-start.55 = (f32[32,12]{0,1:T(8,128)S(1)}, f32[32,12]{0,1:T(8,128)}, u32[]{:S(2)}) copy-start(f32[32,12]{0,1:T(8,128)} %param.17) | copy-start | bytes 4612
  54.5 31.1 %copy-start.10 = (bf16[1,512,1,12,64]{1,0,4,3,2:T(2,128)(2,1)}, bf16[1,512,1,12,64]{1,0,4,3,2:T(2,128)(2,1)S(1)}, u32[]{:S(2)}) copy-start(bf16[1,512,1,12,64]{1,0,4,3,2:T(2,128)(2,1)S(1)} %get-tuple-element.76) | copy-start | bytes 2359300
  83.7 34.5 %copy-start.1 = (f32[12,512,512]{1,2,0:T(8,128)}, f32[12,512,512]{1,2,0:T(8,128)S(1)}, u32[]{:S(2)}) copy-start(f32[12,512,512]{1,2,0:T(8,128)S(1)} %get-tuple-element.86) | copy-start | bytes 37748740
  83.7 34.5 %copy-start.36 = (f32[12,512]{1,0:T(8,128)}, f32[12,512]{1,0:T(8,128)S(1)}, u32[]{:S(2)}) copy-start(f32[12,512]{1,0:T(8,128)S(1)} %get-tuple-element.85) | copy-start | bytes 73732
  85.6 32.6 %copy-start.39 = (f32[12,512]{1,0:T(8,128)}, f32[12,512]{1,0:T(8,128)S(1)}, u32[]{:S(2)}) copy-start(f32[12,512]{1,0:T(8,128)S(1)} %fusion.15) | copy-start | bytes 73732
  105.6 6.5 copy-start.37
  105.6 6.5 copy-start.21
  112.1 6.1 copy-start.40
  112.1 6.1 copy-start.19
  118.2 2.6 copy-start.63
  118.2 2.6 copy-start.4
  118.2 2.6 copy-start.61
  120.8 3.3 copy-start.42
  124.5 3.7 copy-start.17
  128.2 29.5 %all-to-all-start = ((bf16[4,8,40,768]{3,2,1,0:T(8,128)(2,1)}), bf16[4,8,40,768]{3,2,1,0:T(8,128)(2,1)}, u32[]{:S(2)}, u32[]{:S(2)}) async-start(bf16[4,8,40,768]{3,2,1,0:T(8,128)(2,1)} %bitcast.155), calls=%async_computation | async-start | bytes 3932160 | tf_op jit(solution)/shard_map/all_to_all | solution.py:119
  133.4 5.7 copy-start.43
  157.7 27.7 %all-to-all-start.4 = ((bf16[4,8,40,768]{3,2,1,0:T(8,128)(2,1)}), bf16[4,8,40,768]{3,2,1,0:T(8,128)(2,1)}, u32[]{:S(2)}, u32[]{:S(2)}) async-start(bf16[4,8,40,768]{3,2,1,0:T(8,128)(2,1)} %bitcast.156), calls=%async_computation.4 | async-start | bytes 3932160 | tf_op jit(solution)/shard_map/all_to_all | solution.py:150
  185.4 51.2 %all-to-all-start.1 = ((bf16[4,8,40,768]{3,2,0,1:T(8,128)(2,1)}), bf16[4,8,40,768]{3,2,0,1:T(8,128)(2,1)}, u32[]{:S(2)}, u32[]{:S(2)}) async-start(bf16[4,8,40,768]{3,2,0,1:T(8,128)(2,1)} %copy.155), calls=%async_computation.1 | async-start | bytes 3932160 | tf_op jit(solution)/shard_map/all_to_all | solution.py:118
  236.6 50.8 %all-to-all-start.5 = ((bf16[4,8,40,768]{3,2,0,1:T(8,128)(2,1)}), bf16[4,8,40,768]{3,2,0,1:T(8,128)(2,1)}, u32[]{:S(2)}, u32[]{:S(2)}) async-start(bf16[4,8,40,768]{3,2,0,1:T(8,128)(2,1)} %copy.160), calls=%async_computation.5 | async-start | bytes 3932160 | tf_op jit(solution)/shard_map/all_to_all | solution.py:149
  252.4 5.4 copy-start.68
  287.4 37.5 %all-to-all-start.2 = ((bf16[4,8,40,768]{3,2,1,0:T(8,128)(2,1)}), bf16[4,8,40,768]{3,2,1,0:T(8,128)(2,1)}, u32[]{:S(2)}, u32[]{:S(2)}) async-start(bf16[4,8,40,768]{3,2,1,0:T(8,128)(2,1)} %bitcast.154), calls=%async_computation.2 | async-start | bytes 3932160 | tf_op jit(solution)/shard_map/all_to_all | solution.py:134
  293.8 18.1 %copy-start.32 = (bf16[4,8,40,768]{3,2,1,0:T(8,128)(2,1)}, bf16[4,8,40,768]{3,2,1,0:T(8,128)(2,1)S(1)}, u32[]{:S(2)}) copy-start(bf16[4,8,40,768]{3,2,1,0:T(8,128)(2,1)S(1)} %copy.161) | copy-start | bytes 5898244
  312.0 3.2 copy-start.67
  325.0 28.1 %all-to-all-start.6 = ((bf16[4,8,40,768]{3,2,1,0:T(8,128)(2,1)}), bf16[4,8,40,768]{3,2,1,0:T(8,128)(2,1)}, u32[]{:S(2)}, u32[]{:S(2)}) async-start(bf16[4,8,40,768]{3,2,1,0:T(8,128)(2,1)} %bitcast.157), calls=%async_computation.6 | async-start | bytes 3932160 | tf_op jit(solution)/shard_map/all_to_all | solution.py:167
  353.0 50.6 %all-to-all-start.3 = ((bf16[4,8,40,768]{3,2,0,1:T(8,128)(2,1)}), bf16[4,8,40,768]{3,2,0,1:T(8,128)(2,1)}, u32[]{:S(2)}, u32[]{:S(2)}) async-start(bf16[4,8,40,768]{3,2,0,1:T(8,128)(2,1)} %copy.157), calls=%async_computation.3 | async-start | bytes 3932160 | tf_op jit(solution)/shard_map/all_to_all | solution.py:133
  403.7 50.6 %all-to-all-start.7 = ((bf16[4,8,40,768]{3,2,0,1:T(8,128)(2,1)}), bf16[4,8,40,768]{3,2,0,1:T(8,128)(2,1)}, u32[]{:S(2)}, u32[]{:S(2)}) async-start(bf16[4,8,40,768]{3,2,0,1:T(8,128)(2,1)} %copy.162), calls=%async_computation.7 | async-start | bytes 3932160 | tf_op jit(solution)/shard_map/all_to_all | solution.py:166
  408.0 327.4 %all-reduce.4.cloned.1.call-start = ((), (), s32[]{:S(2)}) async-start(), calls=%async_computation.8 | async-start | bytes 19070976 | tf_op jit(solution)/shard_map/psum | solution.py:221
  423.4 4.0 copy-start.45
  423.4 4.6 copy-start.18
  423.4 4.6 copy-start.30
  423.4 4.6 copy-start.48
  456.0 2.4 copy-start.3
  456.0 2.4 copy-start.31
  456.0 2.4 copy-start.38
  456.0 2.4 copy-start.49
  456.0 2.4 copy-start.51
  458.5 2.4 copy-start.25
  458.5 2.4 copy-start.46
  460.8 2.2 copy-start.64
  460.8 2.2 copy-start.66
  463.0 2.9 copy-start.7
  463.0 2.8 copy-start.62
  468.0 7.7 %copy-start.22 = (bf16[1,512,1,12,64]{1,0,4,3,2:T(2,128)(2,1)S(1)}, bf16[1,512,1,12,64]{1,0,4,3,2:T(2,128)(2,1)}, u32[]{:S(2)}) copy-start(bf16[1,512,1,12,64]{1,0,4,3,2:T(2,128)(2,1)} %get-tuple-element.73) | copy-start | bytes 2359300
  468.0 17.3 %slice-start = ((s8[12582912]{0:T(1024)(128)(4,1)}), s8[4194304]{0:T(1024)(128)(4,1)S(1)}, s32[]{:S(2)}) async-start(s8[12582912]{0:T(1024)(128)(4,1)} %bitcast.138), calls=%async_computation.9 | async-start | bytes 8388608
  468.0 17.3 %slice-start.1 = ((s8[12582912]{0:T(1024)(128)(4,1)}), s8[4194304]{0:T(1024)(128)(4,1)S(1)}, s32[]{:S(2)}) async-start(s8[12582912]{0:T(1024)(128)(4,1)} %bitcast.138), calls=%async_computation.10 | async-start | bytes 8388608
  475.8 9.6 %slice-start.2 = ((s8[12582912]{0:T(1024)(128)(4,1)}), s8[4194304]{0:T(1024)(128)(4,1)S(1)}, s32[]{:S(2)}) async-start(s8[12582912]{0:T(1024)(128)(4,1)} %bitcast.138), calls=%async_computation.11 | async-start | bytes 8388608
  475.8 9.6 %copy-start.34 = (f32[12,512]{1,0:T(8,128)S(1)}, f32[12,512]{1,0:T(8,128)}, u32[]{:S(2)}) copy-start(f32[12,512]{1,0:T(8,128)} %get-tuple-element.101) | copy-start | bytes 73732
  485.3 2.9 copy-start.20
  494.9 27.0 %copy-start.14 = (bf16[1,512,1,12,64]{1,0,4,3,2:T(2,128)(2,1)S(1)}, bf16[1,512,1,12,64]{1,0,4,3,2:T(2,128)(2,1)}, u32[]{:S(2)}) copy-start(bf16[1,512,1,12,64]{1,0,4,3,2:T(2,128)(2,1)} %get-tuple-element.74) | copy-start | bytes 2359300
  521.9 5.0 copy-start.13
  521.9 9.1 %slice-start.3 = ((s8[6291456]{0:T(1024)(128)(4,1)}), s8[4194304]{0:T(1024)(128)(4,1)S(1)}, s32[]{:S(2)}) async-start(s8[6291456]{0:T(1024)(128)(4,1)} %bitcast.140), calls=%async_computation.12 | async-start | bytes 8388608
  526.9 4.1 slice-start.4
  526.9 4.1 copy-start.12
  535.3 2.5 copy-start.5
  535.3 2.5 copy-start.53
  535.3 2.5 copy-start.57
  561.1 7.2 copy-start.6
  561.1 7.2 copy-start.8
  574.3 24.8 %copy-start.54 = (f32[768]{0:T(1024)S(1)}, f32[768]{0:T(1024)}, u32[]{:S(2)}) copy-start(f32[768]{0:T(1024)} %get-tuple-element.60) | copy-start | bytes 9220
  735.4 6.6 copy-start.26
  (19 other events, 25.0 us)
Sparse Core Ops, SparseCore 0:
  544.0 191.3 all-reduce.3
where the time goes:
time: 761 us; the launch traced here: 751 us
  waiting for transfers between devices  280 us (37%)
  matrix products  245 us (32%)
  local copies, waits for them, and re-layouts  88.8 us (12%)
  other arithmetic  46.6 us (6%)
  blocking collectives  38.5 us (5%)
  starting transfers between devices  36.9 us (5%)
  between operations  15.4 us (2%)
    psum x1, waiting for transfers between devices, local(): lax.psum((grad_w_qkv, grad_w_out, grad_table, grad_gain_one, grad_gain_tw...  97.8 us
    all_to_all x1, waiting for transfers between devices, local(): lax.all_to_all(lax.all_to_all(packed, 'narrow', split_axis=0, concat_axis...  43.4 us
    all_to_all x1, waiting for transfers between devices, local(): lax.all_to_all(lax.all_to_all(expert_out, 'narrow', split_axis=0, concat_...  43.3 us
    dot_general x7, matrix products, matmul_tn(): lax.dot_general(a, b, (((0,), (0,)), ((), ())), preferred_element_type=jn...  42.9 us
    dot_general x8, matrix products, matmul(): return jnp.dot(a, b, preferred_element_type=jnp.float32)  42.1 us
    unnamed x156, local copies, waits for them, and re-layouts  41.8 us
    psum x1, blocking collectives, local(): lax.psum((grad_w_qkv, grad_w_out, grad_table, grad_gain_one, grad_gain_tw...  38.5 us
    dot_general x5, matrix products, matmul_nt(): lax.dot_general(a, b, (((1,), (1,)), ((), ())), preferred_element_type=jn...  38.3 us
  transfers between devices with their start and end apart: 9, of which 8 were waited for; matrix products, arithmetic and copies ran while one was open for 20% of the time, Pallas kernels for 0%

commit v1 on v0

v1 whole, which is shorter than its diff:
```python
import functools
import jax
import jax.numpy as jnp
from jax import lax
from jax.experimental import pallas as pl
from jax.experimental.pallas import tpu as pltpu
from jax.sharding import PartitionSpec as P

HEADS = 12
HEAD_DIM = 64
LEN = 512
BUCKETS = 32
EPS = 1e-06
LANES = 128
HALF = 256
GROUP = 4
PAIR = 2
GROUPS = HEADS // GROUP
GW = GROUP * HEAD_DIM
F32 = jnp.float32
BF16 = jnp.bfloat16
MIB = 1024 * 1024


def dot_nn(a, b):
    return lax.dot_general(a, b, (((1,), (0,)), ((), ())), preferred_element_type=F32)


def dot_tn(a, b):
    return lax.dot_general(a, b, (((0,), (0,)), ((), ())), preferred_element_type=F32)


def dot_nt(a, b):
    return lax.dot_general(a, b, (((1,), (1,)), ((), ())), preferred_element_type=F32)


def whole(shape):
    rank = len(shape)
    return pl.BlockSpec(shape, lambda *g: (0,) * rank, pipeline_mode=pl.Buffered(1))


def split3(v):
    high = v.astype(BF16)
    rest = v - high.astype(F32)
    mid = rest.astype(BF16)
    low = (rest - mid.astype(F32)).astype(BF16)
    return high, mid, low


def slots_kernel(experts, cap, capp, ids_ref, g_ref, slot_ref, pos_ref, packed_ref):
    tok = ids_ref.shape[1]
    ids = ids_ref[...]
    hot = lax.broadcasted_iota(jnp.int32, (experts, tok), 0) == ids
    before = (
        lax.broadcasted_iota(jnp.int32, (tok, tok), 0)
        < lax.broadcasted_iota(jnp.int32, (tok, tok), 1)
    )
    counts = dot_nn(hot.astype(F32).astype(BF16), before.astype(F32).astype(BF16))
    pos = jnp.sum(jnp.where(hot, counts, 0.0), axis=0, keepdims=True).astype(jnp.int32)
    kept = pos < cap
    slot = jnp.where(kept, ids * capp + pos, -1)
    slot_ref[...] = slot
    pos_ref[...] = jnp.where(kept, pos, -1)
    rows = packed_ref.shape[0]
    step = 256

    @pl.loop(0, rows // step)
    def _(r):
        base = pl.multiple_of(r * step, step)
        table = (lax.broadcasted_iota(jnp.int32, (step, tok), 0) + base == slot)
        packed_ref[pl.ds(base, step), :] = dot_nn(
            table.astype(F32).astype(BF16), g_ref[...]
        ).astype(BF16)


def make_slots(experts, cap, capp, ids_row, g):
    tok, width = g.shape
    return pl.pallas_call(
        functools.partial(slots_kernel, experts, cap, capp),
        out_shape=(
            jax.ShapeDtypeStruct((1, tok), jnp.int32),
            jax.ShapeDtypeStruct((1, tok), jnp.int32),
            jax.ShapeDtypeStruct((experts * capp, width), BF16),
        ),
        compiler_params=pltpu.CompilerParams(vmem_limit_bytes=40 * MIB),
        name="slots",
    )(ids_row, g)


def front_kernel(
    hid_ref, gain1_ref, wq_ref, wk_ref, wv_ref, wout_ref, tab_ref, gain2_ref, wr_ref,
    ids_ref, slot_ref, pos_ref, segr_ref, segc_ref, rel_ref,
    n1_ref, q_ref, k_ref, v_ref, p_ref, attn_ref, resid_ref, n2_ref, route_ref, gate_ref,
    packed_ref, gpack_ref,
    relt, mask, bias,
):
    step = pl.program_id(0)
    seqs = segr_ref.shape[0]
    tok = hid_ref.shape[0]

    @pl.when(step == 0)
    def _():
        for t in range(0, tok, HALF):
            x = hid_ref[t:t + HALF, :].astype(F32).T
            scale = lax.rsqrt(jnp.mean(x * x, axis=0, keepdims=True) + EPS)
            n1_ref[:, t:t + HALF] = (x * scale * gain1_ref[...]).astype(BF16)
        relt[...] = rel_ref[...].T
        for s in range(seqs):
            mask[s] = jnp.where(segc_ref[s] == segr_ref[s], 0.0, -1000000000.0)

    for w_ref, o_ref in ((wq_ref, q_ref), (wk_ref, k_ref), (wv_ref, v_ref)):
        o_ref[...] = dot_tn(w_ref[...], n1_ref[...]).astype(BF16)

    @pl.loop(0, GROUP)
    def _(h):
        head = step * GROUP + h
        row = tab_ref[pl.ds(head, 1), :]
        line = jnp.broadcast_to(row, (LEN, LANES))
        for c in range(0, LEN, LANES):
            bias[:, c:c + LANES] = jnp.take_along_axis(line, relt[:, c:c + LANES], axis=1)
        at = pl.ds(pl.multiple_of(h * HEAD_DIM, HEAD_DIM), HEAD_DIM)
        out_at = pl.ds(pl.multiple_of(head * HEAD_DIM, HEAD_DIM), HEAD_DIM)
        for s in range(seqs):
            key = k_ref[at, s * LEN:(s + 1) * LEN]
            value = v_ref[at, s * LEN:(s + 1) * LEN]
            for c in range(0, LEN, HALF):
                cols = slice(s * LEN + c, s * LEN + c + HALF)
                query = q_ref[at, cols] * jnp.asarray(HEAD_DIM ** -0.5, BF16)
                score = dot_tn(key, query) + bias[:, c:c + HALF] + mask[s, :, c:c + HALF]
                peak = jnp.max(score, axis=0, keepdims=True)
                weight = jnp.exp(score - peak)
                total = jnp.sum(weight, axis=0, keepdims=True)
                prob = (weight * (1.0 / total)).astype(BF16)
                p_ref[h, s, :, c:c + HALF] = prob
                attn_ref[out_at, cols] = dot_nn(value, prob).astype(BF16)

    @pl.when(step == pl.num_programs(0) - 1)
    def _():
        experts = route_ref.shape[0]
        for t in range(0, tok, HALF):
            cols = slice(t, t + HALF)
            x = hid_ref[t:t + HALF, :].astype(F32).T
            resid = x + dot_tn(wout_ref[...], attn_ref[:, cols])
            resid_ref[:, cols] = resid
            scale = lax.rsqrt(jnp.mean(resid * resid, axis=0, keepdims=True) + EPS)
            n2 = (resid * scale * gain2_ref[...]).astype(BF16)
            n2_ref[:, cols] = n2
            logits = dot_tn(wr_ref[...], n2)
            top = jnp.max(logits, axis=0, keepdims=True)
            e = jnp.exp(logits - top)
            route = e / jnp.sum(e, axis=0, keepdims=True)
            route_ref[:, cols] = route
            hot = lax.broadcasted_iota(jnp.int32, (experts, HALF), 0) == ids_ref[:, cols]
            gate_ref[:, cols] = jnp.sum(jnp.where(hot, route, 0.0), axis=0, keepdims=True)
        hot = lax.broadcasted_iota(jnp.int32, (experts, tok), 0) == ids_ref[...]
        gates = jnp.where(hot, gate_ref[...], 0.0)
        place = (
            lax.broadcasted_iota(jnp.int32, (LANES, tok), 0) == pos_ref[...]
        ).astype(F32).astype(BF16)
        parts = [dot_nt(part, place) for part in split3(gates)]
        which = lax.broadcasted_iota(jnp.int32, (experts, 8, LANES), 1)
        spread = [jnp.broadcast_to(part[:, None, :], which.shape) for part in parts]
        gpack_ref[...] = jnp.where(
            which == 0, spread[0],
            jnp.where(which == 1, spread[1], jnp.where(which == 2, spread[2], 0.0)),
        ).astype(BF16)
        rows = packed_ref.shape[0]

        @pl.loop(0, rows // HALF)
        def _(r):
            base = pl.multiple_of(r * HALF, HALF)
            table = (lax.broadcasted_iota(jnp.int32, (HALF, tok), 0) + base == slot_ref[...])
            packed_ref[pl.ds(base, HALF), :] = dot_nt(
                table.astype(F32).astype(BF16), n2_ref[...]
            ).astype(BF16)


def front(hidden, gain1, w_qkv, w_out, table, gain2, w_router, ids, slot, pos, seg, rel, rows):
    tok, width = hidden.shape
    experts = w_router.shape[1]
    seqs = seg.shape[0]
    wspec = lambda part: pl.BlockSpec((width, GW), lambda i: (0, part * GROUPS + i))
    qspec = pl.BlockSpec((GW, tok), lambda i: (i, 0))
    sd = jax.ShapeDtypeStruct
    outs = (
        sd((width, tok), BF16), sd((width, tok), BF16), sd((width, tok), BF16),
        sd((width, tok), BF16), sd((HEADS, seqs, LEN, LEN), BF16), sd((width, tok), BF16),
        sd((width, tok), F32), sd((width, tok), BF16), sd((experts, tok), F32), sd((1, tok), F32),
        sd((rows, width), BF16), sd((experts, 8, LANES), BF16),
    )
    return pl.pallas_call(
        front_kernel,
        grid=(GROUPS,),
        in_specs=[
            whole((tok, width)), whole((width, 1)), wspec(0), wspec(1), wspec(2),
            whole((width, width)), whole((HEADS, LANES)), whole((width, 1)),
            whole((width, experts)), whole((1, tok)), whole((1, tok)), whole((1, tok)),
            whole((seqs, 1, LEN)), whole((seqs, LEN, 1)), whole((LEN, LEN)),
        ],
        out_specs=(
            whole((width, tok)), qspec, qspec, qspec,
            pl.BlockSpec((GROUP, seqs, LEN, LEN), lambda i: (i, 0, 0, 0)),
            whole((width, tok)), whole((width, tok)), whole((width, tok)),
            whole((experts, tok)), whole((1, tok)), whole((rows, width)),
            whole((experts, 8, LANES)),
        ),
        out_shape=outs,
        scratch_shapes=[
            pltpu.VMEM((LEN, LEN), jnp.int32),
            pltpu.VMEM((seqs, LEN, LEN), F32),
            pltpu.VMEM((LEN, LEN), F32),
        ],
        compiler_params=pltpu.CompilerParams(vmem_limit_bytes=58 * MIB),
        name="front",
    )(
        hidden, gain1.reshape(width, 1), w_qkv, w_qkv, w_qkv, w_out, table,
        gain2.reshape(width, 1), w_router, ids, slot, pos,
        seg.reshape(seqs, 1, LEN), seg.reshape(seqs, LEN, 1), rel,
    )


def combine_kernel(rows_ref, slot_ref, gate_ref, resid_ref, out_ref):
    total = rows_ref.shape[0]
    cols = slot_ref.shape[1]
    table = lax.broadcasted_iota(jnp.int32, (total, cols), 0) == slot_ref[...]
    combined = dot_tn(rows_ref[...], table.astype(F32).astype(BF16))
    out_ref[...] = (resid_ref[...] + gate_ref[...] * combined).T.astype(BF16)


def combine(rows, slot, gate, resid):
    total, width = rows.shape
    tok = slot.shape[1]
    line = pl.BlockSpec((1, HALF), lambda i: (0, i))
    return pl.pallas_call(
        combine_kernel,
        grid=(tok // HALF,),
        in_specs=[
            whole((total, width)), line, line, pl.BlockSpec((width, HALF), lambda i: (0, i)),
        ],
        out_specs=pl.BlockSpec((HALF, width), lambda i: (i, 0)),
        out_shape=jax.ShapeDtypeStruct((tok, width), BF16),
        compiler_params=pltpu.CompilerParams(vmem_limit_bytes=40 * MIB),
        name="combine",
    )(rows, slot, gate, resid)


def norm_back(grad, source, gain):
    scale = lax.rsqrt(jnp.mean(source * source, axis=0, keepdims=True) + EPS)
    normed = source * scale
    scaled = grad * gain
    inner = jnp.mean(scaled * normed, axis=0, keepdims=True)
    return scale * (scaled - normed * inner), jnp.sum(grad * normed, axis=1, keepdims=True)


def back_kernel(
    dx_ref, gg_ref, slot_ref, pos_ref, ids_ref, route_ref, gate_ref, resid_ref, n2_ref, attn_ref,
    g_ref, hid_ref, n1_ref, q_ref, k_ref, v_ref, p_ref, gain1_ref, gain2_ref, wr_ref, wout_ref,
    wq_ref, wk_ref, wv_ref,
    ingrad_ref, gain1g_ref, gq_ref, gk_ref, gv_ref, outg_ref, gain2g_ref, routerg_ref, ds_ref,
    gres, ga, gn1, dq, dk, dv,
):
    step = pl.program_id(0)
    pair = pl.program_id(1)
    tok = hid_ref.shape[0]
    seqs = tok // LEN
    experts = route_ref.shape[0]
    total = dx_ref.shape[0]

    @pl.when((step == 0) & (pair == 0))
    def _():
        hot = lax.broadcasted_iota(jnp.int32, (experts, tok), 0) == ids_ref[...]
        place = (
            lax.broadcasted_iota(jnp.int32, (LANES, tok), 0) == pos_ref[...]
        ).astype(F32).astype(BF16)
        found = dot_nn(gg_ref[...].reshape(experts * 8, LANES), place)
        found = jnp.sum(found.reshape(experts, 8, tok), axis=1)
        grad_gate = jnp.sum(jnp.where(hot, found, 0.0), axis=0, keepdims=True)
        grad_logits = (
            (grad_gate * gate_ref[...]) * (hot.astype(F32) - route_ref[...])
        ).astype(BF16)
        routerg_ref[...] = dot_nt(n2_ref[...], grad_logits)
        gain_grad = jnp.zeros(gain2g_ref.shape, F32)
        for t in range(0, tok, HALF):
            cols = slice(t, t + HALF)
            table = lax.broadcasted_iota(jnp.int32, (total, HALF), 0) == slot_ref[:, cols]
            gn2 = dot_tn(dx_ref[...], table.astype(F32).astype(BF16))
            gn2 = gn2 + dot_nn(wr_ref[...], grad_logits[:, cols])
            branch, part = norm_back(gn2, resid_ref[:, cols], gain2_ref[...])
            gain_grad = gain_grad + part
            gr = g_ref[t:t + HALF, :].astype(F32).T + branch
            gres[:, cols] = gr
            ga[:, cols] = gr.astype(BF16)
        gain2g_ref[...] = gain_grad
        outg_ref[...] = dot_nt(attn_ref[...], ga[...])
        for t in range(0, tok, HALF):
            cols = slice(t, t + HALF)
            ga[:, cols] = dot_nn(wout_ref[...], ga[:, cols]).astype(BF16)
        gn1[...] = jnp.zeros_like(gn1)

    @pl.loop(0, PAIR)
    def _(h):
        inside = pair * PAIR + h
        head = step * GROUP + inside
        at = pl.ds(pl.multiple_of(inside * HEAD_DIM, HEAD_DIM), HEAD_DIM)
        all_at = pl.ds(pl.multiple_of(head * HEAD_DIM, HEAD_DIM), HEAD_DIM)
        for s in range(seqs):
            row = slice(s * LEN, (s + 1) * LEN)
            value = v_ref[at, row]
            for c in range(0, LEN, HALF):
                cols = slice(s * LEN + c, s * LEN + c + HALF)
                grad = ga[all_at, cols]
                inner = jnp.sum(
                    grad.astype(F32) * attn_ref[all_at, cols].astype(F32), axis=0, keepdims=True
                )
                gp = dot_tn(value, grad)
                ds_ref[h, s, :, c:c + HALF] = (
                    p_ref[h, s, :, c:c + HALF].astype(F32) * (gp - inner)
                ).astype(BF16)
            ds = ds_ref[h, s]
            dv[at, row] = dot_nt(ga[all_at, row], p_ref[h, s]).astype(BF16)
            factor = HEAD_DIM ** -0.5
            dq[at, row] = (dot_nn(k_ref[at, row], ds) * factor).astype(BF16)
            dk[at, row] = (dot_nt(q_ref[at, row], ds) * factor).astype(BF16)

    @pl.when(pair == pl.num_programs(1) - 1)
    def _():
        for d, o_ref, w_ref in ((dq, gq_ref, wq_ref), (dk, gk_ref, wk_ref), (dv, gv_ref, wv_ref)):
            o_ref[...] = dot_nt(n1_ref[...], d[...])
            gn1[...] += dot_nn(w_ref[...], d[...])

    @pl.when((step == pl.num_programs(0) - 1) & (pair == pl.num_programs(1) - 1))
    def _():
        gain_grad = jnp.zeros(gain1g_ref.shape, F32)
        for t in range(0, tok, HALF):
            cols = slice(t, t + HALF)
            x = hid_ref[t:t + HALF, :].astype(F32).T
            branch, part = norm_back(gn1[:, cols], x, gain1_ref[...])
            gain_grad = gain_grad + part
            ingrad_ref[t:t + HALF, :] = (gres[:, cols] + branch).T
        gain1g_ref[...] = gain_grad


def back(dx, gg, slot, pos, ids, route, gate, resid, n2, attn, g, hidden, n1, q, k, v, p, gain1, gain2,
         w_router, w_out, w_qkv):
    tok, width = hidden.shape
    experts = w_router.shape[1]
    total = dx.shape[0]
    seqs = p.shape[1]
    wspec = lambda part: pl.BlockSpec((width, GW), lambda i, j: (0, part * GROUPS + i))
    qspec = pl.BlockSpec((GW, tok), lambda i, j: (i, 0))
    pspec = pl.BlockSpec((PAIR, seqs, LEN, LEN), lambda i, j: (i * (GROUP // PAIR) + j, 0, 0, 0))
    gspec = pl.BlockSpec((width, GW), lambda i, j: (0, i))
    sd = jax.ShapeDtypeStruct
    return pl.pallas_call(
        back_kernel,
        grid=(GROUPS, GROUP // PAIR),
        in_specs=[
            whole((total, width)), whole((experts, 8, LANES)), whole((1, tok)), whole((1, tok)),
            whole((1, tok)), whole((experts, tok)), whole((1, tok)), whole((width, tok)),
            whole((width, tok)), whole((width, tok)), whole((tok, width)), whole((tok, width)),
            whole((width, tok)), qspec, qspec, qspec, pspec, whole((width, 1)), whole((width, 1)),
            whole((width, experts)), whole((width, width)), wspec(0), wspec(1), wspec(2),
        ],
        out_specs=(
            whole((tok, width)), whole((width, 1)), gspec, gspec, gspec, whole((width, width)),
            whole((width, 1)), whole((width, experts)), pspec,
        ),
        out_shape=(
            sd((tok, width), F32), sd((width, 1), F32), sd((width, width), F32),
            sd((width, width), F32), sd((width, width), F32), sd((width, width), F32),
            sd((width, 1), F32), sd((width, experts), F32), sd((HEADS, seqs, LEN, LEN), BF16),
        ),
        scratch_shapes=[
            pltpu.VMEM((width, tok), F32), pltpu.VMEM((width, tok), BF16),
            pltpu.VMEM((width, tok), F32), pltpu.VMEM((GW, tok), BF16),
            pltpu.VMEM((GW, tok), BF16), pltpu.VMEM((GW, tok), BF16),
        ],
        compiler_params=pltpu.CompilerParams(vmem_limit_bytes=62 * MIB),
        name="back",
    )(
        dx, gg, slot, pos, ids, route, gate, resid, n2, attn, g, hidden, n1, q, k, v, p,
        gain1.reshape(width, 1), gain2.reshape(width, 1), w_router, w_out, w_qkv, w_qkv, w_qkv,
    )


TROWS = 16


def table_kernel(ds_ref, rel_ref, out_ref, acc):
    step = pl.program_id(0)
    pairs = ds_ref.shape[0] * ds_ref.shape[1]
    block = ds_ref.shape[2]

    @pl.when(step == 0)
    def _():
        acc[...] = jnp.zeros_like(acc)

    @pl.loop(0, block // TROWS)
    def _(r):
        base = pl.multiple_of(r * TROWS, TROWS)
        lhs = ds_ref[:, :, pl.ds(base, TROWS), :].reshape(pairs * TROWS, LEN)
        rel = rel_ref[pl.ds(base, TROWS), :]
        hot = (
            rel[:, None, :] == lax.broadcasted_iota(jnp.int32, (TROWS, BUCKETS, LEN), 1)
        ).astype(F32).astype(BF16).reshape(TROWS * BUCKETS, LEN)
        acc[...] += dot_nt(lhs, hot)

    @pl.when(step == pl.num_programs(0) - 1)
    def _():
        rows = lax.broadcasted_iota(jnp.int32, acc.shape, 0) % TROWS
        cols = lax.broadcasted_iota(jnp.int32, acc.shape, 1) // BUCKETS
        kept = jnp.where(rows == cols, acc[...], 0.0)
        per_head = jnp.sum(kept.reshape(HEADS, pairs * TROWS // HEADS, acc.shape[1]), axis=1)
        fold = (
            lax.broadcasted_iota(jnp.int32, (BUCKETS, acc.shape[1]), 1) % BUCKETS
            == lax.broadcasted_iota(jnp.int32, (BUCKETS, acc.shape[1]), 0)
        ).astype(F32)
        out_ref[...] = lax.dot_general(
            fold, per_head, (((1,), (1,)), ((), ())), precision=lax.Precision.HIGHEST,
            preferred_element_type=F32,
        )


def table_grad(ds, relt):
    seqs = ds.shape[1]
    block = 128
    return pl.pallas_call(
        table_kernel,
        grid=(LEN // block,),
        in_specs=[
            pl.BlockSpec((HEADS, seqs, block, LEN), lambda i: (0, 0, i, 0)),
            pl.BlockSpec((block, LEN), lambda i: (i, 0)),
        ],
        out_specs=whole((BUCKETS, HEADS)),
        out_shape=jax.ShapeDtypeStruct((BUCKETS, HEADS), F32),
        scratch_shapes=[pltpu.VMEM((HEADS * seqs * TROWS, TROWS * BUCKETS), F32)],
        compiler_params=pltpu.CompilerParams(vmem_limit_bytes=40 * MIB),
        name="table_grad",
    )(ds, relt)


def matmul(a, b):
    return jnp.dot(a, b, preferred_element_type=F32)


AXES = ("narrow", "wide")


def exchange(v):
    return lax.all_to_all(v, AXES, split_axis=0, concat_axis=0, tiled=True)


def local(
    hidden_in, norm_gain_one, w_qkv, w_out, pos_table, norm_gain_two, w_router, w_in, w_down,
    expert_ids, segment_ids, rel_buckets, out_grad,
):
    experts = lax.axis_size("narrow") * lax.axis_size("wide")
    tok, width = hidden_in.shape
    cap = max(2, (5 * tok + 4 * experts - 1) // (4 * experts))
    capp = (cap + 7) // 8 * 8
    rows = experts * capp
    ids = expert_ids.reshape(1, tok)
    slot, pos, g_packed = make_slots(experts, cap, capp, ids, out_grad)
    g_rows = exchange(g_packed.reshape(experts, capp, width)).reshape(rows, width)
    table = jnp.pad(pos_table.T, ((0, 0), (0, LANES - BUCKETS)))
    (n1, q, k, v, p, attn, resid, n2, route, gate, packed, gpack) = front(
        hidden_in, norm_gain_one, w_qkv, w_out, table, norm_gain_two, w_router, ids, slot, pos,
        segment_ids, rel_buckets, rows,
    )
    expert_in = exchange(packed.reshape(experts, capp, width)).reshape(rows, width)
    gates = jnp.sum(exchange(gpack).astype(F32), axis=1)[:, :capp].reshape(rows, 1)
    inner = matmul(expert_in, w_in[0])
    active = jax.nn.gelu(inner).astype(BF16)
    expert_out = matmul(active, w_down[0]).astype(BF16)
    gg = jnp.sum(g_rows.astype(F32) * expert_out.astype(F32), axis=1).reshape(experts, capp)
    gg = jnp.pad(gg, ((0, 0), (0, LANES - capp)))
    gg = jnp.pad(jnp.stack(split3(gg), axis=1), ((0, 0), (0, 5), (0, 0)))
    grad_slots = (gates * g_rows.astype(F32)).astype(BF16)
    grad_active = lax.dot_general(grad_slots, w_down[0], (((1,), (1,)), ((), ())), preferred_element_type=F32)
    unused, pull = jax.vjp(jax.nn.gelu, inner)
    grad_inner = pull(grad_active)[0].astype(BF16)
    grad_rows = lax.dot_general(grad_inner, w_in[0], (((1,), (1,)), ((), ())), preferred_element_type=F32).astype(BF16)
    dx = exchange(grad_rows.reshape(experts, capp, width)).reshape(rows, width)
    gg = exchange(gg)
    out_rows = exchange(expert_out.reshape(experts, capp, width)).reshape(rows, width)
    grad_w_down = lax.dot_general(active, grad_slots, (((0,), (0,)), ((), ())), preferred_element_type=F32)
    grad_w_in = lax.dot_general(expert_in, grad_inner, (((0,), (0,)), ((), ())), preferred_element_type=F32)
    (in_grad, gain1g, gq, gk, gv, outg, gain2g, routerg, ds) = back(
        dx, gg, slot, pos, ids, route, gate, resid, n2, attn, out_grad, hidden_in, n1, q, k, v, p,
        norm_gain_one, norm_gain_two, w_router, w_out, w_qkv,
    )
    tableg = table_grad(ds, rel_buckets.T)
    layer_out = combine(out_rows, slot, gate, resid)
    gq, gk, gv, outg, tableg, gain1g, gain2g, routerg = lax.psum(
        (gq, gk, gv, outg, tableg, gain1g, gain2g, routerg), AXES
    )
    return (
        layer_out, in_grad, gain1g.reshape(width), jnp.concatenate((gq, gk, gv), axis=1), outg,
        tableg, gain2g.reshape(width), routerg, grad_w_in[None], grad_w_down[None],
    )


def solution(mesh):
    split = P(AXES, None)
    cube = P(AXES, None, None)
    return jax.shard_map(
        local,
        mesh=mesh,
        in_specs=(
            split, P(), P(), P(), P(), P(), P(), cube, cube, split, split, P(), split,
        ),
        out_specs=(split, split, P(), P(), P(), P(), P(), P(), cube, cube),
        check_vma=False,
    )
```

time: 761 us -> 596 us (0.78)
  matrix products: 245 us -> 78 us
  Pallas kernels: 0 us -> 120 us
  blocking collectives: 38.5 us -> 156 us
  waiting for transfers between devices: 280 us -> 173 us
  local copies, waits for them, and re-layouts: 88.8 us -> 28.5 us
  other arithmetic: 46.6 us -> 7.79 us
  starting transfers between devices: 36.9 us -> 9.44 us
    dot_general x34 -> x6, matrix products: 245 us -> 78 us  [the longest x2 27.8 us: matmul(): return jnp.dot(a, b, preferred_element_type=F32)]
    pallas_call x0 -> x5, Pallas kernels: none -> 120 us  [the longest x1 49.2 us: front(): pl.pallas_call(front_kernel, grid=(GROUPS,), in_specs=[whole((tok, width)...]
    all_to_all x0 -> x3, blocking collectives: none -> 118 us  [exchange(): return lax.all_to_all(v, AXES, split_axis=0, concat_axis=0, tiled=True)]
    all_to_all x8 -> x3, waiting for transfers between devices: 183 us -> 77.2 us  [exchange(): return lax.all_to_all(v, AXES, split_axis=0, concat_axis=0, tiled=True)]
    add x4 -> x0, other arithmetic: 33 us -> none  [the longest x1 27 us: local(): bias_grad = bias_grad + grad_scores.astype(jnp.float32)]
    all_to_all x8 -> x3, starting transfers between devices: 36.8 us -> 9.23 us  [exchange(): return lax.all_to_all(v, AXES, split_axis=0, concat_axis=0, tiled=True)]
    unnamed x156 -> x41, local copies, waits for them, and re-layouts: 41.8 us -> 20.8 us
    all_to_all x8 -> x0, local copies, waits for them, and re-layouts: 18.7 us -> none  [the longest x1 2.96 us: local(): lax.all_to_all(packed, 'narrow', split_axis=0, concat_axis=0, tiled=True)]
  transfers between devices with their start and end apart: 9 -> 4, of which waited for: 8 -> 3; matrix products, arithmetic and copies ran while one was open for 20% -> 11% of each run, Pallas kernels for 0% -> 3%
where the time goes in v1:
time: 596 us; the launch traced here: 588 us
  waiting for transfers between devices  173 us (29%)
  blocking collectives  156 us (26%)
  Pallas kernels  120 us (20%)
  matrix products  78 us (13%)
  local copies, waits for them, and re-layouts  28.5 us (5%)
  between operations  14.7 us (2%)
  starting transfers between devices  9.44 us (2%)
  other arithmetic  7.79 us (1%)
    all_to_all x3, blocking collectives, exchange(): return lax.all_to_all(v, AXES, split_axis=0, concat_axis=0, tiled=True)  118 us
    psum x1, waiting for transfers between devices, local(): lax.psum((gq, gk, gv, outg, tableg, gain1g, gain2g, routerg), AXES)  96.2 us
    all_to_all x3, waiting for transfers between devices, exchange(): return lax.all_to_all(v, AXES, split_axis=0, concat_axis=0, tiled=True)  77.2 us
    pallas_call x1, Pallas kernels, front(): pl.pallas_call(front_kernel, grid=(GROUPS,), in_specs=[whole((tok, width)...  49.2 us
    pallas_call x1, Pallas kernels, back(): pl.pallas_call(back_kernel, grid=(GROUPS, GROUP // PAIR), in_specs=[whole...  46.3 us
    psum x1, blocking collectives, local(): lax.psum((gq, gk, gv, outg, tableg, gain1g, gain2g, routerg), AXES)  37.5 us
    dot_general x2, matrix products, matmul(): return jnp.dot(a, b, preferred_element_type=F32)  27.8 us
    unnamed x41, local copies, waits for them, and re-layouts  20.8 us
  transfers between devices with their start and end apart: 4, of which 3 were waited for; matrix products, arithmetic and copies ran while one was open for 11% of the time, Pallas kernels for 3%

profile of v1, /device:TPU:0, one launch (start us, length us, event | category | flops | bytes accessed | tf_op | source)
XLA Modules:
  0.0 588.0 jit_solution(2701668708453131270)
XLA Ops:
  7.2 1.3 reshape.81.segr_ref
  8.5 1.6 copy.56.wr_ref
  10.1 1.6 reshape.94.gain1_ref
  11.7 1.6 reshape.95.gain2_ref
  13.3 1.7 copy.57.segc_ref
  15.0 1.3 pad.12.tab_ref
  16.3 1.4 copy-done.2
  17.7 0.7 copy-done.4
  18.4 4.5 slots.1
  22.9 0.6 copy-done.5
  23.5 0.6 copy-done.8
  24.1 49.2 %front.1 = (bf16[768,1024]{1,0:T(8,128)(2,1)}, bf16[768,1024]{1,0:T(8,128)(2,1)}, bf16[768,1024]{1,0:T(8,128)(2,1)}, bf16[768,1024]{1,0:T(8,128)(2,1)}, bf16[12,...) custom-call(bf16[1024,768]{1,0:T(8,128)(2,1)} %hid_ref.3, ...), custom_call_target="tpu_custom_call" | custom-call | tf_op jit(solution)/shard_map/front/pallas_call | solution.py:191
  73.4 14.7 %all_to_all.30 = bf16[32,8,128]{2,1,0:T(8,128)(2,1)S(1)} all-to-all(bf16[32,8,128]{2,1,0:T(8,128)(2,1)} %get-tuple-element.39), channel_id=1, replica_groups=mesh['narrow'=4,'wide'=8] {'narrow','wide'}, dimensions={0} | all-to-all | bytes 131072 | tf_op jit(solution)/shard_map/all_to_all | solution.py:450
  88.1 50.7 %all_to_all.31 = bf16[32,40,768]{2,1,0:T(8,128)(2,1)} all-to-all(bf16[32,40,768]{2,1,0:T(8,128)(2,1)} %bitcast.60), channel_id=1, replica_groups=mesh['narrow'=4,'wide'=8] {'narrow','wide'}, dimensions={0} | all-to-all | bytes 3932160 | tf_op jit(solution)/shard_map/all_to_all | solution.py:450
  138.7 3.2 all-to-all-start.3
  142.0 0.1 mul.83
  142.1 12.3 %fusion.12 = f32[1280,3072]{1,0:T(8,128)} fusion(bf16[1280,768]{1,0:T(8,128)(2,1)} %bitcast.57, bf16[1,768,3072]{2,1,0:T(8,128)(2,1)} %param.20), kind=kOutput, calls=%fused_computation.18 | convolution fusion | flops 6039797760 | bytes 22413312 | tf_op jit(solution)/shard_map/dot_general | solution.py:443
  154.3 34.9 %all-to-all-done.3 = bf16[32,40,768]{2,1,0:T(8,128)(2,1)S(1)} async-done(((bf16[32,40,768]{2,1,0:T(8,128)(2,1)}), bf16[32,40,768]{2,1,0:T(8,128)(2,1)S(1)}, u32[]{:S(2)}, u32[]{:S(2)}) %all-to-all-start.3) | async-done | bytes 1966112 | tf_op jit(solution)/shard_map/all_to_all | solution.py:450
  189.3 15.6 %fusion.16 = (bf16[1280,768]{1,0:T(8,128)(2,1)}, f32[1280]{0:T(1024)S(1)}, bf16[1280,768]{1,0:T(8,128)(2,1)}) fusion(bf16[32,40,768]{2,1,0:T(8,128)(2,1)S(1)} %all-to-all-done.3, f32[1280]{0:T(1024)S(1)} %mul.83, bf16[1,3072,768]{2,1,0:T(8,128)(2,1)} %param.21, f32[1280,3072]{1,0:T(8,128)} %fusion.12), kind=kOutput, calls=%fused_computation.25 | convolution fusion | flops 6082067456 | bytes 26355712 | tf_op jit(solution)/shard_map/dot_general | solution.py:443
  204.8 0.1 reshape.90
  205.0 0.7 fusion.27
  205.7 2.6 all-to-all-start.5
  208.3 0.2 all-reduce.7.cloned.1.call-start
  208.5 0.0 slice-start
  208.5 0.4 fusion.14
  208.9 0.0 slice-start.1
  208.9 17.6 %fusion.6 = bf16[1280,3072]{1,0:T(8,128)(2,1)S(1)} fusion(f32[1280,3072]{1,0:T(8,128)} %fusion.12, bf16[1280,768]{1,0:T(8,128)(2,1)S(1)} %bitcast.62, bf16[1,3072,768]{2,1,0:T(8,128)(2,1)} %param.21), kind=kOutput, calls=%fused_computation.8 | convolution fusion | flops 6118440960 | bytes 30277632 | tf_op jit(solution)/shard_map/dot_general | solution.py:479
  226.6 0.0 copy-start.14
  226.6 3.2 copy-done.14
  229.8 0.0 slice-done
  229.8 0.0 slice-done.1
  229.8 6.3 %fusion.17 = bf16[1280,768]{1,0:T(8,128)(2,1)S(1)} fusion(bf16[1280,3072]{1,0:T(8,128)(2,1)S(1)} %fusion.6, bf16[1,768,3072]{2,1,0:T(8,128)(2,1)S(1)} %bitcast.68), kind=kOutput, calls=%fused_computation.26 | convolution fusion | flops 6040780800 | bytes 14548992 | tf_op jit(solution)/shard_map/dot_general | solution.py:482
  236.1 0.0 all-to-all-done.5.gg_ref
  236.1 0.0 copy-start.13
  236.1 53.0 %all_to_all.32 = bf16[32,40,768]{2,1,0:T(8,128)(2,1)} all-to-all(bf16[32,40,768]{2,1,0:T(8,128)(2,1)S(1)} %bitcast.61), channel_id=1, replica_groups=mesh['narrow'=4,'wide'=8] {'narrow','wide'}, dimensions={0} | all-to-all | bytes 3932160 | tf_op jit(solution)/shard_map/all_to_all | solution.py:450
  289.1 0.0 copy-done.13
  289.1 46.3 %back.1 = (f32[1024,768]{1,0:T(8,128)}, f32[768,1]{1,0:T(8,128)}, f32[768,768]{1,0:T(8,128)}, f32[768,768]{1,0:T(8,128)}, f32[768,768]{1,0:T(8,128)}, /*index=5*...) custom-call(bf16[1280,768]{1,0:T(8,128)(2,1)} %bitcast.56, ...), custom_call_target="tpu_custom_call" | custom-call | tf_op jit(solution)/shard_map/back/pallas_call | solution.py:354
  335.4 0.0 copy-start.9
  335.4 0.0 copy-start.11
  335.4 0.0 all-reduce.7.cloned.1.call-update
  335.5 1.2 copy-done.9
  336.6 1.3 copy.64
  338.0 3.5 all-to-all-start.1
  341.5 0.0 copy-done.11
  341.5 0.0 copy-start.15
  341.5 12.2 %convolution_bitcast_fusion.1 = f32[1,768,3072]{2,1,0:T(8,128)} fusion(bf16[1280,768]{1,0:T(8,128)(2,1)S(1)} %bitcast.58, bf16[1280,3072]{1,0:T(8,128)(2,1)} %copy-done.14), kind=kOutput, calls=%fused_computation.12 | convolution fusion | flops 6039797760 | bytes 19267584 | tf_op jit(solution)/shard_map/dot_general | solution.py:487
  353.7 0.0 copy-done.15
  353.7 14.1 %convolution_bitcast_fusion = f32[1,3072,768]{2,1,0:T(8,128)} fusion(bf16[1280,768]{1,0:T(8,128)(2,1)S(1)} %copy-done.15, f32[1280,3072]{1,0:T(8,128)} %fusion.12), kind=kOutput, calls=%fused_computation.11 | convolution fusion | flops 6075187200 | bytes 27131904 | tf_op jit(solution)/shard_map/dot_general | solution.py:486
  367.8 42.3 %all-to-all-done.1 = bf16[32,40,768]{2,1,0:T(8,128)(2,1)} async-done(((bf16[32,40,768]{2,1,0:T(8,128)(2,1)}), bf16[32,40,768]{2,1,0:T(8,128)(2,1)}, u32[]{:S(2)}, u32[]{:S(2)}) %all-to-all-start.1) | async-done | bytes 1966112 | tf_op jit(solution)/shard_map/all_to_all | solution.py:450
  410.1 0.0 copy-done
  410.1 0.0 copy-done.6
  410.1 0.0 copy-done.7
  410.1 5.8 combine.1
  415.9 1.2 reduce
  417.1 0.2 reduce.1
  417.3 4.9 copy-done.1
  422.2 1.3 copy-done.3
  423.5 14.3 %table_grad.1 = f32[32,12]{1,0:T(8,128)S(1)} custom-call(bf16[12,2,512,512]{3,2,1,0:T(8,128)(2,1)S(1)} %copy-done.1, s32[512,512]{1,0:T(8,128)S(1)} %bitcast.52), custom_call_target="tpu_custom_call" | custom-call | tf_op jit(solution)/shard_map/table_grad/pallas_call | solution.py:427
  437.8 37.5 %all-reduce.3 = (f32[768]{0:T(1024)}, f32[32,12]{1,0:T(8,128)S(1)}, f32[768]{0:T(1024)}) all-reduce(f32[768]{0:T(1024)S(1)} %reduce, f32[32,12]{1,0:T(8,128)S(1)} %table_grad.1, f32[768]{0:T(1024)S(1)} %reduce.1), channel_id=1, replica_groups=mesh['narrow'=4,'wide'=8] {'narrow','wide'}, use_global_device_ids=true, to_apply=%region_2.3 | all-reduce | flops 1920 | bytes 15360 | tf_op jit(solution)/shard_map/psum | solution.py:494
  475.3 0.7 copy.65
  476.0 96.2 %all-reduce.7.cloned.1.call-done = (f32[768,768]{1,0:T(8,128)}, f32[768,768]{1,0:T(8,128)}, f32[768,768]{1,0:T(8,128)}, f32[768,768]{1,0:T(8,128)}, f32[768,32]{1,0:T(8,128)}) async-done(((f32[768,768]{1,0:T(8,128)}, f32[768,768]{1,0:T(8,128)}, f32[768,768]{1,0:T(8,128)}, f32[768,768]{1,0:T(8,128)}, f32[768,32]{1,0:T(8,128)}), (f32[768,768]{1,0:T(8,128)}, f32[768,768]{1,0:T(8,128)}, f32[768,768]{1,0:T(8,128)}, ...) | async-done | bytes 9535504 | tf_op jit(solution)/shard_map/psum | solution.py:494
  572.2 1.8 copy.66
  573.9 5.3 pad_maximum_fusion
  579.3 1.4 copy.72
  (20 shorter events, 0.1 us)
Async XLA Ops:
  16.3 1.4 copy-start.2
  17.7 0.7 copy-start.4
  22.9 0.6 copy-start.5
  23.5 0.6 copy-start.8
  138.7 50.5 %all-to-all-start.3 = ((bf16[32,40,768]{2,1,0:T(8,128)(2,1)}), bf16[32,40,768]{2,1,0:T(8,128)(2,1)S(1)}, u32[]{:S(2)}, u32[]{:S(2)}) async-start(bf16[32,40,768]{2,1,0:T(8,128)(2,1)} %bitcast.9), calls=%async_computation.3 | async-start | bytes 3932160 | tf_op jit(solution)/shard_map/all_to_all | solution.py:450
  205.7 30.4 %all-to-all-start.5 = ((bf16[32,8,128]{2,1,0:T(8,128)(2,1)}), bf16[32,8,128]{2,1,0:T(8,128)(2,1)S(1)}, u32[]{:S(2)}, u32[]{:S(2)}) async-start(bf16[32,8,128]{2,1,0:T(8,128)(2,1)} %fusion.27), calls=%async_computation.5 | async-start | bytes 131072 | tf_op jit(solution)/shard_map/all_to_all | solution.py:450
  208.3 363.9 %all-reduce.7.cloned.1.call-start = ((), (), s32[]{:S(2)}) async-start(), calls=%async_computation.6 | async-start | bytes 19660800 | tf_op jit(solution)/shard_map/psum | solution.py:494
  208.5 21.3 %slice-start = ((s8[4718592]{0:T(1024)(128)(4,1)}), s8[4194304]{0:T(1024)(128)(4,1)S(1)}, s32[]{:S(2)}) async-start(s8[4718592]{0:T(1024)(128)(4,1)} %bitcast.67), calls=%async_computation.7 | async-start | bytes 8388608
  208.9 20.9 %slice-start.1 = ((s8[4718592]{0:T(1024)(128)(4,1)}), s8[524288]{0:T(1024)(128)(4,1)S(1)}, s32[]{:S(2)}) async-start(s8[4718592]{0:T(1024)(128)(4,1)} %bitcast.67), calls=%async_computation.8 | async-start | bytes 1048576
  226.6 3.2 copy-start.14
  236.1 53.0 %copy-start.13 = (bf16[32,8,128]{2,1,0:T(8,128)(2,1)}, bf16[32,8,128]{2,1,0:T(8,128)(2,1)S(1)}, u32[]{:S(2)}) copy-start(bf16[32,8,128]{2,1,0:T(8,128)(2,1)S(1)} %all-to-all-done.5.gg_ref) | copy-start | bytes 196612
  335.4 1.2 copy-start.9
  335.4 6.0 %copy-start.11 = (bf16[32,40,768]{2,1,0:T(8,128)(2,1)S(1)}, bf16[32,40,768]{2,1,0:T(8,128)(2,1)}, u32[]{:S(2)}) copy-start(bf16[32,40,768]{2,1,0:T(8,128)(2,1)} %all_to_all.31) | copy-start | bytes 5898244
  338.0 72.1 %all-to-all-start.1 = ((bf16[32,40,768]{2,1,0:T(8,128)(2,1)}), bf16[32,40,768]{2,1,0:T(8,128)(2,1)}, u32[]{:S(2)}, u32[]{:S(2)}) async-start(bf16[32,40,768]{2,1,0:T(8,128)(2,1)} %bitcast.59), calls=%async_computation.1 | async-start | bytes 3932160 | tf_op jit(solution)/shard_map/all_to_all | solution.py:450
  341.5 12.2 %copy-start.15 = (bf16[1280,768]{1,0:T(8,128)(2,1)S(1)}, bf16[1280,768]{1,0:T(8,128)(2,1)}, u32[]{:S(2)}) copy-start(bf16[1280,768]{1,0:T(8,128)(2,1)} %get-tuple-element.106) | copy-start | bytes 5898244
  353.7 56.4 %copy-start = (f32[768,1024]{1,0:T(8,128)S(1)}, f32[768,1024]{1,0:T(8,128)}, u32[]{:S(2)}) copy-start(f32[768,1024]{1,0:T(8,128)} %get-tuple-element.38.resid_ref) | copy-start | bytes 9437188
  353.7 56.4 %copy-start.6 = (s32[1,1024]{1,0:T(1,128)S(1)}, s32[1,1024]{1,0:T(1,128)}, u32[]{:S(2)}) copy-start(s32[1,1024]{1,0:T(1,128)} %copy-done.5) | copy-start | bytes 12292
  353.7 56.4 %copy-start.7 = (f32[1,1024]{1,0:T(1,128)S(1)}, f32[1,1024]{1,0:T(1,128)}, u32[]{:S(2)}) copy-start(f32[1,1024]{1,0:T(1,128)} %get-tuple-element.37.gate_ref) | copy-start | bytes 12292
  367.8 49.3 %copy-start.12 = (f32[768,1]{1,0:T(8,128)S(1)}, f32[768,1]{1,0:T(8,128)}, u32[]{:S(2)}) copy-start(f32[768,1]{1,0:T(8,128)} %get-tuple-element.56) | copy-start | bytes 9220
  417.2 4.9 copy-start.1
  422.2 1.3 copy-start.3
  573.9 5.3 copy-start.10
Sparse Core Ops, SparseCore 0:
  335.6 236.5 all-reduce.6

commit v2 on v1

--- a/solution.py
+++ b/solution.py
@@ -20,6 +20,7 @@
 F32 = jnp.float32
 BF16 = jnp.bfloat16
 MIB = 1024 * 1024
+MICRO = 1150000000
 
 
 def dot_nn(a, b):
@@ -83,6 +84,7 @@
             jax.ShapeDtypeStruct((experts * capp, width), BF16),
         ),
         compiler_params=pltpu.CompilerParams(vmem_limit_bytes=40 * MIB),
+        cost_estimate=pl.CostEstimate(flops=5 * MICRO, bytes_accessed=4 * MIB, transcendentals=0),
         name="slots",
     )(ids_row, g)
 
@@ -211,6 +213,7 @@
             pltpu.VMEM((LEN, LEN), F32),
         ],
         compiler_params=pltpu.CompilerParams(vmem_limit_bytes=58 * MIB),
+        cost_estimate=pl.CostEstimate(flops=50 * MICRO, bytes_accessed=30 * MIB, transcendentals=0),
         name="front",
     )(
         hidden, gain1.reshape(width, 1), w_qkv, w_qkv, w_qkv, w_out, table,
@@ -240,6 +243,7 @@
         out_specs=pl.BlockSpec((HALF, width), lambda i: (i, 0)),
         out_shape=jax.ShapeDtypeStruct((tok, width), BF16),
         compiler_params=pltpu.CompilerParams(vmem_limit_bytes=40 * MIB),
+        cost_estimate=pl.CostEstimate(flops=6 * MICRO, bytes_accessed=8 * MIB, transcendentals=0),
         name="combine",
     )(rows, slot, gate, resid)
 
@@ -278,7 +282,7 @@
         grad_logits = (
             (grad_gate * gate_ref[...]) * (hot.astype(F32) - route_ref[...])
         ).astype(BF16)
-        routerg_ref[...] = dot_nt(n2_ref[...], grad_logits)
+        routerg_ref[...] = dot_nt(grad_logits, n2_ref[...]).astype(BF16)
         gain_grad = jnp.zeros(gain2g_ref.shape, F32)
         for t in range(0, tok, HALF):
             cols = slice(t, t + HALF)
@@ -291,7 +295,7 @@
             gres[:, cols] = gr
             ga[:, cols] = gr.astype(BF16)
         gain2g_ref[...] = gain_grad
-        outg_ref[...] = dot_nt(attn_ref[...], ga[...])
+        outg_ref[...] = dot_nt(attn_ref[...], ga[...]).astype(BF16)
         for t in range(0, tok, HALF):
             cols = slice(t, t + HALF)
             ga[:, cols] = dot_nn(wout_ref[...], ga[:, cols]).astype(BF16)
@@ -325,7 +329,7 @@
     @pl.when(pair == pl.num_programs(1) - 1)
     def _():
         for d, o_ref, w_ref in ((dq, gq_ref, wq_ref), (dk, gk_ref, wk_ref), (dv, gv_ref, wv_ref)):
-            o_ref[...] = dot_nt(n1_ref[...], d[...])
+            o_ref[...] = dot_nt(n1_ref[...], d[...]).astype(BF16)
             gn1[...] += dot_nn(w_ref[...], d[...])
 
     @pl.when((step == pl.num_programs(0) - 1) & (pair == pl.num_programs(1) - 1))
@@ -363,12 +367,12 @@
         ],
         out_specs=(
             whole((tok, width)), whole((width, 1)), gspec, gspec, gspec, whole((width, width)),
-            whole((width, 1)), whole((width, experts)), pspec,
+            whole((width, 1)), whole((experts, width)), pspec,
         ),
         out_shape=(
-            sd((tok, width), F32), sd((width, 1), F32), sd((width, width), F32),
-            sd((width, width), F32), sd((width, width), F32), sd((width, width), F32),
-            sd((width, 1), F32), sd((width, experts), F32), sd((HEADS, seqs, LEN, LEN), BF16),
+            sd((tok, width), F32), sd((width, 1), F32), sd((width, width), BF16),
+            sd((width, width), BF16), sd((width, width), BF16), sd((width, width), BF16),
+            sd((width, 1), F32), sd((experts, width), BF16), sd((HEADS, seqs, LEN, LEN), BF16),
         ),
         scratch_shapes=[
             pltpu.VMEM((width, tok), F32), pltpu.VMEM((width, tok), BF16),
@@ -376,6 +380,7 @@
             pltpu.VMEM((GW, tok), BF16), pltpu.VMEM((GW, tok), BF16),
         ],
         compiler_params=pltpu.CompilerParams(vmem_limit_bytes=62 * MIB),
+        cost_estimate=pl.CostEstimate(flops=46 * MICRO, bytes_accessed=50 * MIB, transcendentals=0),
         name="back",
     )(
         dx, gg, slot, pos, ids, route, gate, resid, n2, attn, g, hidden, n1, q, k, v, p,
@@ -435,8 +440,539 @@
         out_shape=jax.ShapeDtypeStruct((BUCKETS, HEADS), F32),
         scratch_shapes=[pltpu.VMEM((HEADS * seqs * TROWS, TROWS * BUCKETS), F32)],
         compiler_params=pltpu.CompilerParams(vmem_limit_bytes=40 * MIB),
+        cost_estimate=pl.CostEstimate(flops=14 * MICRO, bytes_accessed=13 * MIB, transcendentals=0),
         name="table_grad",
     )(ds, relt)
+
+
+CUBE = 0.044715
+ROOT = 0.7978845608028654
+FTILE = 768
+
+
+def gelu_pair(x):
+    square = x * x
+    t = jnp.tanh(ROOT * (x + CUBE * (x * square)))
+    half = 0.5 + 0.5 * t
+    slope = half + (0.5 * x) * (1.0 - t * t) * (ROOT + (3.0 * CUBE * ROOT) * square)
+    return x * half, slope
+
+
+def device_of(index):
+    wide = lax.axis_size("wide")
+    return (index // wide, lax.rem(index, wide))
+
+
+def expert_kernel(
+    block,
+    packed, gpack, grows, w_in, w_down,
+    dx_out, out_out, active_out, ginner_out, gs_out, x_out, gg_out,
+    xbuf, gatebuf, gbuf, win, wdown, active, slope, ginner, gs, dx, outs, ggsend, ggbuf,
+    x_send, x_recv, gate_send, gate_recv, gg_ssem, gg_rsem, self_sem, load_sem, store_sem,
+):
+    count = lax.axis_size("narrow") * lax.axis_size("wide")
+    me = lax.axis_index("narrow") * lax.axis_size("wide") + lax.axis_index("wide")
+    blocks = count // block
+    mine = me // block
+    capp = packed.shape[1]
+    rows = block * capp
+    hidden = w_in.shape[1]
+    mesh_id = pl.DeviceIdType.MESH
+
+    def x_copy(target, source):
+        return pltpu.make_async_remote_copy(
+            src_ref=packed.at[target], dst_ref=xbuf.at[source], send_sem=x_send.at[target],
+            recv_sem=x_recv.at[source], device_id=device_of(target), device_id_type=mesh_id,
+        )
+
+    def gate_copy(target, source):
+        return pltpu.make_async_remote_copy(
+            src_ref=gpack.at[target], dst_ref=gatebuf.at[source], send_sem=gate_send.at[target],
+            recv_sem=gate_recv.at[source], device_id=device_of(target), device_id_type=mesh_id,
+        )
+
+    def gg_copy(target, source):
+        return pltpu.make_async_remote_copy(
+            src_ref=ggsend.at[target], dst_ref=ggbuf.at[source], send_sem=gg_ssem.at[target],
+            recv_sem=gg_rsem.at[source], device_id=device_of(target), device_id_type=mesh_id,
+        )
+
+    barrier = pltpu.get_barrier_semaphore()
+
+    @pl.loop(1, count)
+    def _(s):
+        pl.semaphore_signal(
+            barrier, inc=1, device_id=device_of(lax.rem(me + s, count)), device_id_type=mesh_id
+        )
+
+    loads = [
+        pltpu.make_async_copy(w_in, win, load_sem.at[0]),
+        pltpu.make_async_copy(w_down, wdown, load_sem.at[1]),
+        pltpu.make_async_copy(grows, gbuf, load_sem.at[2]),
+    ]
+    own = [
+        pltpu.make_async_copy(packed.at[me], xbuf.at[me], self_sem.at[0]),
+        pltpu.make_async_copy(gpack.at[me], gatebuf.at[me], self_sem.at[1]),
+    ]
+    pl.semaphore_wait(barrier, count - 1)
+
+    @pl.loop(0, blocks)
+    def _(c):
+        there = lax.rem(mine + blocks - c, blocks)
+
+        @pl.loop(0, block)
+        def _(j):
+            target = there * block + j
+
+            @pl.when(target != me)
+            def _():
+                gate_copy(target, me).start()
+                x_copy(target, me).start()
+
+    for copy in own + loads:
+        copy.start()
+    for copy in own + loads:
+        copy.wait()
+
+    def stores(at):
+        return [
+            pltpu.make_async_copy(dx.at[at], dx_out.at[at], store_sem.at[0]),
+            pltpu.make_async_copy(outs.at[at], out_out.at[at], store_sem.at[1]),
+            pltpu.make_async_copy(active.at[at], active_out.at[at], store_sem.at[2]),
+            pltpu.make_async_copy(ginner.at[at], ginner_out.at[at], store_sem.at[3]),
+            pltpu.make_async_copy(gs.at[at], gs_out.at[at], store_sem.at[4]),
+        ]
+
+    @pl.loop(0, blocks)
+    def _(c):
+        here = lax.rem(mine + c, blocks)
+        first = here * block
+
+        @pl.loop(0, block)
+        def _(j):
+            source = first + j
+
+            @pl.when(source != me)
+            def _():
+                gate_copy(me, source).wait_recv()
+                x_copy(me, source).wait_recv()
+
+        at = pl.ds(pl.multiple_of(here * rows, rows), rows)
+        group = pl.ds(first, block)
+        x = xbuf[group].reshape(rows, xbuf.shape[2])
+
+        @pl.loop(0, hidden // FTILE)
+        def _(f):
+            tile = pl.ds(pl.multiple_of(f * FTILE, FTILE), FTILE)
+            value, grad = gelu_pair(dot_nn(x, win[:, tile]))
+            active[at, tile] = value.astype(BF16)
+            slope[:, tile] = grad
+
+        result = dot_nn(active[at, :], wdown[...]).astype(BF16)
+        outs[at, :] = result
+        g = gbuf[group].astype(F32)
+        diag = (
+            lax.broadcasted_iota(jnp.int32, (block, capp, LANES), 1)
+            == lax.broadcasted_iota(jnp.int32, (block, capp, LANES), 2)
+        )
+        gate = jnp.sum(gatebuf[group].astype(F32), axis=1)
+        gate = jnp.sum(
+            jnp.where(diag, gate[:, None, :], 0.0), axis=2, keepdims=True
+        )
+        gs[at, :] = (gate * g).astype(BF16).reshape(rows, g.shape[2])
+        gg = jnp.sum(g * result.astype(F32).reshape(g.shape), axis=2, keepdims=True)
+        gg = jnp.sum(jnp.where(diag, gg, 0.0), axis=1)
+        which = lax.broadcasted_iota(jnp.int32, (block, 8, LANES), 1)
+        high, mid, low = [part.astype(F32)[:, None, :] for part in split3(gg)]
+        ggsend[group] = jnp.where(
+            which == 0, high, jnp.where(which == 1, mid, jnp.where(which == 2, low, 0.0))
+        ).astype(BF16)
+
+        @pl.loop(0, block)
+        def _(j):
+            source = first + j
+
+            @pl.when(source != me)
+            def _():
+                gg_copy(source, me).start()
+
+        @pl.loop(0, hidden // FTILE)
+        def _(f):
+            tile = pl.ds(pl.multiple_of(f * FTILE, FTILE), FTILE)
+            grad = dot_nt(gs[at, :], wdown[tile, :])
+            ginner[at, tile] = (grad * slope[:, tile]).astype(BF16)
+
+        dx[at, :] = dot_nt(ginner[at, :], win[...]).astype(BF16)
+
+        @pl.when(c > 0)
+        def _():
+            for copy in stores(at):
+                copy.wait()
+
+        for copy in stores(at):
+            copy.start()
+
+    for copy in stores(pl.ds(0, rows)):
+        copy.wait()
+    keep = [
+        pltpu.make_async_copy(xbuf, x_out, load_sem.at[0]),
+        pltpu.make_async_copy(ggsend.at[me], ggbuf.at[me], self_sem.at[0]),
+    ]
+    for copy in keep:
+        copy.start()
+
+    @pl.loop(0, count)
+    def _(other):
+        @pl.when(other != me)
+        def _():
+            x_copy(other, me).wait_send()
+            gate_copy(other, me).wait_send()
+            gg_copy(other, me).wait_send()
+            gg_copy(me, other).wait_recv()
+
+    for copy in keep:
+        copy.wait()
+    last = pltpu.make_async_copy(ggbuf, gg_out, load_sem.at[1])
+    last.start()
+    last.wait()
+
+
+def expert(packed, gpack, grows, w_in, w_down):
+    count, capp, width = packed.shape
+    hidden = w_in.shape[1]
+    block = 1
+    while block * 2 <= count and block * 2 * capp <= 320:
+        block *= 2
+    rows = block * capp
+    total = count * capp
+    sd = jax.ShapeDtypeStruct
+    anyspec = pl.BlockSpec(memory_space=pl.ANY)
+    dma = pltpu.SemaphoreType.DMA
+    return pl.pallas_call(
+        functools.partial(expert_kernel, block),
+        in_specs=[anyspec] * 5,
+        out_specs=(anyspec,) * 7,
+        out_shape=(
+            sd((total, width), BF16), sd((total, width), BF16), sd((total, hidden), BF16),
+            sd((total, hidden), BF16), sd((total, width), BF16), sd((count, capp, width), BF16),
+            sd((count, 8, LANES), BF16),
+        ),
+        scratch_shapes=[
+            pltpu.VMEM((count, capp, width), BF16), pltpu.VMEM((count, 8, LANES), BF16),
+            pltpu.VMEM((count, capp, width), BF16), pltpu.VMEM((width, hidden), BF16),
+            pltpu.VMEM((hidden, width), BF16), pltpu.VMEM((total, hidden), BF16),
+            pltpu.VMEM((rows, hidden), F32), pltpu.VMEM((total, hidden), BF16),
+            pltpu.VMEM((total, width), BF16), pltpu.VMEM((total, width), BF16),
+            pltpu.VMEM((total, width), BF16), pltpu.VMEM((count, 8, LANES), BF16),
+            pltpu.VMEM((count, 8, LANES), BF16),
+            dma((count,)), dma((count,)), dma((count,)), dma((count,)), dma((count,)), dma((count,)),
+            dma((2,)), dma((3,)), dma((5,)),
+        ],
+        compiler_params=pltpu.CompilerParams(
+            collective_id=0, has_side_effects=True, vmem_limit_bytes=62 * MIB
+        ),
+        cost_estimate=pl.CostEstimate(flops=60 * MICRO, bytes_accessed=60 * 1024 * 1024, transcendentals=0),
+        name="expert",
+    )(packed, gpack, grows, w_in, w_down)
+
+
+def weights_kernel(active_ref, gs_ref, x_ref, ginner_ref, down_ref, in_ref, xt):
+    @pl.when(pl.program_id(0) == 0)
+    def _():
+        total = x_ref.shape[0]
+        for t in range(0, total, HALF):
+            xt[:, t:t + HALF] = x_ref[t:t + HALF, :].T
+
+    down_ref[0] = dot_tn(active_ref[...], gs_ref[...])
+    in_ref[0] = dot_nn(xt[...], ginner_ref[...])
+
+
+def weight_grads(active, gs, x, ginner):
+    total, hidden = active.shape
+    width = gs.shape[1]
+    tile = HALF
+    cols = pl.BlockSpec((total, tile), lambda i: (0, i))
+    return pl.pallas_call(
+        weights_kernel,
+        grid=(hidden // tile,),
+        in_specs=[cols, whole((total, width)), whole((total, width)), cols],
+        out_specs=(
+            pl.BlockSpec((1, tile, width), lambda i: (0, i, 0)),
+            pl.BlockSpec((1, width, tile), lambda i: (0, 0, i)),
+        ),
+        out_shape=(
+            jax.ShapeDtypeStruct((1, hidden, width), F32),
+            jax.ShapeDtypeStruct((1, width, hidden), F32),
+        ),
+        scratch_shapes=[pltpu.VMEM((width, total), BF16)],
+        compiler_params=pltpu.CompilerParams(vmem_limit_bytes=40 * MIB),
+        cost_estimate=pl.CostEstimate(flops=18 * MICRO, bytes_accessed=36 * 1024 * 1024, transcendentals=0),
+        name="weight_grads",
+    )(active, gs, x, ginner)
+
+
+PIECES = 32
+SMALL = 24
+
+
+def reduce_kernel(
+    a, b, c, d, router, small, sums_out, router_out, small_out,
+    own, full, got0, got1, got2, got3, extra, rown, rgot, sown, sgot,
+    send, recv, xsend, xrecv, tsend, trecv, load_sem, store_sem,
+):
+    narrow_n, wide_n = lax.axis_size("narrow"), lax.axis_size("wide")
+    n, w = lax.axis_index("narrow"), lax.axis_index("wide")
+    core, zed = lax.rem(w, 2), lax.rem(w // 2, 4)
+    ex, why = lax.rem(n, 2), lax.rem(n // 2, 2)
+    more_n = (narrow_n // 4) * (wide_n // 8)
+    more_w = wide_n // 8
+    more = (n // 4) * more_w + w // 8
+    units = own.shape[0]
+    half = own.shape[4]
+    mesh_id = pl.DeviceIdType.MESH
+    core_dev = (n, w + 1 - 2 * core)
+    ex_dev = (n + 1 - 2 * ex, w)
+    why_dev = (n + 2 - 4 * why, w)
+
+    def zed_dev(step):
+        return (n, w + 2 * (lax.rem(zed + step, 4) - zed))
+
+    def more_dev(step):
+        other = lax.rem(more + step, more_n)
+        return (n + 4 * (other // more_w - more // more_w),
+                w + 8 * (lax.rem(other, more_w) - lax.rem(more, more_w)))
+
+    def spot(q):
+        first, second = (ex, why) if q == 0 else (why, ex)
+        b16 = core * 16
+        b8 = b16 + first * 8
+        b4 = b8 + second * 4
+        return first, second, b16, b8, b4
+
+    def remote(src, dst, k, u, q, dev):
+        return pltpu.make_async_remote_copy(
+            src_ref=src, dst_ref=dst, send_sem=send.at[k, u, q], recv_sem=recv.at[k, u, q],
+            device_id=dev, device_id_type=mesh_id,
+        )
+
+    def outgoing(phase, u, q):
+        first, second, b16, b8, b4 = spot(q)
+        one, two = (ex_dev, why_dev) if q == 0 else (why_dev, ex_dev)
+        if phase == 0:
+            return [remote(own.at[u, q, pl.ds(16 - b16, 16)], got0.at[u, q], 0, u, q, core_dev)]
+        if phase == 1:
+            src = own.at[u, q, pl.ds(b16 + (1 - first) * 8, 8)]
+            return [remote(src, got1.at[u, q], 1, u, q, one)]
+        if phase == 2:
+            src = own.at[u, q, pl.ds(b8 + (1 - second) * 4, 4)]
+            return [remote(src, got2.at[u, q], 2, u, q, two)]
+        if phase == 3:
+            return [
+                remote(own.at[u, q, b4 + lax.rem(zed + step, 4)], got3.at[u, q, step - 1],
+                       2 + step, u, q, zed_dev(step))
+                for step in (1, 2, 3)
+            ]
+        if phase == 4:
+            mine = full.at[u, q, b4 + zed]
+            return [remote(mine, mine, 5 + step, u, q, zed_dev(step)) for step in (1, 2, 3)]
+        if phase == 5:
+            mine = full.at[u, q, pl.ds(b4, 4)]
+            return [remote(mine, mine, 9, u, q, two)]
+        if phase == 6:
+            mine = full.at[u, q, pl.ds(b8, 8)]
+            return [remote(mine, mine, 10, u, q, one)]
+        mine = full.at[u, q, pl.ds(b16, 16)]
+        return [remote(mine, mine, 11, u, q, core_dev)]
+
+    def incoming(phase, u, q):
+        first, second, b16, b8, b4 = spot(q)
+        if phase < 4:
+            return outgoing(phase, u, q)
+        if phase == 4:
+            return [
+                remote(full.at[u, q, b4 + zed], full.at[u, q, b4 + lax.rem(zed + 4 - step, 4)],
+                       5 + step, u, q, zed_dev(step))
+                for step in (1, 2, 3)
+            ]
+        if phase == 5:
+            there = full.at[u, q, pl.ds(b8 + (1 - second) * 4, 4)]
+            return [remote(there, there, 9, u, q, core_dev)]
+        if phase == 6:
+            there = full.at[u, q, pl.ds(b16 + (1 - first) * 8, 8)]
+            return [remote(there, there, 10, u, q, core_dev)]
+        there = full.at[u, q, pl.ds(16 - b16, 16)]
+        return [remote(there, there, 11, u, q, core_dev)]
+
+    def add(u, q, start, count, got):
+        @pl.loop(0, count)
+        def _(i):
+            own[u, q, start + i] = (
+                own[u, q, start + i].astype(F32) + got[u, q, i].astype(F32)
+            ).astype(BF16)
+
+    def spread(u, q, place):
+        extra[u, q, more] = full[u, q, place]
+        copies = [
+            pltpu.make_async_remote_copy(
+                src_ref=extra.at[u, q, more], dst_ref=extra.at[u, q, more],
+                send_sem=xsend.at[u, q, step], recv_sem=xrecv.at[u, q, step],
+                device_id=more_dev(step), device_id_type=mesh_id,
+            )
+            for step in range(1, more_n)
+        ]
+        for copy in copies:
+            copy.start()
+        for step in range(1, more_n):
+            other = lax.rem(more + more_n - step, more_n)
+            pltpu.make_async_remote_copy(
+                src_ref=extra.at[u, q, more], dst_ref=extra.at[u, q, other],
+                send_sem=xsend.at[u, q, step], recv_sem=xrecv.at[u, q, step],
+                device_id=more_dev(step), device_id_type=mesh_id,
+            ).wait_recv()
+        for copy in copies:
+            copy.wait_send()
+        total = extra[u, q, 0].astype(F32)
+        for i in range(1, more_n):
+            total = total + extra[u, q, i].astype(F32)
+        full[u, q, place] = total.astype(BF16)
+
+    def fold(phase, u, q):
+        first, second, b16, b8, b4 = spot(q)
+        if phase == 0:
+            add(u, q, b16, 16, got0)
+        elif phase == 1:
+            add(u, q, b8, 8, got1)
+        elif phase == 2:
+            add(u, q, b4, 4, got2)
+        elif phase == 3:
+            place = b4 + zed
+            full[u, q, place] = (
+                own[u, q, place].astype(F32) + got3[u, q, 0].astype(F32)
+                + (got3[u, q, 1].astype(F32) + got3[u, q, 2].astype(F32))
+            ).astype(BF16)
+            if more_n > 1:
+                spread(u, q, place)
+
+    bits = []
+    for axis, count in (("wide", wide_n), ("narrow", narrow_n)):
+        size = 1
+        while size < count:
+            at = lax.rem((w if axis == "wide" else n) // size, 2)
+            move = size - 2 * size * at
+            bits.append((n, w + move) if axis == "wide" else (n + move, w))
+            size *= 2
+
+    def tail_copies(level):
+        return [
+            pltpu.make_async_remote_copy(
+                src_ref=src.at[level], dst_ref=dst.at[level], send_sem=tsend.at[level, k],
+                recv_sem=trecv.at[level, k], device_id=bits[level], device_id_type=mesh_id,
+            )
+            for k, (src, dst) in enumerate(((rown, rgot), (sown, sgot)))
+        ]
+
+    inputs = [
+        pltpu.make_async_copy(ref.at[:, :, pl.ds(q * half, half)], own.at[u, q], load_sem.at[u, q])
+        for u, ref in enumerate((a, b, c, d)) for q in range(2)
+    ]
+    for copy in inputs:
+        copy.start()
+    rown[0] = router[...]
+    sown[0] = small[...]
+    barrier = pltpu.get_barrier_semaphore()
+    greet = [core_dev, ex_dev, why_dev] + [zed_dev(step) for step in (1, 2, 3)]
+    greet += [more_dev(step) for step in range(1, more_n)] + bits
+    for dev in greet:
+        pl.semaphore_signal(barrier, inc=1, device_id=dev, device_id_type=mesh_id)
+    pl.semaphore_wait(barrier, len(greet))
+
+    for copy in tail_copies(0):
+        copy.start()
+    for copy in inputs:
+        copy.wait()
+
+    @pl.loop(0, units)
+    def _(u):
+        for q in range(2):
+            for copy in outgoing(0, u, q):
+                copy.start()
+
+    for phase in range(8):
+        @pl.loop(0, units)
+        def _(u):
+            for q in range(2):
+                for copy in incoming(phase, u, q):
+                    copy.wait_recv()
+                for copy in outgoing(phase, u, q):
+                    copy.wait_send()
+                fold(phase, u, q)
+                if phase < 7:
+                    for copy in outgoing(phase + 1, u, q):
+                        copy.start()
+
+        if phase < len(bits):
+            tail(phase, bits, tail_copies, rown, rgot, sown, sgot)
+    for level in range(8, len(bits)):
+        tail(level, bits, tail_copies, rown, rgot, sown, sgot)
+    outputs = [
+        pltpu.make_async_copy(full.at[u, q], sums_out.at[u, :, :, pl.ds(q * half, half)], store_sem.at[u, q])
+        for u in range(units) for q in range(2)
+    ]
+    for copy in outputs:
+        copy.start()
+    router_out[...] = rown[len(bits)]
+    small_out[...] = sown[len(bits)]
+    for copy in outputs:
+        copy.wait()
+
+
+def tail(level, bits, tail_copies, rown, rgot, sown, sgot):
+    for copy in tail_copies(level):
+        copy.wait_recv()
+        copy.wait_send()
+    rown[level + 1] = (rown[level].astype(F32) + rgot[level].astype(F32)).astype(BF16)
+    sown[level + 1] = sown[level] + sgot[level]
+    if level + 1 < len(bits):
+        for copy in tail_copies(level + 1):
+            copy.start()
+
+
+def reduce_all(a, b, c, d, router, small):
+    narrow_n, wide_n = lax.axis_size("narrow"), lax.axis_size("wide")
+    levels = (narrow_n * wide_n).bit_length() - 1
+    more_n = (narrow_n // 4) * (wide_n // 8)
+    width, experts = a.shape[0], router.shape[0]
+    rows, half = width // PIECES, width // 2
+    units = 4
+    a, b, c, d = [v.reshape(PIECES, rows, width) for v in (a, b, c, d)]
+    sd = jax.ShapeDtypeStruct
+    anyspec = pl.BlockSpec(memory_space=pl.ANY)
+    vmem = pl.BlockSpec(memory_space=pltpu.VMEM)
+    dma = pltpu.SemaphoreType.DMA
+    buf = lambda *lead: pltpu.VMEM((units, 2) + lead + (rows, half), BF16)
+    return pl.pallas_call(
+        reduce_kernel,
+        in_specs=[anyspec] * 4 + [vmem, vmem],
+        out_specs=(anyspec, vmem, vmem),
+        out_shape=(
+            sd((units, PIECES, rows, width), BF16), sd((experts, width), BF16),
+            sd((SMALL, LANES), F32),
+        ),
+        scratch_shapes=[
+            buf(PIECES), buf(PIECES), buf(16), buf(8), buf(4), buf(3), buf(more_n),
+            pltpu.VMEM((levels + 1, experts, width), BF16),
+            pltpu.VMEM((levels, experts, width), BF16),
+            pltpu.VMEM((levels + 1, SMALL, LANES), F32), pltpu.VMEM((levels, SMALL, LANES), F32),
+            dma((12, units, 2)), dma((12, units, 2)), dma((units, 2, more_n)),
+            dma((units, 2, more_n)), dma((levels, 2)), dma((levels, 2)), dma((units, 2)),
+            dma((units, 2)),
+        ],
+        compiler_params=pltpu.CompilerParams(
+            collective_id=1, has_side_effects=True, vmem_limit_bytes=50 * MIB
+        ),
+        cost_estimate=pl.CostEstimate(flops=50 * MICRO, bytes_accessed=20 * MIB, transcendentals=0),
+        name="reduce_all",
+    )(a, b, c, d, router, small)
 
 
 def matmul(a, b):
@@ -461,42 +997,39 @@
     rows = experts * capp
     ids = expert_ids.reshape(1, tok)
     slot, pos, g_packed = make_slots(experts, cap, capp, ids, out_grad)
-    g_rows = exchange(g_packed.reshape(experts, capp, width)).reshape(rows, width)
+    g_rows = exchange(g_packed.reshape(experts, capp, width))
     table = jnp.pad(pos_table.T, ((0, 0), (0, LANES - BUCKETS)))
     (n1, q, k, v, p, attn, resid, n2, route, gate, packed, gpack) = front(
         hidden_in, norm_gain_one, w_qkv, w_out, table, norm_gain_two, w_router, ids, slot, pos,
         segment_ids, rel_buckets, rows,
     )
-    expert_in = exchange(packed.reshape(experts, capp, width)).reshape(rows, width)
-    gates = jnp.sum(exchange(gpack).astype(F32), axis=1)[:, :capp].reshape(rows, 1)
-    inner = matmul(expert_in, w_in[0])
-    active = jax.nn.gelu(inner).astype(BF16)
-    expert_out = matmul(active, w_down[0]).astype(BF16)
-    gg = jnp.sum(g_rows.astype(F32) * expert_out.astype(F32), axis=1).reshape(experts, capp)
-    gg = jnp.pad(gg, ((0, 0), (0, LANES - capp)))
-    gg = jnp.pad(jnp.stack(split3(gg), axis=1), ((0, 0), (0, 5), (0, 0)))
-    grad_slots = (gates * g_rows.astype(F32)).astype(BF16)
-    grad_active = lax.dot_general(grad_slots, w_down[0], (((1,), (1,)), ((), ())), preferred_element_type=F32)
-    unused, pull = jax.vjp(jax.nn.gelu, inner)
-    grad_inner = pull(grad_active)[0].astype(BF16)
-    grad_rows = lax.dot_general(grad_inner, w_in[0], (((1,), (1,)), ((), ())), preferred_element_type=F32).astype(BF16)
-    dx = exchange(grad_rows.reshape(experts, capp, width)).reshape(rows, width)
-    gg = exchange(gg)
-    out_rows = exchange(expert_out.reshape(experts, capp, width)).reshape(rows, width)
-    grad_w_down = lax.dot_general(active, grad_slots, (((0,), (0,)), ((), ())), preferred_element_type=F32)
-    grad_w_in = lax.dot_general(expert_in, grad_inner, (((0,), (0,)), ((), ())), preferred_element_type=F32)
+    dx, out_rows, active, ginner, gs, expert_in, gg = expert(
+        packed.reshape(experts, capp, width), gpack, g_rows, w_in[0], w_down[0]
+    )
+    dx = exchange(dx.reshape(experts, capp, width)).reshape(rows, width)
+    grad_w_down, grad_w_in = weight_grads(active, gs, expert_in.reshape(rows, width), ginner)
+    dx, out_rows, grad_w_down, grad_w_in = lax.optimization_barrier(
+        (dx, out_rows, grad_w_down, grad_w_in)
+    )
+    out_rows = exchange(out_rows.reshape(experts, capp, width)).reshape(rows, width)
     (in_grad, gain1g, gq, gk, gv, outg, gain2g, routerg, ds) = back(
         dx, gg, slot, pos, ids, route, gate, resid, n2, attn, out_grad, hidden_in, n1, q, k, v, p,
         norm_gain_one, norm_gain_two, w_router, w_out, w_qkv,
     )
     tableg = table_grad(ds, rel_buckets.T)
+    lines = width // LANES
+    small = jnp.concatenate((
+        gain1g.reshape(lines, LANES), gain2g.reshape(lines, LANES),
+        jnp.pad(tableg.T, ((0, 0), (0, LANES - BUCKETS))),
+    ), axis=0)
     layer_out = combine(out_rows, slot, gate, resid)
-    gq, gk, gv, outg, tableg, gain1g, gain2g, routerg = lax.psum(
-        (gq, gk, gv, outg, tableg, gain1g, gain2g, routerg), AXES
-    )
+    sums, routerg, small = reduce_all(gq, gk, gv, outg, routerg, small)
+    sums = sums.reshape(4, width, width).astype(F32)
     return (
-        layer_out, in_grad, gain1g.reshape(width), jnp.concatenate((gq, gk, gv), axis=1), outg,
-        tableg, gain2g.reshape(width), routerg, grad_w_in[None], grad_w_down[None],
+        layer_out, in_grad, small[:lines].reshape(width),
+        jnp.concatenate((sums[0], sums[1], sums[2]), axis=1), sums[3],
+        small[2 * lines:, :BUCKETS].T, small[lines:2 * lines].reshape(width),
+        routerg.T.astype(F32), grad_w_in, grad_w_down,
     )
 
 

time: 596 us -> 359 us (0.60); the launches traced: 588 us -> 358 us
  Pallas kernels: 120 us -> 279 us
  blocking collectives: 156 us -> 0 us
  waiting for transfers between devices: 173 us -> 22.9 us
  matrix products: 78 us -> 0 us
  between operations: 14.7 us -> 0.84 us
  starting transfers between devices: 9.44 us -> 17.6 us
    pallas_call x0 -> x3, Pallas kernels: none -> 162 us  [the longest x1 72.7 us: reduce_all(): pl.pallas_call(reduce_kernel, in_specs=[anyspec] * 4 + [vmem, vmem], out_...]
    all_to_all x3 -> x0, blocking collectives: 118 us -> none  [exchange(): return lax.all_to_all(v, AXES, split_axis=0, concat_axis=0, tiled=True)]
    psum x1 -> x0, waiting for transfers between devices: 96.2 us -> none  [local(): lax.psum((gq, gk, gv, outg, tableg, gain1g, gain2g, routerg), AXES)]
    dot_general x6 -> x0, matrix products: 78 us -> none  [the longest x2 27.8 us: matmul(): return jnp.dot(a, b, preferred_element_type=F32)]
    all_to_all x3, waiting for transfers between devices: 77.2 us -> 22.9 us  [exchange(): return lax.all_to_all(v, AXES, split_axis=0, concat_axis=0, tiled=True)]
    psum x1 -> x0, blocking collectives: 37.5 us -> none  [local(): lax.psum((gq, gk, gv, outg, tableg, gain1g, gain2g, routerg), AXES)]
    all_to_all x3, starting transfers between devices: 9.23 us -> 17.6 us  [exchange(): return lax.all_to_all(v, AXES, split_axis=0, concat_axis=0, tiled=True)]
    unnamed x41 -> x48, local copies, waits for them, and re-layouts: 20.8 us -> 21.7 us
  transfers between devices with their start and end apart: 4 -> 3, of which waited for: 3 -> 1; matrix products, arithmetic and copies ran while one was open for 11% -> 5% of each run, Pallas kernels for 3% -> 56%
where the time goes in v2:
time: 359 us; the launch traced here: 358 us
  Pallas kernels  279 us (78%)
  local copies, waits for them, and re-layouts  31.5 us (9%)
  waiting for transfers between devices  22.9 us (6%)
  starting transfers between devices  17.6 us (5%)
  other arithmetic  6.19 us (2%)
    pallas_call x1, Pallas kernels, reduce_all(): pl.pallas_call(reduce_kernel, in_specs=[anyspec] * 4 + [vmem, vmem], out_...  72.7 us
    pallas_call x1, Pallas kernels, expert(): pl.pallas_call(functools.partial(expert_kernel, block), in_specs=[anyspec...  70.9 us
    pallas_call x1, Pallas kernels, front(): pl.pallas_call(front_kernel, grid=(GROUPS,), in_specs=[whole((tok, width)...  49.2 us
    pallas_call x1, Pallas kernels, back(): pl.pallas_call(back_kernel, grid=(GROUPS, GROUP // PAIR), in_specs=[whole...  44.4 us
    all_to_all x3, waiting for transfers between devices, exchange(): return lax.all_to_all(v, AXES, split_axis=0, concat_axis=0, tiled=True)  22.9 us
    unnamed x48, local copies, waits for them, and re-layouts  21.7 us
    pallas_call x1, Pallas kernels, weight_grads(): pl.pallas_call(weights_kernel, grid=(hidden // tile,), in_specs=[cols, wh...  18.3 us
    all_to_all x3, starting transfers between devices, exchange(): return lax.all_to_all(v, AXES, split_axis=0, concat_axis=0, tiled=True)  17.6 us
  transfers between devices with their start and end apart: 3, of which 1 were waited for; matrix products, arithmetic and copies ran while one was open for 5% of the time, Pallas kernels for 56%

profile of v2, /device:TPU:0, one launch (start us, length us, event | category | flops | bytes accessed | tf_op | source)
XLA Modules:
  0.0 357.8 jit_solution(10698515218428855993)
XLA Ops:
  0.6 0.0 copy-start.1
  0.7 1.4 copy-done.1
  2.1 0.0 copy-start.2
  2.1 0.7 copy-done.2
  2.7 4.5 %slots.1 = (s32[1,1024]{1,0:T(1,128)S(1)}, s32[1,1024]{1,0:T(1,128)S(1)}, bf16[1280,768]{1,0:T(8,128)(2,1)}) custom-call(s32[1,1024]{1,0:T(1,128)S(1)} %bitcast.36, bf16[1024,768]{1,0:T(8,128)(2,1)S(1)} %copy-done.1), custom_call_target="tpu_custom_call" | custom-call | flops 5750000128 | bytes 4194304 | tf_op jit(solution)/shard_map/slots/pallas_call | solution.py:79
  7.3 0.0 copy-start.11
  7.3 0.6 copy-done.11
  7.9 0.0 copy-start.14
  7.9 0.6 copy-done.14
  8.5 0.0 copy-start.21
  8.5 0.0 copy-start.20
  8.5 7.3 %all-to-all-start = ((bf16[32,40,768]{2,1,0:T(8,128)(2,1)}), bf16[32,40,768]{2,1,0:T(8,128)(2,1)S(1)}, u32[]{:S(2)}, u32[]{:S(2)}) async-start(bf16[32,40,768]{2,1,0:T(8,128)(2,1)} %bitcast.4), calls=%async_computation | async-start | bytes 3932160 | tf_op jit(solution)/shard_map/all_to_all | solution.py:986
  15.8 0.0 copy-done.21
  15.8 0.9 reshape.112.gain1_ref
  16.7 0.0 copy-done.22
  16.7 0.9 reshape.113.gain2_ref
  17.7 0.0 copy-done.18
  17.7 0.8 copy.29.wr_ref
  18.5 0.0 copy-done.19
  18.5 0.6 reshape.95.segr_ref
  19.1 1.0 copy.30.segc_ref
  20.1 0.0 copy-done.20
  20.1 0.6 pad.7.tab_ref
  20.7 49.2 %front.1 = (bf16[768,1024]{1,0:T(8,128)(2,1)}, bf16[768,1024]{1,0:T(8,128)(2,1)}, bf16[768,1024]{1,0:T(8,128)(2,1)}, bf16[768,1024]{1,0:T(8,128)(2,1)}, bf16[12,...) custom-call(bf16[1024,768]{1,0:T(8,128)(2,1)} %hid_ref.3, ...), custom_call_target="tpu_custom_call" | custom-call | flops 57500000256 | bytes 31457280 | tf_op jit(solution)/shard_map/front/pallas_call | solution.py:193
  69.9 0.0 all-to-all-done.grows
  70.0 0.0 copy-start.16
  70.0 1.3 copy-done.16
  71.2 70.9 %expert.1 = (bf16[1280,768]{1,0:T(8,128)(2,1)}, bf16[1280,768]{1,0:T(8,128)(2,1)}, bf16[1280,3072]{1,0:T(8,128)(2,1)}, bf16[1280,3072]{1,0:T(8,128)(2,1)}, bf16[...) custom-call(bf16[32,40,768]{2,1,0:T(8,128)(2,1)} %bitcast.54, ...), custom_call_target="tpu_custom_call" | custom-call | flops 69000003584 | bytes 62914560 | tf_op jit(solution)/shard_map/expert/pallas_call | solution.py:651
  142.1 0.0 copy-start.17
  142.1 0.0 copy-start.3
  142.1 7.6 %all-to-all-start.1 = ((bf16[32,40,768]{2,1,0:T(8,128)(2,1)}), bf16[32,40,768]{2,1,0:T(8,128)(2,1)}, u32[]{:S(2)}, u32[]{:S(2)}) async-start(bf16[32,40,768]{2,1,0:T(8,128)(2,1)} %bitcast.46), calls=%async_computation.1 | async-start | bytes 3932160 | tf_op jit(solution)/shard_map/all_to_all | solution.py:986
  149.7 0.0 copy-done.17
  149.7 1.3 copy.34
  151.0 0.0 copy-done.3
  151.0 3.2 copy-done.9
  154.3 1.5 copy-done.10
  155.8 18.3 %weight_grads.1 = (f32[1,3072,768]{2,1,0:T(8,128)}, f32[1,768,3072]{2,1,0:T(8,128)}) custom-call(bf16[1280,3072]{1,0:T(8,128)(2,1)S(1)} %copy-done.9, bf16[1280,768]{1,0:T(8,128)(2,1)S(1)} %copy-done.10, bf16[1280,768]{1,0:T(8,128)(2,1)S(1)} %bitcast.37, bf16[1280,3072]{1,0:T(8,128)(2,1)} %get-tuple-element.60.ginner_ref), custom_call_target="tpu_custom_call" | custom-call | flops 20700000256 | bytes 37748736 | tf_op jit(solution)/shard_map/weight_grads/pallas_call | solution.py:695
  174.1 22.9 %all-to-all-done.1 = bf16[32,40,768]{2,1,0:T(8,128)(2,1)} async-done(((bf16[32,40,768]{2,1,0:T(8,128)(2,1)}), bf16[32,40,768]{2,1,0:T(8,128)(2,1)}, u32[]{:S(2)}, u32[]{:S(2)}) %all-to-all-start.1) | async-done | bytes 1966112 | tf_op jit(solution)/shard_map/all_to_all | solution.py:986
  197.1 2.7 all-to-all-start.2
  199.8 44.4 %back.1 = (f32[1024,768]{1,0:T(8,128)}, f32[768,1]{1,0:T(8,128)}, bf16[768,768]{1,0:T(8,128)(2,1)}, bf16[768,768]{1,0:T(8,128)(2,1)}, bf16[768,768]{1,0:T(8,128)...) custom-call(bf16[1280,768]{1,0:T(8,128)(2,1)} %bitcast.8.dx_ref, ...), custom_call_target="tpu_custom_call" | custom-call | flops 52899999744 | bytes 52428800 | tf_op jit(solution)/shard_map/back/pallas_call | solution.py:358
  244.2 0.0 copy-start
  244.2 1.2 copy-done
  245.5 4.6 %copy-done.8 = bf16[12,2,512,512]{3,2,1,0:T(8,128)(2,1)S(1)} copy-done((bf16[12,2,512,512]{3,2,1,0:T(8,128)(2,1)S(1)}, bf16[12,2,512,512]{3,2,1,0:T(8,128)(2,1)}, u32[]{:S(2)}) %copy-start.8) | copy-done | bytes 12582936
  250.0 14.3 %table_grad.1 = f32[32,12]{1,0:T(8,128)S(1)} custom-call(bf16[12,2,512,512]{3,2,1,0:T(8,128)(2,1)S(1)} %copy-done.8, s32[512,512]{1,0:T(8,128)S(1)} %bitcast.33), custom_call_target="tpu_custom_call" | custom-call | flops 16099999744 | bytes 13631488 | tf_op jit(solution)/shard_map/table_grad/pallas_call | solution.py:432
  264.4 0.1 copy.35
  264.5 1.2 reduce.1
  265.7 1.2 reduce
  266.8 0.0 copy-done.4
  266.9 0.0 copy-done.15
  266.9 0.0 copy-start.5
  266.9 1.3 copy-done.5
  268.1 1.3 copy-done.6
  269.4 72.7 %reduce_all.1 = (bf16[4,32,24,768]{3,2,1,0:T(8,128)(2,1)}, bf16[32,768]{1,0:T(8,128)(2,1)S(1)}, f32[24,128]{1,0:T(8,128)S(1)}) custom-call(bf16[32,24,768]{2,1,0:T(8,128)(2,1)S(1)} %bitcast.38, bf16[32,24,768]{2,1,0:T(8,128)(2,1)S(1)} %bitcast.39, bf16[32,24,768]{2,1,0:T(8,128)(2,1)S(1)} %bitcast.40, bf16[32,24,768]{2,1,0:T(8,128)(2,1)} %bitcast.55, ...), custom_call_target="tpu_custom_call" | custom-call | flops 57500000256 | bytes 20971520 | tf_op jit(solution)/shard_map/reduce_all/pallas_call | solution.py:953
  342.1 0.6 slice_bitcast_fusion.1
  342.7 0.6 slice_bitcast_fusion
  343.3 0.6 convert_bitcast_fusion
  344.0 4.4 %fusion = (f32[1,32,24,768]{3,2,1,0:T(8,128)}, f32[1,32,24,768]{3,2,1,0:T(8,128)S(1)}, f32[1,32,24,768]{3,2,1,0:T(8,128)S(1)}, f32[1,32,24,768]{3,2,1,0:T(8,128)S(1)}) fusion(bf16[4,32,24,768]{3,2,1,0:T(8,128)(2,1)} %get-tuple-element.86), kind=kLoop, calls=%fused_computation.7 | loop fusion | bytes 18874368 | tf_op jit(solution)/shard_map/slice | solution.py:1030
  348.4 3.2 pad_maximum_fusion
  351.6 0.0 all-to-all-done.2
  351.6 0.0 copy-done.12
  351.6 0.0 copy-done.13
  351.6 0.0 copy-start.7
  351.6 1.9 copy-done.7
  353.5 4.3 %combine.1 = bf16[1024,768]{1,0:T(8,128)(2,1)} custom-call(bf16[1280,768]{1,0:T(8,128)(2,1)S(1)} %bitcast.32, s32[1,1024]{1,0:T(1,128)S(1)} %copy-done.12, f32[1,1024]{1,0:T(1,128)S(1)} %copy-done.13, f32[768,1024]{1,0:T(8,128)S(1)} %copy-done.7), custom_call_target="tpu_custom_call" | custom-call | flops 6899999744 | bytes 8388608 | tf_op jit(solution)/shard_map/combine/pallas_call | solution.py:237
  (12 shorter events, 0.0 us)
Async XLA Ops:
  0.6 1.4 copy-start.1
  2.1 0.7 copy-start.2
  7.3 0.6 copy-start.11
  7.9 0.6 copy-start.14
  8.5 7.3 %copy-start.21 = (f32[768]{0:T(1024)S(1)}, f32[768]{0:T(1024)}, u32[]{:S(2)}) copy-start(f32[768]{0:T(1024)} %param.14) | copy-start | bytes 9220
  8.5 8.3 %copy-start.22 = (f32[768]{0:T(1024)S(1)}, f32[768]{0:T(1024)}, u32[]{:S(2)}) copy-start(f32[768]{0:T(1024)} %param.18) | copy-start | bytes 9220
  8.5 9.2 %copy-start.18 = (bf16[768,32]{0,1:T(8,128)(2,1)S(1)}, bf16[768,32]{0,1:T(8,128)(2,1)}, u32[]{:S(2)}) copy-start(bf16[768,32]{0,1:T(8,128)(2,1)} %param.19) | copy-start | bytes 147460
  8.5 10.0 %copy-start.19 = (s32[2,512]{1,0:T(2,128)S(1)}, s32[2,512]{1,0:T(2,128)}, u32[]{:S(2)}) copy-start(s32[2,512]{1,0:T(2,128)} %param.23) | copy-start | bytes 12292
  8.5 11.6 %copy-start.20 = (f32[32,12]{0,1:T(8,128)S(1)}, f32[32,12]{0,1:T(8,128)}, u32[]{:S(2)}) copy-start(f32[32,12]{0,1:T(8,128)} %param.17) | copy-start | bytes 4612
  8.5 61.5 %all-to-all-start = ((bf16[32,40,768]{2,1,0:T(8,128)(2,1)}), bf16[32,40,768]{2,1,0:T(8,128)(2,1)S(1)}, u32[]{:S(2)}, u32[]{:S(2)}) async-start(bf16[32,40,768]{2,1,0:T(8,128)(2,1)} %bitcast.4), calls=%async_computation | async-start | bytes 3932160 | tf_op jit(solution)/shard_map/all_to_all | solution.py:986
  70.0 1.3 copy-start.16
  142.1 7.6 %copy-start.17 = (s32[512,512]{1,0:T(8,128)S(1)}, s32[512,512]{1,0:T(8,128)}, u32[]{:S(2)}) copy-start(s32[512,512]{1,0:T(8,128)} %rel_ref.1) | copy-start | bytes 3145732
  142.1 8.9 %copy-start.3 = (bf16[32,40,768]{2,1,0:T(8,128)(2,1)S(1)}, bf16[32,40,768]{2,1,0:T(8,128)(2,1)}, u32[]{:S(2)}) copy-start(bf16[32,40,768]{2,1,0:T(8,128)(2,1)} %get-tuple-element.59) | copy-start | bytes 5898244
  142.1 54.9 %all-to-all-start.1 = ((bf16[32,40,768]{2,1,0:T(8,128)(2,1)}), bf16[32,40,768]{2,1,0:T(8,128)(2,1)}, u32[]{:S(2)}, u32[]{:S(2)}) async-start(bf16[32,40,768]{2,1,0:T(8,128)(2,1)} %bitcast.46), calls=%async_computation.1 | async-start | bytes 3932160 | tf_op jit(solution)/shard_map/all_to_all | solution.py:986
  151.0 3.2 copy-start.9
  154.3 1.5 copy-start.10
  197.1 154.5 %all-to-all-start.2 = ((bf16[32,40,768]{2,1,0:T(8,128)(2,1)}), bf16[32,40,768]{2,1,0:T(8,128)(2,1)S(1)}, u32[]{:S(2)}, u32[]{:S(2)}) async-start(bf16[32,40,768]{2,1,0:T(8,128)(2,1)} %bitcast.45), calls=%async_computation.2 | async-start | bytes 3932160 | tf_op jit(solution)/shard_map/all_to_all | solution.py:986
  244.2 1.2 copy-start
  245.5 4.6 %copy-start.8 = (bf16[12,2,512,512]{3,2,1,0:T(8,128)(2,1)S(1)}, bf16[12,2,512,512]{3,2,1,0:T(8,128)(2,1)}, u32[]{:S(2)}) copy-start(bf16[12,2,512,512]{3,2,1,0:T(8,128)(2,1)} %get-tuple-element.84.ds_ref) | copy-start | bytes 37748740
  250.0 16.8 %copy-start.4 = (bf16[768,768]{1,0:T(8,128)(2,1)S(1)}, bf16[768,768]{1,0:T(8,128)(2,1)}, u32[]{:S(2)}) copy-start(bf16[768,768]{1,0:T(8,128)(2,1)} %get-tuple-element.77) | copy-start | bytes 3538948
  250.0 16.8 %copy-start.15 = (bf16[32,768]{1,0:T(8,128)(2,1)S(1)}, bf16[32,768]{1,0:T(8,128)(2,1)}, u32[]{:S(2)}) copy-start(bf16[32,768]{1,0:T(8,128)(2,1)} %get-tuple-element.81.router) | copy-start | bytes 147460
  266.9 1.3 copy-start.5
  268.1 1.3 copy-start.6
  348.4 3.2 copy-start.12
  348.4 3.2 copy-start.13
  351.6 1.9 copy-start.7

commit v3 on v2

v3 whole, which is shorter than its diff:
```python
import functools
import jax
import jax.numpy as jnp
from jax import lax
from jax.experimental import pallas as pl
from jax.experimental.pallas import tpu as pltpu
from jax.sharding import PartitionSpec as P

HEADS = 12
HEAD_DIM = 64
LEN = 512
BUCKETS = 32
EPS = 1e-06
LANES = 128
HALF = 256
GROUP = 4
PAIR = 2
GROUPS = HEADS // GROUP
GW = GROUP * HEAD_DIM
F32 = jnp.float32
BF16 = jnp.bfloat16
MIB = 1024 * 1024
MICRO = 1150000000


def dot_nn(a, b):
    return lax.dot_general(a, b, (((1,), (0,)), ((), ())), preferred_element_type=F32)


def dot_tn(a, b):
    return lax.dot_general(a, b, (((0,), (0,)), ((), ())), preferred_element_type=F32)


def dot_nt(a, b):
    return lax.dot_general(a, b, (((1,), (1,)), ((), ())), preferred_element_type=F32)


def whole(shape):
    rank = len(shape)
    return pl.BlockSpec(shape, lambda *g: (0,) * rank, pipeline_mode=pl.Buffered(1))


def split3(v):
    high = v.astype(BF16)
    rest = v - high.astype(F32)
    mid = rest.astype(BF16)
    low = (rest - mid.astype(F32)).astype(BF16)
    return high, mid, low


def slots_kernel(experts, cap, capp, ids_ref, g_ref, slot_ref, pos_ref, packed_ref):
    tok = ids_ref.shape[1]
    ids = ids_ref[...]
    hot = lax.broadcasted_iota(jnp.int32, (experts, tok), 0) == ids
    before = (
        lax.broadcasted_iota(jnp.int32, (tok, tok), 0)
        < lax.broadcasted_iota(jnp.int32, (tok, tok), 1)
    )
    counts = dot_nn(hot.astype(F32).astype(BF16), before.astype(F32).astype(BF16))
    pos = jnp.sum(jnp.where(hot, counts, 0.0), axis=0, keepdims=True).astype(jnp.int32)
    kept = pos < cap
    slot = jnp.where(kept, ids * capp + pos, -1)
    slot_ref[...] = slot
    pos_ref[...] = jnp.where(kept, pos, -1)
    rows = packed_ref.shape[0]
    step = 256

    @pl.loop(0, rows // step)
    def _(r):
        base = pl.multiple_of(r * step, step)
        table = (lax.broadcasted_iota(jnp.int32, (step, tok), 0) + base == slot)
        packed_ref[pl.ds(base, step), :] = dot_nn(
            table.astype(F32).astype(BF16), g_ref[...]
        ).astype(BF16)


def make_slots(experts, cap, capp, ids_row, g):
    tok, width = g.shape
    return pl.pallas_call(
        functools.partial(slots_kernel, experts, cap, capp),
        out_shape=(
            jax.ShapeDtypeStruct((1, tok), jnp.int32),
            jax.ShapeDtypeStruct((1, tok), jnp.int32),
            jax.ShapeDtypeStruct((experts * capp, width), BF16),
        ),
        compiler_params=pltpu.CompilerParams(vmem_limit_bytes=40 * MIB),
        cost_estimate=pl.CostEstimate(flops=5 * MICRO, bytes_accessed=4 * MIB, transcendentals=0),
        name="slots",
    )(ids_row, g)


def front_kernel(
    hid_ref, gain1_ref, wq_ref, wk_ref, wv_ref, wout_ref, tab_ref, gain2_ref, wr_ref,
    ids_ref, slot_ref, pos_ref, segr_ref, segc_ref, rel_ref,
    n1_ref, q_ref, k_ref, v_ref, p_ref, attn_ref, resid_ref, n2_ref, route_ref, gate_ref,
    packed_ref, gpack_ref,
    relt, mask, bias,
):
    step = pl.program_id(0)
    seqs = segr_ref.shape[0]
    tok = hid_ref.shape[0]

    @pl.when(step == 0)
    def _():
        for t in range(0, tok, HALF):
            x = hid_ref[t:t + HALF, :].astype(F32).T
            scale = lax.rsqrt(jnp.mean(x * x, axis=0, keepdims=True) + EPS)
            n1_ref[:, t:t + HALF] = (x * scale * gain1_ref[...]).astype(BF16)
        relt[...] = rel_ref[...].T
        for s in range(seqs):
            mask[s] = jnp.where(segc_ref[s] == segr_ref[s], 0.0, -1000000000.0)

    for w_ref, o_ref in ((wq_ref, q_ref), (wk_ref, k_ref), (wv_ref, v_ref)):
        o_ref[...] = dot_tn(w_ref[...], n1_ref[...]).astype(BF16)

    @pl.loop(0, GROUP)
    def _(h):
        head = step * GROUP + h
        row = tab_ref[pl.ds(head, 1), :]
        line = jnp.broadcast_to(row, (LEN, LANES))
        for c in range(0, LEN, LANES):
            bias[:, c:c + LANES] = jnp.take_along_axis(line, relt[:, c:c + LANES], axis=1)
        at = pl.ds(pl.multiple_of(h * HEAD_DIM, HEAD_DIM), HEAD_DIM)
        out_at = pl.ds(pl.multiple_of(head * HEAD_DIM, HEAD_DIM), HEAD_DIM)
        for s in range(seqs):
            key = k_ref[at, s * LEN:(s + 1) * LEN]
            value = v_ref[at, s * LEN:(s + 1) * LEN]
            for c in range(0, LEN, HALF):
                cols = slice(s * LEN + c, s * LEN + c + HALF)
                query = q_ref[at, cols] * jnp.asarray(HEAD_DIM ** -0.5, BF16)
                score = dot_tn(key, query) + bias[:, c:c + HALF] + mask[s, :, c:c + HALF]
                peak = jnp.max(score, axis=0, keepdims=True)
                weight = jnp.exp(score - peak)
                total = jnp.sum(weight, axis=0, keepdims=True)
                prob = (weight * (1.0 / total)).astype(BF16)
                p_ref[h, s, :, c:c + HALF] = prob
                attn_ref[out_at, cols] = dot_nn(value, prob).astype(BF16)

    @pl.when(step == pl.num_programs(0) - 1)
    def _():
        experts = route_ref.shape[0]
        for t in range(0, tok, HALF):
            cols = slice(t, t + HALF)
            x = hid_ref[t:t + HALF, :].astype(F32).T
            resid = x + dot_tn(wout_ref[...], attn_ref[:, cols])
            resid_ref[:, cols] = resid
            scale = lax.rsqrt(jnp.mean(resid * resid, axis=0, keepdims=True) + EPS)
            n2 = (resid * scale * gain2_ref[...]).astype(BF16)
            n2_ref[:, cols] = n2
            logits = dot_tn(wr_ref[...], n2)
            top = jnp.max(logits, axis=0, keepdims=True)
            e = jnp.exp(logits - top)
            route = e / jnp.sum(e, axis=0, keepdims=True)
            route_ref[:, cols] = route
            hot = lax.broadcasted_iota(jnp.int32, (experts, HALF), 0) == ids_ref[:, cols]
            gate_ref[:, cols] = jnp.sum(jnp.where(hot, route, 0.0), axis=0, keepdims=True)
        hot = lax.broadcasted_iota(jnp.int32, (experts, tok), 0) == ids_ref[...]
        gates = jnp.where(hot, gate_ref[...], 0.0)
        place = (
            lax.broadcasted_iota(jnp.int32, (LANES, tok), 0) == pos_ref[...]
        ).astype(F32).astype(BF16)
        parts = [dot_nt(part, place) for part in split3(gates)]
        which = lax.broadcasted_iota(jnp.int32, (experts, 8, LANES), 1)
        spread = [jnp.broadcast_to(part[:, None, :], which.shape) for part in parts]
        gpack_ref[...] = jnp.where(
            which == 0, spread[0],
            jnp.where(which == 1, spread[1], jnp.where(which == 2, spread[2], 0.0)),
        ).astype(BF16)
        rows = packed_ref.shape[0]

        @pl.loop(0, rows // HALF)
        def _(r):
            base = pl.multiple_of(r * HALF, HALF)
            table = (lax.broadcasted_iota(jnp.int32, (HALF, tok), 0) + base == slot_ref[...])
            packed_ref[pl.ds(base, HALF), :] = dot_nt(
                table.astype(F32).astype(BF16), n2_ref[...]
            ).astype(BF16)


def front(hidden, gain1, w_qkv, w_out, table, gain2, w_router, ids, slot, pos, seg, rel, rows):
    tok, width = hidden.shape
    experts = w_router.shape[1]
    seqs = seg.shape[0]
    wspec = lambda part: pl.BlockSpec((width, GW), lambda i: (0, part * GROUPS + i))
    qspec = pl.BlockSpec((GW, tok), lambda i: (i, 0))
    sd = jax.ShapeDtypeStruct
    outs = (
        sd((width, tok), BF16), sd((width, tok), BF16), sd((width, tok), BF16),
        sd((width, tok), BF16), sd((HEADS, seqs, LEN, LEN), BF16), sd((width, tok), BF16),
        sd((width, tok), F32), sd((width, tok), BF16), sd((experts, tok), F32), sd((1, tok), F32),
        sd((rows, width), BF16), sd((experts, 8, LANES), BF16),
    )
    return pl.pallas_call(
        front_kernel,
        grid=(GROUPS,),
        in_specs=[
            whole((tok, width)), whole((width, 1)), wspec(0), wspec(1), wspec(2),
            whole((width, width)), whole((HEADS, LANES)), whole((width, 1)),
            whole((width, experts)), whole((1, tok)), whole((1, tok)), whole((1, tok)),
            whole((seqs, 1, LEN)), whole((seqs, LEN, 1)), whole((LEN, LEN)),
        ],
        out_specs=(
            whole((width, tok)), qspec, qspec, qspec,
            pl.BlockSpec((GROUP, seqs, LEN, LEN), lambda i: (i, 0, 0, 0)),
            whole((width, tok)), whole((width, tok)), whole((width, tok)),
            whole((experts, tok)), whole((1, tok)), whole((rows, width)),
            whole((experts, 8, LANES)),
        ),
        out_shape=outs,
        scratch_shapes=[
            pltpu.VMEM((LEN, LEN), jnp.int32),
            pltpu.VMEM((seqs, LEN, LEN), F32),
            pltpu.VMEM((LEN, LEN), F32),
        ],
        compiler_params=pltpu.CompilerParams(vmem_limit_bytes=58 * MIB),
        cost_estimate=pl.CostEstimate(flops=50 * MICRO, bytes_accessed=30 * MIB, transcendentals=0),
        name="front",
    )(
        hidden, gain1.reshape(width, 1), w_qkv, w_qkv, w_qkv, w_out, table,
        gain2.reshape(width, 1), w_router, ids, slot, pos,
        seg.reshape(seqs, 1, LEN), seg.reshape(seqs, LEN, 1), rel,
    )


def combine_kernel(rows_ref, slot_ref, gate_ref, resid_ref, out_ref):
    total = rows_ref.shape[0]
    cols = slot_ref.shape[1]
    table = lax.broadcasted_iota(jnp.int32, (total, cols), 0) == slot_ref[...]
    combined = dot_tn(rows_ref[...], table.astype(F32).astype(BF16))
    out_ref[...] = (resid_ref[...] + gate_ref[...] * combined).T.astype(BF16)


def combine(rows, slot, gate, resid):
    total, width = rows.shape
    tok = slot.shape[1]
    line = pl.BlockSpec((1, HALF), lambda i: (0, i))
    return pl.pallas_call(
        combine_kernel,
        grid=(tok // HALF,),
        in_specs=[
            whole((total, width)), line, line, pl.BlockSpec((width, HALF), lambda i: (0, i)),
        ],
        out_specs=pl.BlockSpec((HALF, width), lambda i: (i, 0)),
        out_shape=jax.ShapeDtypeStruct((tok, width), BF16),
        compiler_params=pltpu.CompilerParams(vmem_limit_bytes=40 * MIB),
        cost_estimate=pl.CostEstimate(flops=6 * MICRO, bytes_accessed=8 * MIB, transcendentals=0),
        name="combine",
    )(rows, slot, gate, resid)


CUBE = 0.044715
ROOT = 0.7978845608028654
FTILE = 768


def gelu_pair(x):
    square = x * x
    t = jnp.tanh(ROOT * (x + CUBE * (x * square)))
    half = 0.5 + 0.5 * t
    slope = half + (0.5 * x) * (1.0 - t * t) * (ROOT + (3.0 * CUBE * ROOT) * square)
    return x * half, slope


def device_of(index):
    wide = lax.axis_size("wide")
    return (index // wide, lax.rem(index, wide))


def expert_kernel(
    block,
    packed, gpack, grows, w_in, w_down,
    dx_out, out_got, rest_out, active_out, ginner_out, gs_out, x_out, gg_out,
    xbuf, gatebuf, gbuf, win, wdown, active, slope, ginner, gs, dx, outs, ggsend, ggbuf,
    x_send, x_recv, gate_send, gate_recv, gg_ssem, gg_rsem, o_send, o_recv, self_sem, load_sem, store_sem,
):
    count = lax.axis_size("narrow") * lax.axis_size("wide")
    me = lax.axis_index("narrow") * lax.axis_size("wide") + lax.axis_index("wide")
    blocks = count // block
    mine = me // block
    capp = packed.shape[1]
    rows = block * capp
    total = count * capp
    hidden = w_in.shape[1]
    mesh_id = pl.DeviceIdType.MESH

    def x_copy(target, source):
        return pltpu.make_async_remote_copy(
            src_ref=packed.at[target], dst_ref=xbuf.at[source], send_sem=x_send.at[target],
            recv_sem=x_recv.at[source], device_id=device_of(target), device_id_type=mesh_id,
        )

    def gate_copy(target, source):
        return pltpu.make_async_remote_copy(
            src_ref=gpack.at[target], dst_ref=gatebuf.at[source], send_sem=gate_send.at[target],
            recv_sem=gate_recv.at[source], device_id=device_of(target), device_id_type=mesh_id,
        )

    def gg_copy(target, source):
        return pltpu.make_async_remote_copy(
            src_ref=ggsend.at[target], dst_ref=ggbuf.at[source], send_sem=gg_ssem.at[target],
            recv_sem=gg_rsem.at[source], device_id=device_of(target), device_id_type=mesh_id,
        )

    ahead = blocks // 2
    inner = lax.rem(me, block)

    def out_copy(c, j):
        target = lax.rem(mine + c, blocks) * block + j
        return pltpu.make_async_remote_copy(
            src_ref=outs.at[c * block + j], dst_ref=out_got.at[c * block + inner],
            send_sem=o_send.at[c * block + j], recv_sem=o_recv.at[c * block + inner],
            device_id=device_of(target), device_id_type=mesh_id,
        )

    def out_wait(c, j):
        return pltpu.make_async_remote_copy(
            src_ref=outs.at[c * block + j], dst_ref=out_got.at[c * block + j],
            send_sem=o_send.at[c * block + j], recv_sem=o_recv.at[c * block + j],
            device_id=device_of(lax.rem(me + 1, count)), device_id_type=mesh_id,
        )

    barrier = pltpu.get_barrier_semaphore()

    @pl.loop(1, count)
    def _(s):
        pl.semaphore_signal(
            barrier, inc=1, device_id=device_of(lax.rem(me + s, count)), device_id_type=mesh_id
        )

    loads = [
        pltpu.make_async_copy(w_in, win, load_sem.at[0]),
        pltpu.make_async_copy(w_down, wdown, load_sem.at[1]),
        pltpu.make_async_copy(grows, gbuf, load_sem.at[2]),
    ]
    own = [
        pltpu.make_async_copy(packed.at[me], xbuf.at[me], self_sem.at[0]),
        pltpu.make_async_copy(gpack.at[me], gatebuf.at[me], self_sem.at[1]),
    ]
    for copy in own + loads:
        copy.start()
    pl.semaphore_wait(barrier, count - 1)

    @pl.loop(0, blocks)
    def _(c):
        there = lax.rem(mine + blocks - c, blocks)

        @pl.loop(0, block)
        def _(j):
            target = there * block + j

            @pl.when(target != me)
            def _():
                gate_copy(target, me).start()
                x_copy(target, me).start()

    for copy in own + loads:
        copy.wait()

    def stores(at):
        return [
            pltpu.make_async_copy(dx.at[at], dx_out.at[at], store_sem.at[0]),
            pltpu.make_async_copy(active.at[at], active_out.at[at], store_sem.at[1]),
            pltpu.make_async_copy(ginner.at[at], ginner_out.at[at], store_sem.at[2]),
            pltpu.make_async_copy(gs.at[at], gs_out.at[at], store_sem.at[3]),
        ]

    @pl.loop(0, blocks)
    def _(c):
        here = lax.rem(mine + c, blocks)
        first = here * block

        @pl.loop(0, block)
        def _(j):
            source = first + j

            @pl.when(source != me)
            def _():
                gate_copy(me, source).wait_recv()
                x_copy(me, source).wait_recv()

        at = pl.ds(pl.multiple_of(here * rows, rows), rows)
        group = pl.ds(first, block)
        x = xbuf[group].reshape(rows, xbuf.shape[2])

        @pl.loop(0, hidden // FTILE)
        def _(f):
            tile = pl.ds(pl.multiple_of(f * FTILE, FTILE), FTILE)
            value, grad = gelu_pair(dot_nn(x, win[:, tile]))
            active[at, tile] = value.astype(BF16)
            slope[:, tile] = grad

        result = dot_nn(active[at, :], wdown[...]).astype(BF16)
        outs[pl.ds(c * block, block)] = result.reshape(block, capp, result.shape[1])

        @pl.when(c < ahead)
        def _():
            @pl.loop(0, block)
            def _(j):
                @pl.when(first + j != me)
                def _():
                    out_copy(c, j).start()

        g = gbuf[group].astype(F32)
        diag = (
            lax.broadcasted_iota(jnp.int32, (block, capp, LANES), 1)
            == lax.broadcasted_iota(jnp.int32, (block, capp, LANES), 2)
        )
        gate = jnp.sum(gatebuf[group].astype(F32), axis=1)
        gate = jnp.sum(
            jnp.where(diag, gate[:, None, :], 0.0), axis=2, keepdims=True
        )
        gs[at, :] = (gate * g).astype(BF16).reshape(rows, g.shape[2])
        gg = jnp.sum(g * result.astype(F32).reshape(g.shape), axis=2, keepdims=True)
        gg = jnp.sum(jnp.where(diag, gg, 0.0), axis=1)
        which = lax.broadcasted_iota(jnp.int32, (block, 8, LANES), 1)
        high, mid, low = [part.astype(F32)[:, None, :] for part in split3(gg)]
        ggsend[group] = jnp.where(
            which == 0, high, jnp.where(which == 1, mid, jnp.where(which == 2, low, 0.0))
        ).astype(BF16)

        @pl.loop(0, block)
        def _(j):
            source = first + j

            @pl.when(source != me)
            def _():
                gg_copy(source, me).start()

        @pl.loop(0, hidden // FTILE)
        def _(f):
            tile = pl.ds(pl.multiple_of(f * FTILE, FTILE), FTILE)
            grad = dot_nt(gs[at, :], wdown[tile, :])
            ginner[at, tile] = (grad * slope[:, tile]).astype(BF16)

        dx[at, :] = dot_nt(ginner[at, :], win[...]).astype(BF16)

        for copy in stores(at):
            copy.start()

    for copy in stores(pl.ds(0, total)):
        copy.wait()
    keep = [
        pltpu.make_async_copy(xbuf, x_out, load_sem.at[0]),
        pltpu.make_async_copy(ggsend.at[me], ggbuf.at[me], self_sem.at[0]),
        pltpu.make_async_copy(outs.at[inner], out_got.at[inner], self_sem.at[1]),
        pltpu.make_async_copy(
            outs.at[pl.ds(ahead * block, count - ahead * block)], rest_out, load_sem.at[1]
        ),
    ]
    for copy in keep:
        copy.start()

    @pl.loop(0, count)
    def _(other):
        @pl.when(other != me)
        def _():
            x_copy(other, me).wait_send()
            gate_copy(other, me).wait_send()
            gg_copy(other, me).wait_send()
            gg_copy(me, other).wait_recv()

    @pl.loop(0, ahead * block)
    def _(i):
        @pl.when(i != inner)
        def _():
            out_wait(i // block, lax.rem(i, block)).wait_send()
            out_wait(i // block, lax.rem(i, block)).wait_recv()

    for copy in keep:
        copy.wait()
    last = pltpu.make_async_copy(ggbuf, gg_out, load_sem.at[1])
    last.start()
    last.wait()


def block_of(count, capp):
    block = 1
    while block * 4 <= count and block * 2 * capp <= 320:
        block *= 2
    return block


def expert(packed, gpack, grows, w_in, w_down):
    count, capp, width = packed.shape
    hidden = w_in.shape[1]
    block = block_of(count, capp)
    early = (count // block // 2) * block
    rows = block * capp
    total = count * capp
    sd = jax.ShapeDtypeStruct
    anyspec = pl.BlockSpec(memory_space=pl.ANY)
    dma = pltpu.SemaphoreType.DMA
    return pl.pallas_call(
        functools.partial(expert_kernel, block),
        in_specs=[anyspec] * 5,
        out_specs=(anyspec,) * 8,
        out_shape=(
            sd((total, width), BF16), sd((early, capp, width), BF16),
            sd((count - early, capp, width), BF16), sd((total, hidden), BF16), sd((total, hidden), BF16), sd((total, width), BF16), sd((count, capp, width), BF16),
            sd((count, 8, LANES), BF16),
        ),
        scratch_shapes=[
            pltpu.VMEM((count, capp, width), BF16), pltpu.VMEM((count, 8, LANES), BF16),
            pltpu.VMEM((count, capp, width), BF16), pltpu.VMEM((width, hidden), BF16),
            pltpu.VMEM((hidden, width), BF16), pltpu.VMEM((total, hidden), BF16),
            pltpu.VMEM((rows, hidden), F32), pltpu.VMEM((total, hidden), BF16),
            pltpu.VMEM((total, width), BF16), pltpu.VMEM((total, width), BF16),
            pltpu.VMEM((count, capp, width), BF16), pltpu.VMEM((count, 8, LANES), BF16),
            pltpu.VMEM((count, 8, LANES), BF16),
            dma((count,)), dma((count,)), dma((count,)), dma((count,)), dma((count,)), dma((count,)),
            dma((early,)), dma((early,)), dma((2,)), dma((3,)), dma((4,)),
        ],
        compiler_params=pltpu.CompilerParams(
            collective_id=0, has_side_effects=True, vmem_limit_bytes=62 * MIB
        ),
        cost_estimate=pl.CostEstimate(flops=60 * MICRO, bytes_accessed=60 * 1024 * 1024, transcendentals=0),
        name="expert",
    )(packed, gpack, grows, w_in, w_down)


def weights_kernel(active_ref, gs_ref, x_ref, ginner_ref, down_ref, in_ref, xt):
    @pl.when(pl.program_id(0) == 0)
    def _():
        total = x_ref.shape[0]
        for t in range(0, total, HALF):
            xt[:, t:t + HALF] = x_ref[t:t + HALF, :].T

    down_ref[0] = dot_tn(active_ref[...], gs_ref[...])
    in_ref[0] = dot_nn(xt[...], ginner_ref[...])


def weight_grads(active, gs, x, ginner):
    total, hidden = active.shape
    width = gs.shape[1]
    tile = HALF
    cols = pl.BlockSpec((total, tile), lambda i: (0, i))
    return pl.pallas_call(
        weights_kernel,
        grid=(hidden // tile,),
        in_specs=[cols, whole((total, width)), whole((total, width)), cols],
        out_specs=(
            pl.BlockSpec((1, tile, width), lambda i: (0, i, 0)),
            pl.BlockSpec((1, width, tile), lambda i: (0, 0, i)),
        ),
        out_shape=(
            jax.ShapeDtypeStruct((1, hidden, width), F32),
            jax.ShapeDtypeStruct((1, width, hidden), F32),
        ),
        scratch_shapes=[pltpu.VMEM((width, total), BF16)],
        compiler_params=pltpu.CompilerParams(vmem_limit_bytes=40 * MIB),
        cost_estimate=pl.CostEstimate(flops=18 * MICRO, bytes_accessed=36 * 1024 * 1024, transcendentals=0),
        name="weight_grads",
    )(active, gs, x, ginner)
PIECES = 32
BIG = 2
UNITS = BIG + GROUPS
TROWS = 16
LATE = 24
LAST_PHASE = 7


def norm_back(grad, source, gain):
    scale = lax.rsqrt(jnp.mean(source * source, axis=0, keepdims=True) + EPS)
    normed = source * scale
    scaled = grad * gain
    inner = jnp.mean(scaled * normed, axis=0, keepdims=True)
    part = grad * normed
    part = part[:, :LANES] + part[:, LANES:]
    return scale * (scaled - normed * inner), part


def back_kernel(
    block,
    dx_ref, gg_ref, slot_ref, pos_ref, ids_ref, route_ref, gate_ref, n2_ref, attn_ref,
    gain1_ref, gain2_ref, wr_ref, wout_ref, resid_any, g_any, hid_any, n1_any, q_any, k_any, v_any, p_any,
    wqkv_any, rel_any, rest_any,
    ingrad_any, out_got, big_out, small_out, early_out, late_out,
    gres, ga, gn1, dv, soft, hid_ref, n1_ref, q_ref, k_ref, v_ref, wqkv_ref, rel_ref, acc,
    *buffers_and_rest,
):
    big, small = buffers_and_rest[:7] + (big_out,), buffers_and_rest[7:14] + (small_out,)
    (
        early, early_got, late, late_got, send, recv, xsend, xrecv, esend, erecv, lsend, lrecv, osend, orecv, load_sem, store_sem, stage_sem,
    ) = buffers_and_rest[14:]
    dq, dk = dv.at[pl.ds(0, GW)], dv.at[pl.ds(GW, GW)]
    step = pl.program_id(0)
    pair = pl.program_id(1)
    tok = g_any.shape[0]
    seqs = tok // LEN
    experts = route_ref.shape[0]
    total = dx_ref.shape[0]
    width = g_any.shape[1]
    narrow_n, wide_n = lax.axis_size("narrow"), lax.axis_size("wide")
    n, w = lax.axis_index("narrow"), lax.axis_index("wide")
    core, zed = lax.rem(w, 2), lax.rem(w // 2, 4)
    ex, why = lax.rem(n, 2), lax.rem(n // 2, 2)
    more_n = (narrow_n // 4) * (wide_n // 8)
    more_w = wide_n // 8
    more = (n // 4) * more_w + w // 8
    mesh_id = pl.DeviceIdType.MESH
    core_dev = (n, w + 1 - 2 * core)
    ex_dev = (n + 1 - 2 * ex, w)
    why_dev = (n + 2 - 4 * why, w)

    def zed_dev(step):
        return (n, w + 2 * (lax.rem(zed + step, 4) - zed))

    def more_dev(step):
        other = lax.rem(more + step, more_n)
        return (n + 4 * (other // more_w - more // more_w),
                w + 8 * (lax.rem(other, more_w) - lax.rem(more, more_w)))

    def unit(u):
        if isinstance(u, int):
            return (big, u, u) if u < BIG else (small, u - BIG, u)
        return small, u, u + BIG

    def ref(which, u):
        group, at, _ = unit(u)
        return group[which], at

    def view(which, u, *more):
        group, at, _ = unit(u)
        return group[which].at[(at,) + more]

    def land(u, q, at):
        return view(7, u, q, at)

    def spot(q):
        first, second = (ex, why) if q == 0 else (why, ex)
        b16 = core * 16
        b8 = b16 + first * 8
        b4 = b8 + second * 4
        return first, second, b16, b8, b4

    def remote(src, dst, k, u, q, dev):
        return pltpu.make_async_remote_copy(
            src_ref=src, dst_ref=dst, send_sem=send.at[k, unit(u)[2], q], recv_sem=recv.at[k, unit(u)[2], q],
            device_id=dev, device_id_type=mesh_id,
        )

    def outgoing(phase, u, q):
        first, second, b16, b8, b4 = spot(q)
        one, two = (ex_dev, why_dev) if q == 0 else (why_dev, ex_dev)
        if phase == 0:
            return [remote(view(0, u, q, pl.ds(16 - b16, 16)), view(2, u, q), 0, u, q, core_dev)]
        if phase == 1:
            src = view(0, u, q, pl.ds(b16 + (1 - first) * 8, 8))
            return [remote(src, view(3, u, q), 1, u, q, one)]
        if phase == 2:
            src = view(0, u, q, pl.ds(b8 + (1 - second) * 4, 4))
            return [remote(src, view(4, u, q), 2, u, q, two)]
        if phase == 3:
            return [
                remote(view(0, u, q, b4 + lax.rem(zed + step, 4)), view(5, u, q, step - 1),
                       2 + step, u, q, zed_dev(step))
                for step in (1, 2, 3)
            ]
        if phase == 4:
            mine = land(u, q, b4 + zed)
            return [remote(view(1, u, q), mine, 5 + step, u, q, zed_dev(step)) for step in (1, 2, 3)]
        if phase == 5:
            mine = land(u, q, pl.ds(b4, 4))
            return [remote(mine, mine, 9, u, q, two)]
        if phase == 6:
            mine = land(u, q, pl.ds(b8, 8))
            return [remote(mine, mine, 10, u, q, one)]
        mine = land(u, q, pl.ds(b16, 16))
        return [remote(mine, mine, 11, u, q, core_dev)]

    def incoming(phase, u, q):
        first, second, b16, b8, b4 = spot(q)
        if phase < 4:
            return outgoing(phase, u, q)
        if phase == 4:
            return [
                remote(view(1, u, q), land(u, q, b4 + lax.rem(zed + 4 - step, 4)),
                       5 + step, u, q, zed_dev(step))
                for step in (1, 2, 3)
            ]
        if phase == 5:
            there = land(u, q, pl.ds(b8 + (1 - second) * 4, 4))
            return [remote(there, there, 9, u, q, core_dev)]
        if phase == 6:
            there = land(u, q, pl.ds(b16 + (1 - first) * 8, 8))
            return [remote(there, there, 10, u, q, core_dev)]
        there = land(u, q, pl.ds(16 - b16, 16))
        return [remote(there, there, 11, u, q, core_dev)]

    def add(u, q, start, count, which):
        own, at = ref(0, u)
        got = ref(which, u)[0]

        @pl.loop(0, count)
        def _(i):
            own[at, q, start + i] = (
                own[at, q, start + i].astype(F32) + got[at, q, i].astype(F32)
            ).astype(BF16)

    def spread(u, q):
        (done, at), (extra, _) = ref(1, u), ref(6, u)
        extra[at, q, more] = done[at, q]
        copies = [
            pltpu.make_async_remote_copy(
                src_ref=view(6, u, q, more), dst_ref=view(6, u, q, more),
                send_sem=xsend.at[unit(u)[2], q, step], recv_sem=xrecv.at[unit(u)[2], q, step],
                device_id=more_dev(step), device_id_type=mesh_id,
            )
            for step in range(1, more_n)
        ]
        for copy in copies:
            copy.start()
        for step in range(1, more_n):
            other = lax.rem(more + more_n - step, more_n)
            pltpu.make_async_remote_copy(
                src_ref=view(6, u, q, more), dst_ref=view(6, u, q, other),
                send_sem=xsend.at[unit(u)[2], q, step], recv_sem=xrecv.at[unit(u)[2], q, step],
                device_id=more_dev(step), device_id_type=mesh_id,
            ).wait_recv()
        for copy in copies:
            copy.wait_send()
        total = extra[at, q, 0].astype(F32)
        for i in range(1, more_n):
            total = total + extra[at, q, i].astype(F32)
        done[at, q] = total.astype(BF16)

    def keep(u, q):
        at = spot(q)[4] + zed
        return pltpu.make_async_copy(view(1, u, q), land(u, q, at), store_sem.at[unit(u)[2], q])

    def settle(phase, u, q):
        first, second, b16, b8, b4 = spot(q)
        if phase == 0:
            add(u, q, b16, 16, 2)
        elif phase == 1:
            add(u, q, b8, 8, 3)
        elif phase == 2:
            add(u, q, b4, 4, 4)
        elif phase == 3:
            (own, at), (done, _), (got, _) = ref(0, u), ref(1, u), ref(5, u)
            done[at, q] = (
                own[at, q, b4 + zed].astype(F32) + got[at, q, 0].astype(F32)
                + (got[at, q, 1].astype(F32) + got[at, q, 2].astype(F32))
            ).astype(BF16)
            if more_n > 1:
                spread(u, q)
            keep(u, q).start()
        elif phase == 4:
            keep(u, q).wait()

    bits = []
    for axis, count in (("wide", wide_n), ("narrow", narrow_n)):
        size = 1
        while size < count:
            at = lax.rem((w if axis == "wide" else n) // size, 2)
            move = size - 2 * size * at
            bits.append((n, w + move) if axis == "wide" else (n + move, w))
            size *= 2
    levels = len(bits)
    early_levels = early_got.shape[0] if early.shape[0] > 1 else 0

    def swap(level, mine, got, ssem, rsem):
        return pltpu.make_async_remote_copy(
            src_ref=mine.at[level], dst_ref=got.at[level], send_sem=ssem.at[level],
            recv_sem=rsem.at[level], device_id=bits[level], device_id_type=mesh_id,
        )

    def climb(level, mine, got, ssem, rsem):
        copy = swap(level, mine, got, ssem, rsem)
        copy.wait_recv()
        copy.wait_send()
        mine[level + 1] = mine[level] + got[level]
        if level + 1 < levels:
            swap(level + 1, mine, got, ssem, rsem).start()

    def climb_early(level):
        climb(level, early, early_got, esend, erecv)

    def climb_late(level):
        climb(level, late, late_got, lsend, lrecv)

    count = narrow_n * wide_n
    blocks = count // block
    ahead = blocks // 2
    index = n * wide_n + w
    rest = rest_any.shape[0]

    def out_copy(i):
        target = lax.rem(index // block + ahead + i // block, blocks) * block + lax.rem(i, block)
        return pltpu.make_async_remote_copy(
            src_ref=rest_any.at[i],
            dst_ref=out_got.at[(i // block) * block + lax.rem(index, block)],
            send_sem=osend.at[i], recv_sem=orecv.at[(i // block) * block + lax.rem(index, block)],
            device_id=device_of(target), device_id_type=mesh_id,
        )

    def out_wait(i):
        return pltpu.make_async_remote_copy(
            src_ref=rest_any.at[i], dst_ref=out_got.at[i], send_sem=osend.at[i],
            recv_sem=orecv.at[i], device_id=core_dev, device_id_type=mesh_id,
        )

    def begin(u):
        for q in range(2):
            for copy in outgoing(0, u, q):
                copy.start()

    def advance(u, phase):
        for q in range(2):
            for copy in incoming(phase, u, q):
                copy.wait_recv()
            for copy in outgoing(phase, u, q):
                copy.wait_send()
            settle(phase, u, q)
            if phase < LAST_PHASE:
                for copy in outgoing(phase + 1, u, q):
                    copy.start()

    def place(u, first, value):
        own, at = ref(0, u)
        half = own.shape[4]
        count = value.shape[1]
        blocks = value.reshape(PIECES, width // PIECES, count).astype(BF16)
        done = 0
        while done < count:
            q, inside = (first + done) // half, (first + done) % half
            size = min(half - inside, count - done)
            own[at, q, :, :, inside:inside + size] = blocks[:, :, done:done + size]
            done += size

    def soft_load(group):
        at = pl.ds(group * GROUP, GROUP)
        return pltpu.make_async_copy(p_any.at[at], soft.at[at], load_sem.at[group])

    pairs = ((q_any, q_ref), (k_any, k_ref), (v_any, v_ref), (n1_any, n1_ref), (wqkv_any, wqkv_ref),
             (rel_any, rel_ref))
    loads = [
        pltpu.make_async_copy(src, dst, load_sem.at[GROUPS + i]) for i, (src, dst) in enumerate(pairs)
    ]

    rows_load = [
        pltpu.make_async_copy(src, hid_ref, load_sem.at[GROUPS + 6 + i])
        for i, src in enumerate((g_any, hid_any))
    ]

    barrier = pltpu.get_barrier_semaphore()
    greet = [core_dev, ex_dev, why_dev] + [zed_dev(move) for move in (1, 2, 3)]
    greet += [more_dev(move) for move in range(1, more_n)] + bits

    @pl.when((step == 0) & (pair == 0))
    def _():
        first = pltpu.make_async_copy(resid_any, gres, stage_sem)
        first.start()
        rows_load[0].start()
        soft_load(0).start()
        for copy in loads:
            copy.start()
        for group in range(1, GROUPS):
            soft_load(group).start()
        for dev in greet:
            pl.semaphore_signal(barrier, inc=1, device_id=dev, device_id_type=mesh_id)

        @pl.loop(0, rest)
        def _(i):
            source = lax.rem(
                index // block + 2 * blocks - ahead - i // block, blocks
            ) * block + lax.rem(i, block)
            pl.semaphore_signal(
                barrier, inc=1, device_id=device_of(source), device_id_type=mesh_id
            )

        pl.semaphore_wait(barrier, len(greet) + rest)

        @pl.loop(0, rest)
        def _(i):
            out_copy(i).start()

        hot = lax.broadcasted_iota(jnp.int32, (experts, tok), 0) == ids_ref[...]
        where = (
            lax.broadcasted_iota(jnp.int32, (LANES, tok), 0) == pos_ref[...]
        ).astype(F32).astype(BF16)
        grad_gate = jnp.zeros((1, tok), F32)
        for e in range(0, experts, 32):
            found = dot_nn(gg_ref[e:e + 32].reshape(256, LANES), where)
            found = jnp.sum(found.reshape(32, 8, tok), axis=1)
            grad_gate += jnp.sum(jnp.where(hot[e:e + 32], found, 0.0), axis=0, keepdims=True)
        first.wait()
        rows_load[0].wait()
        grad_logits = (
            (grad_gate * gate_ref[...]) * (hot.astype(F32) - route_ref[...])
        ).astype(BF16)
        early[0, :experts, :] = dot_nt(grad_logits, n2_ref[...])
        gain_grad = jnp.zeros((width, LANES), F32)
        for t in range(0, tok, HALF):
            cols = slice(t, t + HALF)
            gn2 = dot_nn(wr_ref[...], grad_logits[:, cols])
            size = total if total <= 1280 else 512
            for r in range(0, total, size):
                table = lax.broadcasted_iota(jnp.int32, (size, HALF), 0) + r == slot_ref[:, cols]
                gn2 = gn2 + dot_tn(dx_ref[r:r + size, :], table.astype(F32).astype(BF16))
            branch, part = norm_back(gn2, gres[:, cols], gain2_ref[...])
            gain_grad = gain_grad + part
            gr = hid_ref[t:t + HALF, :].astype(F32).T + branch
            gres[:, cols] = gr
            ga[:, cols] = gr.astype(BF16)
        early[0, experts:, :] = jnp.broadcast_to(
            jnp.sum(gain_grad.T, axis=0, keepdims=True), (8, width)
        )
        for c in range(0, width, HALF):
            place(0, c, dot_nt(attn_ref[...], ga[c:c + HALF, :]))
        rows_load[1].start()
        begin(0)
        if early_levels:
            swap(0, early, early_got, esend, erecv).start()
        for t in range(0, tok, HALF):
            cols = slice(t, t + HALF)
            ga[:, cols] = dot_nn(wout_ref[...], ga[:, cols]).astype(BF16)
        soft_load(0).wait()
        for copy in loads:
            copy.wait()
        for group in range(1, GROUPS):
            soft_load(group).wait()

        @pl.loop(0, HEADS)
        def _(head):
            at = pl.ds(pl.multiple_of(head * HEAD_DIM, HEAD_DIM), HEAD_DIM)
            for s in range(seqs):
                row = slice(s * LEN, (s + 1) * LEN)
                dv[at, row] = dot_nt(ga[at, row], soft[head, s]).astype(BF16)

        for c in range(0, width, GW):
            place(1, c, dot_nt(n1_ref[...], dv[c:c + GW, :]))
        begin(1)
        for t in range(0, tok, HALF):
            gn1[:, t:t + HALF] = dot_nn(wqkv_ref[:, 2 * width:], dv[:, t:t + HALF])

    @pl.loop(0, PAIR)
    def _(h):
        inside = pair * PAIR + h
        head = step * GROUP + inside
        at = pl.ds(pl.multiple_of(inside * HEAD_DIM, HEAD_DIM), HEAD_DIM)
        all_at = pl.ds(pl.multiple_of(head * HEAD_DIM, HEAD_DIM), HEAD_DIM)
        for s in range(seqs):
            row = slice(s * LEN, (s + 1) * LEN)
            value = v_ref[all_at, row]
            for c in range(0, LEN, HALF):
                cols = slice(s * LEN + c, s * LEN + c + HALF)
                grad = ga[all_at, cols]
                inner = jnp.sum(
                    grad.astype(F32) * attn_ref[all_at, cols].astype(F32), axis=0, keepdims=True
                )
                gp = dot_tn(value, grad)
                soft[head, s, :, c:c + HALF] = (
                    soft[head, s, :, c:c + HALF].astype(F32) * (gp - inner)
                ).astype(BF16)
            ds = soft[head, s]
            factor = HEAD_DIM ** -0.5
            dq[at, row] = (dot_nn(k_ref[all_at, row], ds) * factor).astype(BF16)
            dk[at, row] = (dot_nt(q_ref[all_at, row], ds) * factor).astype(BF16)

        for number in range(HEADS):
            todo = [(u, phase) for u, phase, at_head in SCHEDULE if at_head == number]
            rise = [level for level, at_head in enumerate(EARLY_LEVELS)
                    if at_head == number and level < early_levels]
            if todo or rise:
                @pl.when(head == number)
                def _():
                    for u, phase in todo:
                        advance(u, phase)
                    for level in rise:
                        climb_early(level)

    @pl.when(pair == pl.num_programs(1) - 1)
    def _():
        for part, d in enumerate((dq, dk)):
            place(step, part * GW, dot_nt(n1_ref[...], d[...]))
        begin(step)
        for part, d in enumerate((dq, dk)):
            cols = pl.ds(pl.multiple_of(part * width + step * GW, GW), GW)
            gn1[...] += dot_nn(wqkv_ref[:, cols], d[...])

    @pl.when((step == pl.num_programs(0) - 1) & (pair == pl.num_programs(1) - 1))
    def _():
        planned = {(u, phase) for u, phase, at_head in SCHEDULE}
        left = {u: [phase for phase in range(LAST_PHASE + 1) if (u, phase) not in planned]
                for u in range(UNITS)}

        def push():
            for u in range(UNITS):
                if left[u]:
                    advance(u, left[u].pop(0))

        rows_load[1].wait()
        gain_grad = jnp.zeros((width, LANES), F32)
        for t in range(0, tok, HALF):
            cols = slice(t, t + HALF)
            x = hid_ref[t:t + HALF, :].astype(F32).T
            branch, part = norm_back(gn1[:, cols], x, gain1_ref[...])
            gain_grad = gain_grad + part
            gres[:, cols] = gres[:, cols] + branch
            if t == HALF:
                push()
        pltpu.make_async_copy(gres, ingrad_any, stage_sem).start()
        line = jnp.sum(gain_grad.T, axis=0, keepdims=True)
        late[0] = jnp.zeros((LATE, LANES), F32)
        for i in range(width // LANES):
            late[0, i:i + 1, :] = line[:, i * LANES:(i + 1) * LANES]
        push()
        lines = HEADS * seqs
        acc[...] = jnp.zeros_like(acc)
        chunks = 4
        for chunk in range(chunks):
            @pl.loop(chunk * (LEN // TROWS // chunks), (chunk + 1) * (LEN // TROWS // chunks))
            def _(r):
                base = pl.multiple_of(r * TROWS, TROWS)
                lhs = soft[:, :, pl.ds(base, TROWS), :].reshape(lines * TROWS, LEN)
                rel = rel_ref[pl.ds(base, TROWS), :]
                hot = (
                    rel[:, None, :]
                    == lax.broadcasted_iota(jnp.int32, (TROWS, BUCKETS, LEN), 1)
                ).astype(F32).astype(BF16).reshape(TROWS * BUCKETS, LEN)
                acc[...] += dot_nt(lhs, hot)

            push()
        rows = lax.broadcasted_iota(jnp.int32, acc.shape, 0) % TROWS
        cols = lax.broadcasted_iota(jnp.int32, acc.shape, 1) // BUCKETS
        kept = jnp.where(rows == cols, acc[...], 0.0)
        per_head = jnp.sum(kept.reshape(HEADS, seqs * TROWS, acc.shape[1]), axis=1)
        fold = (
            lax.broadcasted_iota(jnp.int32, (LANES, acc.shape[1]), 1) % BUCKETS
            == lax.broadcasted_iota(jnp.int32, (LANES, acc.shape[1]), 0)
        ).astype(F32)
        late[0, 8:8 + HEADS, :] = lax.dot_general(
            per_head, fold, (((1,), (1,)), ((), ())), precision=lax.Precision.HIGHEST,
            preferred_element_type=F32,
        )
        swap(0, late, late_got, lsend, lrecv).start()
        level = 0
        while any(left.values()) or level < levels:
            push()
            if level < levels:
                climb_late(level)
                level += 1
        for level in range(early_levels):
            if level >= len(EARLY_LEVELS):
                climb_early(level)
        pltpu.make_async_copy(gres, ingrad_any, stage_sem).wait()

        @pl.loop(0, rest)
        def _(i):
            out_wait(i).wait_send()
            out_wait(i).wait_recv()

        early_out[...] = early[early_levels]
        late_out[...] = late[levels]


EARLY_MOST = 64
EARLY_LEVELS = (1, 3, 5, 7, 9)
SCHEDULE = (
    [(0, phase, at) for phase, at in enumerate((0, 2, 4, 6, 8, 10))]
    + [(1, phase, at) for phase, at in enumerate((1, 3, 5, 8, 11))]
    + [(2, phase, at) for phase, at in enumerate((5, 7, 10))]
    + [(3, phase, at) for phase, at in enumerate((9, 11))]
)


def back(dx, gg, slot, pos, ids, route, gate, resid, n2, attn, g, hidden, n1, q, k, v, p, gain1, gain2,
         w_router, w_out, w_qkv, relt, rest, block):
    tok, width = hidden.shape
    experts = w_router.shape[1]
    total = dx.shape[0]
    seqs = p.shape[1]
    narrow_n, wide_n = lax.axis_size("narrow"), lax.axis_size("wide")
    levels = (narrow_n * wide_n).bit_length() - 1
    more_n = (narrow_n // 4) * (wide_n // 8)
    early_levels = levels if experts <= EARLY_MOST else 0
    rows = width // PIECES
    anyspec = pl.BlockSpec(memory_space=pl.ANY)
    sd = jax.ShapeDtypeStruct
    dma = pltpu.SemaphoreType.DMA
    vm = pltpu.VMEM

    def bufs(number, half):
        return [
            vm((number, 2) + lead + (rows, half), BF16)
            for lead in ((PIECES,), (), (16,), (8,), (4,), (3,), (more_n,))
        ]

    return pl.pallas_call(
        functools.partial(back_kernel, block),
        grid=(GROUPS, GROUP // PAIR),
        in_specs=[
            whole((total, width)), whole((experts, 8, LANES)), whole((1, tok)), whole((1, tok)),
            whole((1, tok)), whole((experts, tok)), whole((1, tok)), whole((width, tok)),
            whole((width, tok)), whole((width, 1)), whole((width, 1)),
            whole((width, experts)), whole((width, width)),
        ] + [anyspec] * 11,
        out_specs=(
            anyspec, anyspec, anyspec, anyspec, whole((experts + 8, width)), whole((LATE, LANES)),
        ),
        out_shape=(
            sd((width, tok), F32), sd(rest.shape, BF16), sd((BIG, 2, PIECES, rows, width // 2), BF16),
            sd((GROUPS, 2, PIECES, rows, GW), BF16),
            sd((experts + 8, width), F32), sd((LATE, LANES), F32),
        ),
        scratch_shapes=[
            vm((width, tok), F32), vm((width, tok), BF16), vm((width, tok), F32),
            vm((width, tok), BF16),
            vm((HEADS, seqs, LEN, LEN), BF16), vm((tok, width), BF16), vm((width, tok), BF16),
            vm((width, tok), BF16), vm((width, tok), BF16), vm((width, tok), BF16),
            vm(w_qkv.shape, BF16), vm((LEN, LEN), jnp.int32), vm((HEADS * seqs * TROWS, TROWS * BUCKETS), F32),
            *bufs(BIG, width // 2), *bufs(GROUPS, GW),
            vm((early_levels + 1, experts + 8, width), F32),
            vm((max(early_levels, 1), experts + 8, width) if early_levels else (1, 8, width), F32),
            vm((levels + 1, LATE, LANES), F32), vm((levels, LATE, LANES), F32),
            dma((12, UNITS, 2)), dma((12, UNITS, 2)), dma((UNITS, 2, more_n)),
            dma((UNITS, 2, more_n)), dma((levels,)), dma((levels,)), dma((levels,)), dma((levels,)),
            dma((rest.shape[0],)), dma((rest.shape[0],)),
            dma((GROUPS + 8,)), dma((UNITS, 2)), dma(()),
        ],
        compiler_params=pltpu.CompilerParams(
            collective_id=1, has_side_effects=True, vmem_limit_bytes=63 * MIB
        ),
        cost_estimate=pl.CostEstimate(flops=80 * MICRO, bytes_accessed=50 * MIB, transcendentals=0),
        name="back",
    )(
        dx, gg, slot, pos, ids, route, gate, n2, attn, gain1.reshape(width, 1),
        gain2.reshape(width, 1), w_router, w_out, resid, g, hidden, n1, q, k, v, p, w_qkv, relt, rest,
    )


def finish_kernel(
    early_ref, late_ref, slot_ref, gate_ref, resid_ref, big_ref, small_ref, grad_ref, out_ref, qkv_ref, proj_ref,
    ingrad_ref,
):
    ingrad_ref[...] = grad_ref[...].T
    rows_a = early_ref.shape[0]
    cols = slot_ref.shape[1]
    combined = None
    for base, ref in ((0, early_ref), (rows_a, late_ref)):
        table = (
            lax.broadcasted_iota(jnp.int32, (ref.shape[0], cols), 0) + base == slot_ref[...]
        )
        part = dot_tn(ref[...], table.astype(F32).astype(BF16))
        combined = part if combined is None else combined + part
    out_ref[...] = (resid_ref[...] + gate_ref[...] * combined).T.astype(BF16)
    rows = qkv_ref.shape[0]
    half = big_ref.shape[4]
    width = 2 * half
    for q in range(2):
        proj_ref[:, q * half:(q + 1) * half] = big_ref[0, q].astype(F32).reshape(rows, half)
        start = 2 * width + q * half
        qkv_ref[:, start:start + half] = big_ref[1, q].astype(F32).reshape(rows, half)
        for group in range(GROUPS):
            start = q * width + group * GW
            qkv_ref[:, start:start + GW] = small_ref[group, q].astype(F32).reshape(rows, GW)


def finish(out_a, out_b, slot, gate, resid, big, small, grad):
    tok = slot.shape[1]
    width = resid.shape[0]
    steps = tok // HALF
    line = pl.BlockSpec((1, HALF), lambda i: (0, i))
    pieces = big.shape[2] // steps
    rows = width // steps
    return pl.pallas_call(
        finish_kernel,
        grid=(steps,),
        in_specs=[
            whole(out_a.shape), whole(out_b.shape), line, line,
            pl.BlockSpec((width, HALF), lambda i: (0, i)),
            pl.BlockSpec(big.shape[:2] + (pieces,) + big.shape[3:], lambda i: (0, 0, i, 0, 0)),
            pl.BlockSpec(small.shape[:2] + (pieces,) + small.shape[3:], lambda i: (0, 0, i, 0, 0)),
            pl.BlockSpec((width, HALF), lambda i: (0, i)),
        ],
        out_specs=(
            pl.BlockSpec((HALF, width), lambda i: (i, 0)),
            pl.BlockSpec((rows, 3 * width), lambda i: (i, 0)),
            pl.BlockSpec((rows, width), lambda i: (i, 0)),
            pl.BlockSpec((HALF, width), lambda i: (i, 0)),
        ),
        out_shape=(
            jax.ShapeDtypeStruct((tok, width), BF16),
            jax.ShapeDtypeStruct((width, 3 * width), F32),
            jax.ShapeDtypeStruct((width, width), F32),
            jax.ShapeDtypeStruct((tok, width), F32),
        ),
        compiler_params=pltpu.CompilerParams(vmem_limit_bytes=40 * MIB),
        cost_estimate=pl.CostEstimate(flops=8 * MICRO, bytes_accessed=20 * MIB, transcendentals=0),
        name="finish",
    )(out_a, out_b, slot, gate, resid, big, small, grad)


def matmul(a, b):
    return jnp.dot(a, b, preferred_element_type=F32)


AXES = ("narrow", "wide")


def exchange(v):
    return lax.all_to_all(v, AXES, split_axis=0, concat_axis=0, tiled=True)


def local(
    hidden_in, norm_gain_one, w_qkv, w_out, pos_table, norm_gain_two, w_router, w_in, w_down,
    expert_ids, segment_ids, rel_buckets, out_grad,
):
    experts = lax.axis_size("narrow") * lax.axis_size("wide")
    tok, width = hidden_in.shape
    cap = max(2, (5 * tok + 4 * experts - 1) // (4 * experts))
    capp = (cap + 7) // 8 * 8
    rows = experts * capp
    ids = expert_ids.reshape(1, tok)
    slot, pos, g_packed = make_slots(experts, cap, capp, ids, out_grad)
    g_rows = exchange(g_packed.reshape(experts, capp, width))
    table = jnp.pad(pos_table.T, ((0, 0), (0, LANES - BUCKETS)))
    (n1, q, k, v, p, attn, resid, n2, route, gate, packed, gpack) = front(
        hidden_in, norm_gain_one, w_qkv, w_out, table, norm_gain_two, w_router, ids, slot, pos,
        segment_ids, rel_buckets, rows,
    )
    block = block_of(experts, capp)
    dx, out_a, rest, active, ginner, gs, expert_in, gg = expert(
        packed.reshape(experts, capp, width), gpack, g_rows, w_in[0], w_down[0]
    )
    dx = exchange(dx.reshape(experts, capp, width)).reshape(rows, width)
    grad_w_down, grad_w_in = weight_grads(active, gs, expert_in.reshape(rows, width), ginner)
    dx, grad_w_down, grad_w_in = lax.optimization_barrier((dx, grad_w_down, grad_w_in))
    grad, out_b, big, small, early, late = back(
        dx, gg, slot, pos, ids, route, gate, resid, n2, attn, out_grad, hidden_in, n1, q, k, v, p,
        norm_gain_one, norm_gain_two, w_router, w_out, w_qkv, rel_buckets.T, rest, block,
    )
    if experts > EARLY_MOST:
        early = lax.psum(early, AXES)
    blocks = experts // block
    index = lax.axis_index("narrow") * lax.axis_size("wide") + lax.axis_index("wide")
    turn = lax.rem(index // block + blocks - ids // block, blocks)
    place = jnp.where(pos >= 0, (turn * block + lax.rem(ids, block)) * capp + pos, -1)
    layer_out, qkv_grad, out_grad_w, in_grad = finish(
        out_a.reshape(-1, width), out_b.reshape(-1, width), place, gate, resid, big, small, grad
    )
    lines = width // LANES
    return (
        layer_out, in_grad, late[:lines].reshape(width), qkv_grad, out_grad_w,
        late[8:8 + HEADS, :BUCKETS].T, early[experts], early[:experts].T, grad_w_in, grad_w_down,
    )


def solution(mesh):
    split = P(AXES, None)
    cube = P(AXES, None, None)
    return jax.shard_map(
        local,
        mesh=mesh,
        in_specs=(
            split, P(), P(), P(), P(), P(), P(), cube, cube, split, split, P(), split,
        ),
        out_specs=(split, split, P(), P(), P(), P(), P(), P(), cube, cube),
        check_vma=False,
    )
```

time: 359 us -> 337 us (0.939)
  Pallas kernels: 279 us -> 266 us
  other arithmetic: 6.19 us -> 0.04 us
    pallas_call x4 -> x2, Pallas kernels: 136 us -> 116 us  [the longest x1 109 us: back(): pl.pallas_call(functools.partial(back_kernel, block), grid=(GROUPS, GROUP...]
    pallas_call x1, Pallas kernels: 70.9 us -> 78 us  [expert(): pl.pallas_call(functools.partial(expert_kernel, block), in_specs=[anyspec...]
    all_to_all x3 -> x2, starting transfers between devices: 17.6 us -> 15.4 us  [exchange(): return lax.all_to_all(v, AXES, split_axis=0, concat_axis=0, tiled=True)]
    all_to_all x3 -> x2, waiting for transfers between devices: 22.9 us -> 22.3 us  [exchange(): return lax.all_to_all(v, AXES, split_axis=0, concat_axis=0, tiled=True)]
  transfers between devices with their start and end apart: 3 -> 2, of which waited for: 1 -> 1; matrix products, arithmetic and copies ran while one was open for 5% -> 2% of each run, Pallas kernels for 56% -> 20%
where the time goes in v3:
time: 337 us; the launch traced here: 336 us
  Pallas kernels  266 us (79%)
  local copies, waits for them, and re-layouts  31.1 us (9%)
  waiting for transfers between devices  22.3 us (7%)
  starting transfers between devices  15.4 us (5%)
    pallas_call x1, Pallas kernels, back(): pl.pallas_call(functools.partial(back_kernel, block), grid=(GROUPS, GROUP...  109 us
    pallas_call x1, Pallas kernels, expert(): pl.pallas_call(functools.partial(expert_kernel, block), in_specs=[anyspec...  78 us
    pallas_call x1, Pallas kernels, front(): pl.pallas_call(front_kernel, grid=(GROUPS,), in_specs=[whole((tok, width)...  49.2 us
    all_to_all x2, waiting for transfers between devices, exchange(): return lax.all_to_all(v, AXES, split_axis=0, concat_axis=0, tiled=True)  22.3 us
    unnamed x48, local copies, waits for them, and re-layouts  21.6 us
    pallas_call x1, Pallas kernels, weight_grads(): pl.pallas_call(weights_kernel, grid=(hidden // tile,), in_specs=[cols, wh...  18.3 us
    all_to_all x2, starting transfers between devices, exchange(): return lax.all_to_all(v, AXES, split_axis=0, concat_axis=0, tiled=True)  15.4 us
    pallas_call x1, Pallas kernels, finish(): pl.pallas_call(finish_kernel, grid=(steps,), in_specs=[whole(out_a.shape)...  7.31 us
  transfers between devices with their start and end apart: 2, of which 1 were waited for; matrix products, arithmetic and copies ran while one was open for 2% of the time, Pallas kernels for 20%

profile of v3, /device:TPU:0, one launch (start us, length us, event | category | flops | bytes accessed | tf_op | source)
XLA Modules:
  0.0 335.6 jit_solution(4799044466435787522)
XLA Ops:
  0.6 0.0 copy-start
  0.7 0.7 copy-done
  1.3 0.0 copy-start.4
  1.3 1.4 copy-done.4
  2.7 4.5 %slots.1 = (s32[1,1024]{1,0:T(1,128)S(1)}, s32[1,1024]{1,0:T(1,128)S(1)}, bf16[1280,768]{1,0:T(8,128)(2,1)}) custom-call(s32[1,1024]{1,0:T(1,128)S(1)} %bitcast.22, bf16[1024,768]{1,0:T(8,128)(2,1)S(1)} %copy-done.4), custom_call_target="tpu_custom_call" | custom-call | flops 5750000128 | bytes 4194304 | tf_op jit(solution)/shard_map/slots/pallas_call | solution.py:79
  7.3 0.0 copy-start.2
  7.3 0.6 copy-done.2
  7.9 0.0 copy-start.14
  7.9 0.6 copy-done.14
  8.5 0.0 copy-start.21
  8.5 0.0 copy-start.22
  8.5 0.0 copy-start.18
  8.5 0.0 copy-start.19
  8.5 0.0 copy-start.20
  8.5 7.3 %all-to-all-start = ((bf16[32,40,768]{2,1,0:T(8,128)(2,1)}), bf16[32,40,768]{2,1,0:T(8,128)(2,1)S(1)}, u32[]{:S(2)}, u32[]{:S(2)}) async-start(bf16[32,40,768]{2,1,0:T(8,128)(2,1)} %bitcast.4), calls=%async_computation | async-start | bytes 3932160 | tf_op jit(solution)/shard_map/all_to_all | solution.py:1203
  15.8 0.0 copy-done.21
  15.8 0.9 reshape.215.gain1_ref
  16.7 0.0 copy-done.22
  16.8 0.9 reshape.216.gain2_ref
  17.7 0.0 copy-done.18
  17.7 0.8 copy.28.wr_ref
  18.5 0.0 copy-done.19
  18.5 0.6 reshape.205.segr_ref
  19.1 1.0 copy.29.segc_ref
  20.1 0.0 copy-done.20
  20.1 0.6 pad.4.tab_ref
  20.7 49.2 %front.1 = (bf16[768,1024]{1,0:T(8,128)(2,1)}, bf16[768,1024]{1,0:T(8,128)(2,1)}, bf16[768,1024]{1,0:T(8,128)(2,1)}, bf16[768,1024]{1,0:T(8,128)(2,1)}, bf16[12,...) custom-call(bf16[1024,768]{1,0:T(8,128)(2,1)} %hid_any.1, ...), custom_call_target="tpu_custom_call" | custom-call | flops 57500000256 | bytes 31457280 | tf_op jit(solution)/shard_map/front/pallas_call | solution.py:193
  69.9 0.0 all-to-all-done.grows
  70.0 0.0 copy-start.16
  70.0 1.3 copy-done.16
  71.2 78.0 %expert.1 = (bf16[1280,768]{1,0:T(8,128)(2,1)}, bf16[16,40,768]{2,1,0:T(8,128)(2,1)}, bf16[16,40,768]{2,1,0:T(8,128)(2,1)}, bf16[1280,3072]{1,0:T(8,128)(2,1)}, ...) custom-call(bf16[32,40,768]{2,1,0:T(8,128)(2,1)} %bitcast.32, ...), custom_call_target="tpu_custom_call" | custom-call | flops 69000003584 | bytes 62914560 | tf_op jit(solution)/shard_map/expert/pallas_call | solution.py:493
  149.2 0.0 copy-start.17
  149.2 8.1 %all-to-all-start.1 = ((bf16[32,40,768]{2,1,0:T(8,128)(2,1)}), bf16[32,40,768]{2,1,0:T(8,128)(2,1)}, u32[]{:S(2)}, u32[]{:S(2)}) async-start(bf16[32,40,768]{2,1,0:T(8,128)(2,1)} %bitcast.26), calls=%async_computation.1 | async-start | bytes 3932160 | tf_op jit(solution)/shard_map/all_to_all | solution.py:1203
  157.3 0.0 copy-done.17
  157.4 0.0 copy-start.1
  157.4 0.0 copy-start.3
  157.4 0.0 copy-start.5
  157.4 1.3 copy.30
  158.7 0.0 copy-done.1
  158.7 0.0 copy-done.3
  158.7 0.6 copy-done.5
  159.3 0.0 copy-start.12
  159.3 3.2 copy-done.12
  162.5 0.0 copy-start.13
  162.5 1.5 copy-done.13
  164.1 18.3 %weight_grads.1 = (f32[1,3072,768]{2,1,0:T(8,128)}, f32[1,768,3072]{2,1,0:T(8,128)}) custom-call(bf16[1280,3072]{1,0:T(8,128)(2,1)S(1)} %copy-done.12, bf16[1280,768]{1,0:T(8,128)(2,1)S(1)} %copy-done.13, bf16[1280,768]{1,0:T(8,128)(2,1)S(1)} %bitcast.23, bf16[1280,3072]{1,0:T(8,128)(2,1)} %get-tuple-element.58.ginner_ref), custom_call_target="tpu_custom_call" | custom-call | flops 20700000256 | bytes 37748736 | tf_op jit(solution)/shard_map/weight_grads/pallas_call | solution.py:537
  182.4 22.3 %all-to-all-done.1 = bf16[32,40,768]{2,1,0:T(8,128)(2,1)} async-done(((bf16[32,40,768]{2,1,0:T(8,128)(2,1)}), bf16[32,40,768]{2,1,0:T(8,128)(2,1)}, u32[]{:S(2)}, u32[]{:S(2)}) %all-to-all-start.1) | async-done | bytes 1966112 | tf_op jit(solution)/shard_map/all_to_all | solution.py:1203
  204.7 0.0 copy-start.15
  204.7 108.7 %back.1 = (f32[768,1024]{1,0:T(8,128)}, bf16[16,40,768]{2,1,0:T(8,128)(2,1)}, bf16[2,2,32,24,384]{4,3,2,1,0:T(8,128)(2,1)}, bf16[3,2,32,24,256]{4,3,2,1,0:T(8,12...) custom-call(bf16[1280,768]{1,0:T(8,128)(2,1)} %bitcast.9.dx_ref, bf16[32,8,128]{2,1,0:T(8,128)(2,1)} %get-tuple-element.62.gg_ref, ...), custom_call_target="tpu_custom_call" | custom-call | flops 92000002048 | bytes 52428800 | tf_op jit(solution)/shard_map/back/pallas_call | solution.py:1090
  313.4 1.3 slice_bitcast_fusion.1
  314.7 1.3 slice_bitcast_fusion.2
  315.9 1.5 slice_bitcast_fusion
  317.5 1.3 slice_reduce_fusion
  318.8 0.0 copy-done.15
  318.8 0.0 copy-start.6
  318.8 1.2 copy-done.6
  320.0 0.0 copy-start.7
  320.0 1.2 copy-done.7
  321.2 0.0 copy-start.8
  321.2 1.9 copy-done.8
  323.1 1.9 copy-done.9
  325.0 1.7 copy-done.10
  326.7 1.7 copy-done.11
  328.3 7.3 %finish.1 = (bf16[1024,768]{1,0:T(8,128)(2,1)}, f32[768,2304]{1,0:T(8,128)}, f32[768,768]{1,0:T(8,128)}, f32[1024,768]{1,0:T(8,128)}) custom-call(bf16[640,768]{1,0:T(8,128)(2,1)S(1)} %bitcast.24, bf16[640,768]{1,0:T(8,128)(2,1)S(1)} %bitcast.25, s32[1,1024]{1,0:T(1,128)S(1)} %compare_select_fusion.2.slot_ref, f32[1,1024]{1,0:T(1,128)S(1)} %copy-done.15, ...), custom_call_target="tpu_custom_call" | custom-call | flops 9200000000 | bytes 20971520 | tf_op jit(solution)/shard_map/finish/pallas_call | solution.py:1167
  (4 shorter events, 0.0 us)
Async XLA Ops:
  0.6 0.7 copy-start
  1.3 1.4 copy-start.4
  7.3 0.6 copy-start.2
  7.9 0.6 copy-start.14
  8.5 7.3 %copy-start.21 = (f32[768]{0:T(1024)S(1)}, f32[768]{0:T(1024)}, u32[]{:S(2)}) copy-start(f32[768]{0:T(1024)} %param.14) | copy-start | bytes 9220
  8.5 8.3 %copy-start.22 = (f32[768]{0:T(1024)S(1)}, f32[768]{0:T(1024)}, u32[]{:S(2)}) copy-start(f32[768]{0:T(1024)} %param.18) | copy-start | bytes 9220
  8.5 9.2 %copy-start.18 = (bf16[768,32]{0,1:T(8,128)(2,1)S(1)}, bf16[768,32]{0,1:T(8,128)(2,1)}, u32[]{:S(2)}) copy-start(bf16[768,32]{0,1:T(8,128)(2,1)} %param.19) | copy-start | bytes 147460
  8.5 10.0 %copy-start.19 = (s32[2,512]{1,0:T(2,128)S(1)}, s32[2,512]{1,0:T(2,128)}, u32[]{:S(2)}) copy-start(s32[2,512]{1,0:T(2,128)} %param.23) | copy-start | bytes 12292
  8.5 11.6 %copy-start.20 = (f32[32,12]{0,1:T(8,128)S(1)}, f32[32,12]{0,1:T(8,128)}, u32[]{:S(2)}) copy-start(f32[32,12]{0,1:T(8,128)} %param.17) | copy-start | bytes 4612
  8.5 61.5 %all-to-all-start = ((bf16[32,40,768]{2,1,0:T(8,128)(2,1)}), bf16[32,40,768]{2,1,0:T(8,128)(2,1)S(1)}, u32[]{:S(2)}, u32[]{:S(2)}) async-start(bf16[32,40,768]{2,1,0:T(8,128)(2,1)} %bitcast.4), calls=%async_computation | async-start | bytes 3932160 | tf_op jit(solution)/shard_map/all_to_all | solution.py:1203
  70.0 1.3 copy-start.16
  149.2 8.1 %copy-start.17 = (s32[512,512]{1,0:T(8,128)S(1)}, s32[512,512]{1,0:T(8,128)}, u32[]{:S(2)}) copy-start(s32[512,512]{1,0:T(8,128)} %rel_ref.1) | copy-start | bytes 3145732
  149.2 55.5 %all-to-all-start.1 = ((bf16[32,40,768]{2,1,0:T(8,128)(2,1)}), bf16[32,40,768]{2,1,0:T(8,128)(2,1)}, u32[]{:S(2)}, u32[]{:S(2)}) async-start(bf16[32,40,768]{2,1,0:T(8,128)(2,1)} %bitcast.26), calls=%async_computation.1 | async-start | bytes 3932160 | tf_op jit(solution)/shard_map/all_to_all | solution.py:1203
  157.4 1.3 copy-start.1
  157.4 1.3 copy-start.3
  157.4 1.9 copy-start.5
  159.3 3.2 copy-start.12
  162.5 1.5 copy-start.13
  204.7 114.1 %copy-start.15 = (f32[1,1024]{1,0:T(1,128)S(1)}, f32[1,1024]{1,0:T(1,128)}, u32[]{:S(2)}) copy-start(f32[1,1024]{1,0:T(1,128)} %get-tuple-element.64.gate_ref) | copy-start | bytes 12292
  318.8 1.2 copy-start.6
  320.0 1.2 copy-start.7
  321.2 1.9 copy-start.8
  323.1 1.9 copy-start.9
  325.0 1.7 copy-start.10
  326.7 1.7 copy-start.11
